TPU v7x, 32 devices: a whole 2x2x4 slice. The times are simulated.
32 devices in a mesh: groups: 2 (over x), seq: 16 (over z, y, core).
Axes of the slice: x: 2, y: 2, z: 4, core: 2. Of those that a mesh axis runs over, the one named last changes fastest.
Arguments:
- images: bfloat16 [4, 2048, 3072], P('groups', 'seq'), parts along dimension 0, may hold values from -6 to 6
- w_qkv: bfloat16 [3072, 1152], replicated, may hold values from -0.109375 to 0.109375
- b_qkv: float32 [1152], replicated, may hold values from -3 to 3
- q_gain: float32 [128], replicated, may hold values from 0.5 to 2.5
- k_gain: float32 [128], replicated, may hold values from 0.5 to 2.5
- key_basis: float32 [3, 128, 32], replicated, may hold values from -0.5 to 0.5
- value_basis: float32 [3, 128, 32], replicated, may hold values from -0.5 to 0.5
- centers: float32 [4, 2, 3, 128], P('groups'), parts along dimension 0, may hold values from -22 to 22
- refresh: int32 [2, 3], replicated, may hold values 0 or 1
- w_out: bfloat16 [384, 3072], replicated, may hold values from -0.3125 to 0.3125
Outputs:
- mixed: bfloat16 [4, 2048, 3072], P('groups', 'seq'), parts along dimension 0
- new_centers: float32 [4, 2, 3, 128], P('groups'), parts along dimension 0
There are 2 independent parts, one for each index of `groups`. A program takes and returns all parts, laid end to end along the dimension named above; an argument that names none is the same for every part. Nothing has to cross between parts.
All inputs are finite; a program needn't handle non-finite values.
Results may differ from a plain program's by a relative error of at most 0.0051.
Values may be sent and summed in bfloat16 or wider, within the bound.
No kernel may reach another device: no remote copies, remote signals or barrier semaphores. Data moves between devices by JAX's collectives and lax.ppermute only.
A program may use at most 64 MiB of HBM per device.

v0:
```python
import math

import jax
import jax.numpy as jnp
from jax import lax
from jax.sharding import PartitionSpec as P

epsilon = 1e-06
highest = lax.Precision.HIGHEST


def normalize(values, gain):
    mean_square = jnp.mean(values * values, axis=-1, keepdims=True)
    return values * lax.rsqrt(mean_square + epsilon) * gain


def per_device(
    images, w_qkv, b_qkv, q_gain, k_gain, key_basis, value_basis, centers, refresh, w_out
):
    sample_count, tokens_dev, model_width = images.shape
    head_count, head_dim, code_rank = key_basis.shape
    seq_count = lax.axis_size("seq")
    first_row = lax.axis_index("seq") * tokens_dev
    factor = 1.0 / math.sqrt(head_dim)
    flat_images = images.reshape(sample_count * tokens_dev, model_width)
    projected = jnp.dot(flat_images, w_qkv, preferred_element_type=jnp.float32) + b_qkv
    projected = projected.reshape(sample_count, tokens_dev, 3, head_count, head_dim)
    queries = normalize(projected[:, :, 0], q_gain)
    keys_local = normalize(projected[:, :, 1], k_gain)
    values_local = projected[:, :, 2]
    key_center = centers[:, 0]
    value_center = centers[:, 1]
    key_codes = jnp.einsum(
        "bthd,hdr->bthr", keys_local - key_center[:, None], key_basis, precision=highest
    ).astype(jnp.bfloat16)
    value_codes = jnp.einsum(
        "bthd,hdr->bthr", values_local - value_center[:, None], value_basis, precision=highest
    ).astype(jnp.bfloat16)
    local_sums = jnp.stack([jnp.sum(keys_local, axis=1), jnp.sum(values_local, axis=1)], axis=1)
    summed = lax.psum(local_sums, "seq")
    fresh_means = summed / (tokens_dev * seq_count)
    new_centers = jnp.where(refresh[None, :, :, None] == 1, fresh_means, centers)
    query_heads = queries.transpose(0, 2, 1, 3)
    key_heads = keys_local.transpose(0, 2, 1, 3)
    value_heads = values_local.transpose(0, 2, 1, 3)
    near_scores = jnp.einsum("bhqd,bhsd->bhqs", query_heads, key_heads, precision=highest) * factor
    start_max = jnp.max(near_scores, axis=-1)
    near_weights = jnp.exp(near_scores - start_max[..., None])
    start_sum = jnp.sum(near_weights, axis=-1)
    start_weighted = jnp.einsum("bhqs,bhsd->bhqd", near_weights, value_heads, precision=highest)
    packed = jnp.stack([key_codes, value_codes], axis=2)
    packed = packed.transpose(1, 0, 2, 3, 4).reshape(
        tokens_dev, sample_count, 2 * head_count * code_rank
    )

    def absorb(running, code_block, owned, low_sample, high_sample):
        row_max, row_sum, weighted = running
        block_values = code_block.astype(jnp.float32)
        key_part = block_values[:, :, 0]
        value_part = block_values[:, :, 1]
        key_rebuilt = (
            jnp.einsum("sbhr,hdr->bhsd", key_part, key_basis, precision=highest)
            + key_center[low_sample:high_sample, :, None, :]
        )
        scores = jnp.einsum("bhqd,bhsd->bhqs", query_heads, key_rebuilt, precision=highest) * factor
        scores = jnp.where(owned[None, None, None, :], -jnp.inf, scores)
        new_max = jnp.maximum(row_max, jnp.max(scores, axis=-1))
        fading = jnp.exp(row_max - new_max)
        weights = jnp.exp(scores - new_max[..., None])
        weight_sum = jnp.sum(weights, axis=-1)
        value_rebuilt = (
            jnp.einsum("sbhr,hdr->bhsd", value_part, value_basis, precision=highest)
            + value_center[low_sample:high_sample, :, None, :]
        )
        addition = jnp.einsum("bhqs,bhsd->bhqd", weights, value_rebuilt, precision=highest)
        return (new_max, row_sum * fading + weight_sum, weighted * fading[..., None] + addition)

    start_state = (start_max, start_sum, start_weighted)
    whole_codes = packed.reshape(tokens_dev, sample_count * 2 * head_count * code_rank)
    shard_codes = lax.all_gather(whole_codes, "seq", axis=0, tiled=True)
    row_count = shard_codes.shape[0]
    code_block = shard_codes.reshape(row_count, sample_count - 0, 2, head_count, code_rank)
    positions = jnp.arange(row_count, dtype=jnp.int32)
    owned = (positions >= first_row) & (positions < first_row + tokens_dev)
    block_rows = 512
    block_count = row_count // block_rows

    def advance(inner, blocks):
        return (absorb(inner, blocks[0], blocks[1], 0, sample_count), None)

    stacked = (
        code_block.reshape(block_count, block_rows, sample_count - 0, 2, head_count, code_rank),
        owned.reshape(block_count, block_rows),
    )
    result, unused = lax.scan(advance, start_state, stacked)
    final_max, final_sum, final_weighted = result
    attended = (final_weighted / final_sum[..., None]).transpose(0, 2, 1, 3)
    attended = attended.reshape(sample_count * tokens_dev, head_count * head_dim).astype(
        jnp.bfloat16
    )
    mixed = jnp.dot(attended, w_out, preferred_element_type=jnp.float32).astype(jnp.bfloat16)
    return (mixed.reshape(sample_count, tokens_dev, model_width), new_centers)


def solution(mesh):
    return jax.shard_map(
        per_device,
        mesh=mesh,
        in_specs=(
            P("groups", "seq", None),
            P(),
            P(),
            P(),
            P(),
            P(),
            P(),
            P("groups", None, None, None),
            P(),
            P(),
        ),
        out_specs=(P("groups", "seq", None), P("groups", None, None, None)),
        check_vma=False,
    )
```

profile of v0, /device:TPU:0, one launch (start us, length us, event | category | flops | bytes accessed | tf_op | source)
XLA Modules:
  0.0 120.2 jit_solution(16905698591683552414)
XLA Ops:
  7.2 0.0 copy-start
  7.2 0.0 all-gather.2.cloned.1.call-start
  7.2 5.8 %convolution_add_fusion = f32[256,1152]{1,0:T(8,128)S(1)} fusion(bf16[256,3072]{1,0:T(8,128)(2,1)} %bitcast.143, bf16[3072,1152]{1,0:T(8,128)(2,1)} %param.13, f32[1152]{0:T(1024)} %param.14), kind=kOutput, calls=%fused_computation.24 | convolution fusion | flops 1812234240 | bytes 9835008 | tf_op jit(solution)/shard_map/dot_general | solution.py:26
  13.0 1.4 %copy.42 = f32[256,1152]{0,1:T(8,128)} copy(f32[256,1152]{1,0:T(8,128)S(1)} %convolution_add_fusion) | data formatting | bytes 2359296 | tf_op jit(solution)/shard_map/add | solution.py:26
  14.4 1.9 %reshape.48 = f32[2,128,3,3,128]{1,0,4,3,2:T(2,128)S(1)} reshape(f32[256,1152]{0,1:T(8,128)} %copy.42) | data formatting | bytes 2359296 | tf_op jit(solution)/shard_map/reshape | solution.py:27
  16.3 0.0 copy-start.11
  16.3 0.9 multiply_reduce_fusion
  17.2 1.8 %slice_reduce_fusion = (f32[2,3,128]{0,2,1:T(8,128)}, f32[2,128,1,3,128]{1,0,4,3,2:T(2,128)}) fusion(f32[2,128,3,3,128]{1,0,4,3,2:T(2,128)S(1)} %reshape.48), kind=kLoop, calls=%fused_computation.64 | loop fusion | flops 97536 | bytes 789504 | tf_op jit(solution)/shard_map/reduce_sum | solution.py:39
  18.9 1.9 %copy.64 = f32[2,128,1,3,128]{4,1,3,0,2:T(8,128)} copy(f32[2,128,1,3,128]{1,0,4,3,2:T(2,128)} %get-tuple-element.119) | data formatting | bytes 786432
  20.8 0.0 copy-done.11
  20.9 0.8 copy.48
  21.7 0.7 add_rsqrt_fusion
  22.4 0.0 copy-start.1
  22.4 0.0 copy-start.5
  22.5 2.6 %fusion.32 = (f32[2,3,128]{0,2,1:T(8,128)}, f32[2,128,3,128]{1,0,3,2:T(2,128)S(1)}, f32[2,3,128,128]{2,0,3,1:T(2,128)}) fusion(f32[128]{0:T(128)} %param.16, f32[2,128,3]{1,0,2:T(2,128)S(1)} %get-tuple-element.129, f32[2,128,3,3,128]{1,0,4,3,2:T(2,128)S(1)} %reshape.48, f32[128]{0:T(128)} %param.15, f32[2,128,3]{1,0,2:T(2,128)S(1)} %get-tuple-element.130), kind=kLoop, calls=%fused_computation.65 | loop fusion | flops 490752 | bytes 1583104 | tf_op jit(solution)/shard_map/reduce_sum | solution.py:39
  25.0 0.5 broadcast_subtract_fusion
  25.5 0.3 fusion.15
  25.9 0.5 fusion.16
  26.4 0.6 copy.52
  27.1 0.0 all-gather.2.cloned.1.call-update
  27.1 1.2 copy.43
  28.3 1.6 %copy.56 = f32[2,3,128]{2,0,1:T(2,128)} copy(f32[2,3,128]{0,2,1:T(8,128)} %get-tuple-element.114) | data formatting | bytes 6144 | tf_op jit(solution)/shard_map/reduce_sum | solution.py:39
  29.9 1.6 %copy.57 = f32[2,3,128]{2,0,1:T(2,128)} copy(f32[2,3,128]{0,2,1:T(8,128)} %get-tuple-element.118) | data formatting | bytes 6144 | tf_op jit(solution)/shard_map/reduce_sum | solution.py:39
  31.5 0.7 pad_maximum_fusion
  32.2 36.7 %psum.7 = f32[2,2,3,128]{3,0,2,1:T(2,128)} all-reduce(f32[2,2,3,128]{3,0,2,1:T(2,128)S(1)} %pad_maximum_fusion), channel_id=1, replica_groups=mesh['groups'=2,'seq'=16] {'seq'}, use_global_device_ids=true, to_apply=%region_10.11 | all-reduce | flops 1536 | bytes 12288 | tf_op jit(solution)/shard_map/psum | solution.py:40
  68.9 0.7 broadcast_compare_fusion
  69.5 0.8 copy_select_fusion
  70.3 0.6 copy.59
  70.9 0.6 fusion.31
  71.5 0.8 fusion.36
  72.4 0.1 fusion.22
  72.5 0.8 fusion.17
  73.3 0.0 all-gather.2.cloned.1.call-done
  73.3 3.9 %reshape_reshape.7 = bf16[4,512,2,2,3,32]{1,0,5,4,3,2:T(4,128)(2,1)} reshape(bf16[2048,384]{0,1:T(8,128)(2,1)} %all-gather.2.cloned.1.call-done) | data formatting | bytes 3145728 | tf_op jit(solution)/shard_map/reshape;reshape | solution.py:92
  77.2 2.9 %copy.53 = bf16[4,512,2,2,3,32]{1,5,4,2,3,0:T(8,128)(2,1)} copy(bf16[4,512,2,2,3,32]{1,0,5,4,3,2:T(4,128)(2,1)} %reshape_reshape.7) | data formatting | bytes 3145728 | tf_op jit(solution)/shard_map/while | solution.py:95
  80.1 0.0 copy-done.10
  80.1 30.7 %while.14 = (s32[]{:T(128)}, f32[2,3,128]{2,1,0:T(4,128)S(1)}, f32[2,3,128]{2,1,0:T(4,128)S(1)}, f32[2,3,128,128]{3,2,1,0:T(8,128)S(1)}, pred[4,512]{1,0:T(4,128...) while((s32[]{:T(128)}, f32[2,3,128]{2,1,0:T(4,128)S(1)}, ...), condition=%wide.region_7.8_spmd, body=%wide.region_4.7_spmd.sunk | while | flops 1513293312 | bytes 13524605 | solution.py:95
  80.1 1.0 dynamic-slice_bitcast_fusion.2
  81.1 0.9 fusion.54
  82.1 1.6 %bitcast_reduce_fusion.2 = (f32[2,3,128]{2,1,0:T(4,128)S(1)}, f32[2,3,512,128]{3,2,1,0:T(8,128)S(1)}) fusion(f32[2,3,128,128]{3,2,1,0:T(8,128)S(1)} %get-tuple-element.240, f32[3,512,2,128]{3,1,0,2:T(8,128)S(1)} %fusion.54, f32[2,3,128]{2,1,0:T(4,128)S(1)} %bitcast.140, pred[512]{0:T(512)(128)(4,1)S(1)} %dynamic-slice_reduce_fusion.2), kind=kOutput, calls=%fused_computation.3.clone.1 | convolution fusion | flops 605551872 | bytes 3545600 | tf_op jit(solution)/shard_map/while/body/eval_jaxpr/bhqd,bhsd->bhqs/dot_general | solution.py:65
  83.7 0.2 fusion.55
  84.0 0.9 fusion.56
  84.9 2.9 %fusion.57 = f32[2,3,128,128]{3,2,1,0:T(8,128)S(1)} fusion(f32[3,512,2,128]{3,1,0,2:T(8,128)S(1)} %fusion.56, f32[2,3,512,128]{3,2,1,0:T(8,128)S(1)} %get-tuple-element.205, f32[2,3,128]{2,1,0:T(4,128)S(1)} %bitcast.139, f32[2,3,128]{2,1,0:T(4,128)S(1)} %max.4, f32[2,3,128,128]{3,2,1,0:T(8,128)S(1)} %get-tuple-element.223, ...), kind=kOutput, calls=%fused_computation.9.clone.1 | convolution fusion | flops 604962816 | bytes 3941376 | tf_op jit(solution)/shard_map/while/body/eval_jaxpr/bhqs,bhsd->bhqd/dot_general | solution.py:75
  87.8 1.0 dynamic-slice_bitcast_fusion.2
  88.8 0.9 fusion.54
  89.7 1.6 %bitcast_reduce_fusion.2 = (f32[2,3,128]{2,1,0:T(4,128)S(1)}, f32[2,3,512,128]{3,2,1,0:T(8,128)S(1)}) fusion(f32[2,3,128,128]{3,2,1,0:T(8,128)S(1)} %get-tuple-element.240, f32[3,512,2,128]{3,1,0,2:T(8,128)S(1)} %fusion.54, f32[2,3,128]{2,1,0:T(4,128)S(1)} %bitcast.140, pred[512]{0:T(512)(128)(4,1)S(1)} %dynamic-slice_reduce_fusion.2), kind=kOutput, calls=%fused_computation.3.clone.1 | convolution fusion | flops 605551872 | bytes 3545600 | tf_op jit(solution)/shard_map/while/body/eval_jaxpr/bhqd,bhsd->bhqs/dot_general | solution.py:65
  91.4 0.2 fusion.55
  91.7 0.9 fusion.56
  92.6 2.9 %fusion.57 = f32[2,3,128,128]{3,2,1,0:T(8,128)S(1)} fusion(f32[3,512,2,128]{3,1,0,2:T(8,128)S(1)} %fusion.56, f32[2,3,512,128]{3,2,1,0:T(8,128)S(1)} %get-tuple-element.205, f32[2,3,128]{2,1,0:T(4,128)S(1)} %bitcast.139, f32[2,3,128]{2,1,0:T(4,128)S(1)} %max.4, f32[2,3,128,128]{3,2,1,0:T(8,128)S(1)} %get-tuple-element.223, ...), kind=kOutput, calls=%fused_computation.9.clone.1 | convolution fusion | flops 604962816 | bytes 3941376 | tf_op jit(solution)/shard_map/while/body/eval_jaxpr/bhqs,bhsd->bhqd/dot_general | solution.py:75
  95.5 1.0 dynamic-slice_bitcast_fusion.2
  96.5 0.9 fusion.54
  97.4 1.6 %bitcast_reduce_fusion.2 = (f32[2,3,128]{2,1,0:T(4,128)S(1)}, f32[2,3,512,128]{3,2,1,0:T(8,128)S(1)}) fusion(f32[2,3,128,128]{3,2,1,0:T(8,128)S(1)} %get-tuple-element.240, f32[3,512,2,128]{3,1,0,2:T(8,128)S(1)} %fusion.54, f32[2,3,128]{2,1,0:T(4,128)S(1)} %bitcast.140, pred[512]{0:T(512)(128)(4,1)S(1)} %dynamic-slice_reduce_fusion.2), kind=kOutput, calls=%fused_computation.3.clone.1 | convolution fusion | flops 605551872 | bytes 3545600 | tf_op jit(solution)/shard_map/while/body/eval_jaxpr/bhqd,bhsd->bhqs/dot_general | solution.py:65
  99.1 0.2 fusion.55
  99.3 0.9 fusion.56
  100.2 2.9 %fusion.57 = f32[2,3,128,128]{3,2,1,0:T(8,128)S(1)} fusion(f32[3,512,2,128]{3,1,0,2:T(8,128)S(1)} %fusion.56, f32[2,3,512,128]{3,2,1,0:T(8,128)S(1)} %get-tuple-element.205, f32[2,3,128]{2,1,0:T(4,128)S(1)} %bitcast.139, f32[2,3,128]{2,1,0:T(4,128)S(1)} %max.4, f32[2,3,128,128]{3,2,1,0:T(8,128)S(1)} %get-tuple-element.223, ...), kind=kOutput, calls=%fused_computation.9.clone.1 | convolution fusion | flops 604962816 | bytes 3941376 | tf_op jit(solution)/shard_map/while/body/eval_jaxpr/bhqs,bhsd->bhqd/dot_general | solution.py:75
  103.1 1.0 dynamic-slice_bitcast_fusion.2
  104.2 0.9 fusion.54
  105.1 1.6 %bitcast_reduce_fusion.2 = (f32[2,3,128]{2,1,0:T(4,128)S(1)}, f32[2,3,512,128]{3,2,1,0:T(8,128)S(1)}) fusion(f32[2,3,128,128]{3,2,1,0:T(8,128)S(1)} %get-tuple-element.240, f32[3,512,2,128]{3,1,0,2:T(8,128)S(1)} %fusion.54, f32[2,3,128]{2,1,0:T(4,128)S(1)} %bitcast.140, pred[512]{0:T(512)(128)(4,1)S(1)} %dynamic-slice_reduce_fusion.2), kind=kOutput, calls=%fused_computation.3.clone.1 | convolution fusion | flops 605551872 | bytes 3545600 | tf_op jit(solution)/shard_map/while/body/eval_jaxpr/bhqd,bhsd->bhqs/dot_general | solution.py:65
  106.7 0.2 fusion.55
  107.0 0.9 fusion.56
  107.9 2.9 %fusion.57 = f32[2,3,128,128]{3,2,1,0:T(8,128)S(1)} fusion(f32[3,512,2,128]{3,1,0,2:T(8,128)S(1)} %fusion.56, f32[2,3,512,128]{3,2,1,0:T(8,128)S(1)} %get-tuple-element.205, f32[2,3,128]{2,1,0:T(4,128)S(1)} %bitcast.139, f32[2,3,128]{2,1,0:T(4,128)S(1)} %max.4, f32[2,3,128,128]{3,2,1,0:T(8,128)S(1)} %get-tuple-element.223, ...), kind=kOutput, calls=%fused_computation.9.clone.1 | convolution fusion | flops 604962816 | bytes 3941376 | tf_op jit(solution)/shard_map/while/body/eval_jaxpr/bhqs,bhsd->bhqd/dot_general | solution.py:75
  110.8 0.2 fusion.26
  111.0 0.2 copy.55
  111.2 2.2 %convolution_convert_fusion = bf16[256,3072]{1,0:T(8,128)(2,1)} fusion(bf16[384,3072]{1,0:T(8,128)(2,1)S(1)} %copy-done, bf16[48,8,2,128]{3,2,1,0:T(2,128)(2,1)S(1)} %bitcast.137), kind=kOutput, calls=%fused_computation.23 | convolution fusion | flops 604766208 | bytes 4128768 | tf_op jit(solution)/shard_map/dot_general | solution.py:101
  (37 shorter events, 0.3 us)
Async XLA Ops:
  7.2 104.0 %copy-start = (bf16[384,3072]{1,0:T(8,128)(2,1)S(1)}, bf16[384,3072]{1,0:T(8,128)(2,1)}, u32[]{:S(2)}) copy-start(bf16[384,3072]{1,0:T(8,128)(2,1)} %param.21) | copy-start | bytes 7077892
  7.2 66.1 %all-gather.2.cloned.1.call-start = ((), (), s32[]{:S(2)}) async-start(), calls=%async_computation | async-start | bytes 1671168 | tf_op jit(solution)/shard_map/all_gather | solution.py:80
  16.3 4.6 %copy-start.11 = (f32[2,2,3,128]{3,1,2,0:T(2,128)S(1)}, f32[2,2,3,128]{3,1,2,0:T(2,128)}, u32[]{:S(2)}) copy-start(f32[2,2,3,128]{3,1,2,0:T(2,128)} %param.19) | copy-start | bytes 18436
  21.7 3.3 %copy-start.9 = (f32[2,3,128]{0,2,1:T(8,128)S(1)}, f32[2,3,128]{0,2,1:T(8,128)}, u32[]{:S(2)}) copy-start(f32[2,3,128]{0,2,1:T(8,128)} %copy.48) | copy-start | bytes 9220
  21.7 3.8 %copy-start.7 = (f32[3,128,32]{1,2,0:T(8,128)S(1)}, f32[3,128,32]{1,2,0:T(8,128)}, u32[]{:S(2)}) copy-start(f32[3,128,32]{1,2,0:T(8,128)} %param.17) | copy-start | bytes 147460
  22.4 3.4 %copy-start.1 = (f32[2,128,1,3,128]{4,1,3,0,2:T(8,128)S(1)}, f32[2,128,1,3,128]{4,1,3,0,2:T(8,128)}, u32[]{:S(2)}) copy-start(f32[2,128,1,3,128]{4,1,3,0,2:T(8,128)} %copy.64) | copy-start | bytes 1179652
  22.4 3.4 %copy-start.5 = (f32[3,128,32]{1,2,0:T(8,128)S(1)}, f32[3,128,32]{1,2,0:T(8,128)}, u32[]{:S(2)}) copy-start(f32[3,128,32]{1,2,0:T(8,128)} %param.18) | copy-start | bytes 147460
  25.0 1.4 %copy-start.3 = (f32[2,128,3,128]{1,0,3,2:T(2,128)}, f32[2,128,3,128]{1,0,3,2:T(2,128)S(1)}, u32[]{:S(2)}) copy-start(f32[2,128,3,128]{1,0,3,2:T(2,128)S(1)} %get-tuple-element.115) | copy-start | bytes 1179652
  26.4 45.1 %copy-start.4 = (f32[2,128,3,128]{1,0,3,2:T(2,128)S(1)}, f32[2,128,3,128]{1,0,3,2:T(2,128)}, u32[]{:S(2)}) copy-start(f32[2,128,3,128]{1,0,3,2:T(2,128)} %copy-done.3) | copy-start | bytes 1179652
  26.4 46.0 %copy-start.2 = (f32[2,128,1,3,128]{4,1,3,0,2:T(8,128)S(1)}, f32[2,128,1,3,128]{4,1,3,0,2:T(8,128)}, u32[]{:S(2)}) copy-start(f32[2,128,1,3,128]{4,1,3,0,2:T(8,128)} %copy.64) | copy-start | bytes 1179652
  77.2 2.9 %copy-start.6 = (f32[3,128,32]{1,2,0:T(8,128)S(1)}, f32[3,128,32]{1,2,0:T(8,128)}, u32[]{:S(2)}) copy-start(f32[3,128,32]{1,2,0:T(8,128)} %param.18) | copy-start | bytes 147460
  77.2 2.9 %copy-start.8 = (f32[3,128,32]{1,2,0:T(8,128)S(1)}, f32[3,128,32]{1,2,0:T(8,128)}, u32[]{:S(2)}) copy-start(f32[3,128,32]{1,2,0:T(8,128)} %param.17) | copy-start | bytes 147460
  77.2 2.9 %copy-start.10 = (pred[4,512]{1,0:T(4,128)(4,1)S(1)}, pred[4,512]{1,0:T(4,128)(4,1)}, u32[]{:S(2)}) copy-start(pred[4,512]{1,0:T(4,128)(4,1)} %fusion.31) | copy-start | bytes 6148
Sparse Core Ops, SparseCore 0:
  27.2 42.0 all-gather.1
where the time goes:
time: 121 us; the launch traced here: 120 us
  blocking collectives  36.7 us (30%)
  matrix products  35.6 us (29%)
  local copies, waits for them, and re-layouts  22.8 us (19%)
  between operations  14.3 us (12%)
  other arithmetic  10.5 us (9%)
    psum x1, blocking collectives, per_device(): summed = lax.psum(local_sums, 'seq')  36.7 us
    dot_general x4, matrix products, absorb(): jnp.einsum('bhqs,bhsd->bhqd', weights, value_rebuilt, precision=highest)  11.5 us
    dot_general x4, matrix products, absorb(): jnp.einsum('bhqd,bhsd->bhqs', query_heads, key_rebuilt, precision=highest)  6.57 us
    dot_general x1, matrix products, per_device(): jnp.dot(flat_images, w_qkv, preferred_element_type=jnp.float32) + b_qkv  5.77 us
    squeeze x4, local copies, waits for them, and re-layouts, per_device(): result, unused = lax.scan(advance, start_state, stacked)  4.1 us
    another operation x1, local copies, waits for them, and re-layouts, per_device(): code_block.reshape(block_count, block_rows, sample_count - 0, 2, head_cou...  3.85 us
    dot_general x4, matrix products, absorb(): jnp.einsum('sbhr,hdr->bhsd', key_part, key_basis, precision=highest)  3.58 us
    dot_general x4, matrix products, absorb(): jnp.einsum('sbhr,hdr->bhsd', value_part, value_basis, precision=highest)  3.56 us
  transfers between devices with their start and end apart: 1, of which 0 were waited for; matrix products, arithmetic and copies ran while one was open for 8% of the time, Pallas kernels for 0%

commit v1 on v0

v1 whole, which is shorter than its diff:
```python
import functools
import math

import jax
import jax.numpy as jnp
from jax import lax
from jax.experimental import pallas as pl
from jax.experimental.pallas import tpu as pltpu
from jax.sharding import PartitionSpec as P

epsilon = 1e-06
f32 = jnp.float32
bf16 = jnp.bfloat16
SUM_ROWS = 16
NT = (((1,), (1,)), ((), ()))
NN = (((1,), (0,)), ((), ()))


def dot(a, b, dims=NN):
    return lax.dot_general(a, b, dims, preferred_element_type=f32)


def split(x):
    high = x.astype(bf16)
    low = (x - high.astype(f32)).astype(bf16)
    return high, low


def dot3(a, b, dims=NN):
    return dot(a[0], b[0], dims) + (dot(a[0], b[1], dims) + dot(a[1], b[0], dims))


def lane_ids(rows, lanes):
    return lax.broadcasted_iota(jnp.int32, (rows, lanes), 1)


def key_lane(sample, head, rank):
    return head * rank if sample == 0 else (head + 1) * rank


def value_lane(sample, head, rank, heads):
    if head == 0:
        return heads * rank if sample == 0 else 0
    return ((heads - 1) * sample + head - 1) * rank


def free_lane(sample, rank):
    return 2 * rank if sample == 0 else rank


def project_kernel(
    images_ref, w_ref, b_ref, qg_ref, kg_ref, kb_ref, vb_ref, centers_ref,
    payload_ref, query_ref, qkv_ref, acc_ref, tiles_h, tiles_l, last_h, last_l, sums_ref,
    *, samples, tokens, heads, dim, rank, log_factor,
):
    step = pl.program_id(0)
    width = heads * dim
    part = dot(images_ref[...], w_ref[...])

    @pl.when(step == 0)
    def _():
        acc_ref[...] = part
        tiles_h[...] = jnp.zeros_like(tiles_h)
        tiles_l[...] = jnp.zeros_like(tiles_l)
        last_h[...] = jnp.zeros_like(last_h)
        last_l[...] = jnp.zeros_like(last_l)
        sums_ref[...] = jnp.zeros_like(sums_ref)
        for h in range(heads):
            kh, kl = split(kb_ref[h])
            vh, vl = split(vb_ref[h])
            for b in range(samples):
                at = key_lane(b, h, rank)
                tiles_h[b, at : at + rank, h * dim : (h + 1) * dim] = kh
                tiles_l[b, at : at + rank, h * dim : (h + 1) * dim] = kl
                at = value_lane(b, h, rank, heads)
                if h == 0:
                    tiles_h[b, at : at + rank, width : width + dim] = vh
                    tiles_l[b, at : at + rank, width : width + dim] = vl
                else:
                    last_h[at : at + rank, (h - 1) * dim : h * dim] = vh
                    last_l[at : at + rank, (h - 1) * dim : h * dim] = vl

    @pl.when(step > 0)
    def _():
        acc_ref[...] += part

    @pl.when(step == pl.num_programs(0) - 1)
    def _():
        def normed(column, gain):
            x = acc_ref[:, column : column + dim] + b_ref[:, column : column + dim]
            mean_square = jnp.mean(x * x, axis=-1, keepdims=True)
            return x * lax.rsqrt(mean_square + epsilon) * gain

        queries, keys, values = [], [], []
        for h in range(heads):
            at = h * dim
            q = normed(at, qg_ref[...])
            k = normed(width + at, kg_ref[...])
            v = acc_ref[:, 2 * width + at : 2 * width + at + dim]
            v = v + b_ref[:, 2 * width + at : 2 * width + at + dim]
            queries.append(q)
            keys.append(k)
            values.append(v)
            for b in range(samples):
                rows = slice(b * tokens, (b + 1) * tokens)
                row = (b * heads + h) * 2
                sums_ref[row : row + 1, :] = jnp.sum(k[rows], axis=0, keepdims=True)
                sums_ref[row + 1 : row + 2, :] = jnp.sum(v[rows], axis=0, keepdims=True)
        rest = sums_ref[...]
        for piece in range(3):
            top = rest.astype(bf16)
            payload_ref[0, tokens : tokens + SUM_ROWS, piece * dim : (piece + 1) * dim] = top
            rest = rest - top.astype(f32)
        lasts = []
        for b in range(samples):
            rows = slice(b * tokens, (b + 1) * tokens)
            shifted = [keys[h][rows] - centers_ref[b, h, 0:1, :] for h in range(heads)]
            shifted += [values[h][rows] - centers_ref[b, h, 1:2, :] for h in range(heads)]
            main = split(jnp.concatenate(shifted[: heads + 1], axis=1))
            code = dot3(main, (tiles_h[b], tiles_l[b]), NT)
            payload_ref[0, :tokens, b * dim : (b + 1) * dim] = code.astype(bf16)
            tail = split(jnp.concatenate(shifted[heads + 1 :], axis=1))
            lasts.append(dot3(tail, (last_h[...], last_l[...]), NT))
            query = split(jnp.concatenate([q[rows] for q in queries], axis=1))
            query_code = dot3(query, (tiles_h[b, :, :width], tiles_l[b, :, :width]), NT)
            high, low = split(query_code * log_factor)
            query_ref[rows, :dim] = high
            query_ref[rows, dim:] = low
        lanes = lane_ids(tokens, dim)
        last = jnp.where(lanes < (heads - 1) * rank, lasts[0], lasts[1])
        payload_ref[0, :tokens, samples * dim :] = last.astype(bf16)
        for h in range(heads):
            qkv_ref[:, h * dim : (h + 1) * dim] = queries[h] * log_factor
            qkv_ref[:, width + h * dim : width + (h + 1) * dim] = keys[h]
            qkv_ref[:, 2 * width + h * dim : 2 * width + (h + 1) * dim] = values[h]


def near_kernel(qkv_ref, centers_ref, acc_ref, stat_ref, *, samples, tokens, heads, dim):
    width = heads * dim
    lanes = lane_ids(tokens, dim)
    for b in range(samples):
        rows = slice(b * tokens, (b + 1) * tokens)
        stats = jnp.zeros((tokens, dim), f32)
        for h in range(heads):
            q = qkv_ref[rows, h * dim : (h + 1) * dim]
            k = split(qkv_ref[rows, width + h * dim : width + (h + 1) * dim])
            v = split(qkv_ref[rows, 2 * width + h * dim : 2 * width + (h + 1) * dim])
            scores = dot3(split(q), k, NT)
            row_max = jnp.max(scores, axis=-1, keepdims=True)
            weights = jnp.exp2(scores - row_max)
            row_sum = jnp.sum(weights, axis=-1, keepdims=True)
            acc_ref[rows, h * dim : (h + 1) * dim] = dot3(split(weights), v)
            center = jnp.sum(q * centers_ref[b, h, 0:1, :], axis=-1, keepdims=True)
            stats = jnp.where(lanes == h, row_max, stats)
            stats = jnp.where(lanes == heads + h, row_sum, stats)
            stats = jnp.where(lanes == 2 * heads + h, center, stats)
        stat_ref[rows, :] = stats


def code_attention(query_ref, tiles, out_ref, *, samples, tokens, heads, dim, rank):
    lanes = lane_ids(tokens, dim)
    for b in range(samples):
        rows = slice(b * tokens, (b + 1) * tokens)
        high = query_ref[rows, :dim]
        low = query_ref[rows, dim:]
        stacked = []
        for h in range(heads):
            at = key_lane(b, h, rank)
            own = (lanes >= at) & (lanes < at + rank)
            zero = jnp.zeros_like(high)
            stacked.append(
                jnp.concatenate([jnp.where(own, high, zero), jnp.where(own, low, zero)], axis=1)
            )
        left = jnp.concatenate(stacked, axis=0)
        scores = []
        for ref, i in tiles:
            code = ref[i, :tokens, b * dim : (b + 1) * dim]
            scores.append(dot(left, jnp.concatenate([code, code], axis=1), NT))
        best = scores[0]
        for part in scores[1:]:
            best = jnp.maximum(best, part)
        row_max = jnp.max(best, axis=-1, keepdims=True)
        total = jnp.zeros_like(best)
        result = jnp.zeros((heads * tokens, 2 * dim), f32)
        for part, (ref, i) in zip(scores, tiles):
            weights = jnp.exp2(part - row_max).astype(bf16)
            total = total + weights.astype(f32)
            values = jnp.concatenate(
                [ref[i, :tokens, b * dim : (b + 1) * dim], ref[i, :tokens, samples * dim :]], axis=1
            )
            result = result + dot(weights, values)
        row_sum = jnp.sum(total, axis=-1, keepdims=True)
        out = jnp.zeros((tokens, dim), f32)
        for h in range(heads):
            head_rows = slice(h * tokens, (h + 1) * tokens)
            at = value_lane(b, h, rank, heads)
            part = result[head_rows, :dim] if h == 0 else result[head_rows, dim:]
            out = jnp.where((lanes >= at) & (lanes < at + rank), part, out)
            spot = free_lane(b, rank)
            out = jnp.where(lanes == spot + h, row_max[head_rows], out)
            out = jnp.where(lanes == spot + heads + h, row_sum[head_rows], out)
        out_ref[rows, :] = out


def tree_sum(parts):
    while len(parts) > 1:
        parts = [parts[i] + parts[i + 1] for i in range(0, len(parts), 2)]
    return parts[0]


def partner_kernel(query_ref, *refs, samples, tokens, heads, dim, rank, order):
    out_ref = refs[-1]
    tiles = [(ref, i) for ref in refs[:-1] for i in range(ref.shape[0])]
    parts = []
    for place in order:
        ref, i = tiles[place]
        rows = slice(tokens, tokens + SUM_ROWS)
        pieces = [ref[i, rows, p * dim : (p + 1) * dim].astype(f32) for p in range(3)]
        parts.append(pieces[0] + (pieces[1] + pieces[2]))
    out_ref[samples * tokens :, :] = tree_sum(parts)
    code_attention(
        query_ref, tiles, out_ref, samples=samples, tokens=tokens, heads=heads, dim=dim, rank=rank
    )


def own_kernel(query_ref, *refs, samples, tokens, heads, dim, rank):
    tiles = [(ref, i) for ref in refs[:-1] for i in range(ref.shape[0])]
    code_attention(
        query_ref, tiles, refs[-1], samples=samples, tokens=tokens, heads=heads, dim=dim, rank=rank
    )


def finish_kernel(
    back_ref, half_ref, own_ref, near_ref, stat_ref, centers_ref, refresh_ref, vb_ref, w_ref,
    mixed_ref, new_ref, attended_ref, basis_h, basis_l,
    *, samples, tokens, heads, dim, rank, length,
):
    @pl.when(pl.program_id(0) == 0)
    def _():
        basis_h[...] = jnp.zeros_like(basis_h)
        basis_l[...] = jnp.zeros_like(basis_l)
        for h in range(heads):
            vh, vl = split(vb_ref[h])
            for b in range(samples):
                at = value_lane(b, h, rank, heads)
                basis_h[b, at : at + rank, h * dim : (h + 1) * dim] = vh
                basis_l[b, at : at + rank, h * dim : (h + 1) * dim] = vl
        lanes = lane_ids(tokens, dim)
        for b in range(samples):
            rows = slice(b * tokens, (b + 1) * tokens)
            stats = stat_ref[rows, :]
            one, two = own_ref[rows, :], back_ref[rows, :]
            spot = free_lane(b, rank)
            scale_one = jnp.zeros((tokens, dim), f32)
            scale_two = jnp.zeros((tokens, dim), f32)
            rest = []
            for h in range(heads):
                center = stats[:, 2 * heads + h : 2 * heads + h + 1]
                near_max = stats[:, h : h + 1]
                max_one = one[:, spot + h : spot + h + 1] + center
                max_two = two[:, spot + h : spot + h + 1] + center
                top = jnp.maximum(near_max, jnp.maximum(max_one, max_two))
                near_scale = jnp.exp2(near_max - top)
                fade_one = jnp.exp2(max_one - top)
                fade_two = jnp.exp2(max_two - top)
                far_sum = fade_one * one[:, spot + heads + h : spot + heads + h + 1]
                far_sum = far_sum + fade_two * two[:, spot + heads + h : spot + heads + h + 1]
                whole = near_scale * stats[:, heads + h : heads + h + 1] + far_sum
                inverse = 1.0 / whole
                at = value_lane(b, h, rank, heads)
                own = (lanes >= at) & (lanes < at + rank)
                scale_one = jnp.where(own, fade_one * inverse, scale_one)
                scale_two = jnp.where(own, fade_two * inverse, scale_two)
                near = near_ref[rows, h * dim : (h + 1) * dim] * (near_scale * inverse)
                rest.append(near + (far_sum * inverse) * centers_ref[b, h, 1:2, :])
            codes = split(one * scale_one + two * scale_two)
            far = dot3(codes, (basis_h[b], basis_l[b]))
            attended_ref[rows, :] = (far + jnp.concatenate(rest, axis=1)).astype(bf16)
            for h in range(heads):
                for j in range(2):
                    row = samples * tokens + (b * heads + h) * 2 + j
                    row_sum = half_ref[row : row + 1, :] + back_ref[row : row + 1, :]
                    fresh = row_sum * (1.0 / length)
                    old = centers_ref[b, h, j : j + 1, :]
                    new_ref[b, h, j : j + 1, :] = jnp.where(refresh_ref[j, h] == 1, fresh, old)

    mixed_ref[...] = dot(attended_ref[...], w_ref[...]).astype(bf16)


VMEM = pl.BlockSpec(memory_space=pltpu.VMEM)


def per_device(
    images, w_qkv, b_qkv, q_gain, k_gain, key_basis, value_basis, centers, refresh, w_out
):
    samples, tokens, model = images.shape
    heads, dim, rank = key_basis.shape
    seq = lax.axis_size("seq")
    rows = samples * tokens
    width = heads * dim
    sizes = dict(samples=samples, tokens=tokens, heads=heads, dim=dim)
    log_factor = math.log2(math.e) / math.sqrt(dim)
    flat = images.reshape(rows, model)
    key_rows = key_basis.transpose(0, 2, 1)
    value_rows = value_basis.transpose(0, 2, 1)
    center_rows = centers.transpose(0, 2, 1, 3)
    depth = 512
    shard = (1, tokens + SUM_ROWS, width)
    whole = lambda *shape: pl.BlockSpec(shape, lambda i: (0,) * len(shape))
    params = lambda mib, **kw: pltpu.CompilerParams(vmem_limit_bytes=mib * 2**20, **kw)

    payload, query, qkv = pl.pallas_call(
        functools.partial(project_kernel, **sizes, rank=rank, log_factor=log_factor),
        grid=(model // depth,),
        in_specs=[
            pl.BlockSpec((rows, depth), lambda i: (0, i)),
            pl.BlockSpec((depth, 3 * width), lambda i: (i, 0)),
            whole(1, 3 * width),
            whole(1, dim),
            whole(1, dim),
            whole(heads, rank, dim),
            whole(heads, rank, dim),
            whole(samples, heads, 2, dim),
        ],
        out_specs=[whole(*shard), whole(rows, 2 * dim), whole(rows, 3 * width)],
        out_shape=[
            jax.ShapeDtypeStruct(shard, bf16),
            jax.ShapeDtypeStruct((rows, 2 * dim), bf16),
            jax.ShapeDtypeStruct((rows, 3 * width), f32),
        ],
        scratch_shapes=[
            pltpu.VMEM((rows, 3 * width), f32),
            pltpu.VMEM((samples, dim, width + dim), bf16),
            pltpu.VMEM((samples, dim, width + dim), bf16),
            pltpu.VMEM((dim, width - dim), bf16),
            pltpu.VMEM((dim, width - dim), bf16),
            pltpu.VMEM((SUM_ROWS, dim), f32),
        ],
        compiler_params=params(24),
        name="project",
    )(
        flat, w_qkv, b_qkv.reshape(1, -1), q_gain.reshape(1, -1), k_gain.reshape(1, -1),
        key_rows, value_rows, center_rows,
    )

    def swap(x, mask):
        return lax.ppermute(x, "seq", [(i, i ^ mask) for i in range(seq)])

    far_mask = seq // 2
    bits = [m for m in (2 ** i for i in range(1, seq.bit_length() - 1)) if m < far_mask]
    query_far = swap(query, far_mask)
    held = [(payload, [0])]
    direct = bits[:2]
    masks = [m for m in range(2, 2 * sum(direct), 2) if m & ~sum(direct) == 0] if direct else []
    for mask in masks:
        held.append((swap(payload, mask), [mask]))
    for bit in bits[2:]:
        block = jnp.concatenate([a for a, _ in held], axis=0)
        names = [m for _, ms in held for m in ms]
        held.append((swap(block, bit), [m ^ bit for m in names]))

    near, stats = pl.pallas_call(
        functools.partial(near_kernel, **sizes),
        in_specs=[VMEM, VMEM],
        out_specs=[VMEM, VMEM],
        out_shape=[
            jax.ShapeDtypeStruct((rows, width), f32),
            jax.ShapeDtypeStruct((rows, dim), f32),
        ],
        compiler_params=params(24),
        cost_estimate=pl.CostEstimate(
            flops=12 * rows * tokens * width, bytes_accessed=5 * rows * width * 4, transcendentals=0
        ),
        name="near",
    )(qkv, center_rows)

    held += [(swap(a, 1), [m ^ 1 for m in ms]) for a, ms in held]
    arrays = [a for a, _ in held]
    names = [m for _, ms in held for m in ms]
    order = tuple(names.index(m) for m in range(len(names)))
    far_flops = 8 * rows * tokens * len(names) * width
    cost = pl.CostEstimate(
        flops=far_flops, bytes_accessed=len(names) * 2 * tokens * width, transcendentals=0
    )
    back = pl.pallas_call(
        functools.partial(partner_kernel, **sizes, rank=rank, order=order),
        in_specs=[VMEM] * (1 + len(arrays)),
        out_specs=VMEM,
        out_shape=jax.ShapeDtypeStruct((rows + SUM_ROWS, dim), f32),
        compiler_params=params(32),
        cost_estimate=cost,
        name="partner",
    )(query_far, *arrays)
    returned = swap(back, far_mask)
    own = pl.pallas_call(
        functools.partial(own_kernel, **sizes, rank=rank),
        in_specs=[VMEM] * len(arrays),
        out_specs=VMEM,
        out_shape=jax.ShapeDtypeStruct((rows, dim), f32),
        compiler_params=params(32),
        cost_estimate=cost,
        name="own",
    )(query, *arrays[1:])

    columns = 1024
    mixed, new_centers = pl.pallas_call(
        functools.partial(finish_kernel, **sizes, rank=rank, length=tokens * seq),
        grid=(model // columns,),
        in_specs=[
            whole(rows + SUM_ROWS, dim),
            whole(rows + SUM_ROWS, dim),
            whole(rows, dim),
            whole(rows, width),
            whole(rows, dim),
            whole(samples, heads, 2, dim),
            pl.BlockSpec(memory_space=pltpu.SMEM),
            whole(heads, rank, dim),
            pl.BlockSpec((width, columns), lambda i: (0, i)),
        ],
        out_specs=[pl.BlockSpec((rows, columns), lambda i: (0, i)), whole(samples, heads, 2, dim)],
        out_shape=[
            jax.ShapeDtypeStruct((rows, model), bf16),
            jax.ShapeDtypeStruct((samples, heads, 2, dim), f32),
        ],
        scratch_shapes=[
            pltpu.VMEM((rows, width), bf16),
            pltpu.VMEM((samples, dim, width), bf16),
            pltpu.VMEM((samples, dim, width), bf16),
        ],
        compiler_params=params(24),
        name="finish",
    )(returned, back, own, near, stats, center_rows, refresh, value_rows, w_out)
    return (mixed.reshape(samples, tokens, model), new_centers.transpose(0, 2, 1, 3))


def solution(mesh):
    return jax.shard_map(
        per_device,
        mesh=mesh,
        in_specs=(
            P("groups", "seq", None),
            P(),
            P(),
            P(),
            P(),
            P(),
            P(),
            P("groups", None, None, None),
            P(),
            P(),
        ),
        out_specs=(P("groups", "seq", None), P("groups", None, None, None)),
        check_vma=False,
    )
```

time: 121 us -> 45.7 us (0.38)
  blocking collectives: 36.7 us -> 0 us
  matrix products: 35.6 us -> 0 us
  Pallas kernels: 0 us -> 16.8 us
  local copies, waits for them, and re-layouts: 22.8 us -> 8.74 us
  between operations: 14.3 us -> 0.72 us
  other arithmetic: 10.5 us -> 0 us
  waiting for transfers between devices: 0.04 us -> 9.56 us
  starting transfers between devices: 0.04 us -> 9.46 us
    psum x1 -> x0, blocking collectives: 36.7 us -> none  [per_device(): summed = lax.psum(local_sums, 'seq')]
    dot_general x22 -> x0, matrix products: 35.6 us -> none  [the longest x4 11.5 us: absorb(): jnp.einsum('bhqs,bhsd->bhqd', weights, value_rebuilt, precision=highest)]
    pallas_call x0 -> x5, Pallas kernels: none -> 16.8 us  [the longest x1 4.74 us: per_device(): pl.pallas_call(functools.partial(project_kernel, **sizes, rank=rank, log_...]
    ppermute x0 -> x9, waiting for transfers between devices: none -> 9.56 us  [swap(): return lax.ppermute(x, 'seq', [(i, i ^ mask) for i in range(seq)])]
    ppermute x0 -> x9, starting transfers between devices: none -> 9.46 us  [swap(): return lax.ppermute(x, 'seq', [(i, i ^ mask) for i in range(seq)])]
    reduce_sum x8 -> x0, other arithmetic: 6.22 us -> none  [the longest x1 2.55 us: per_device(): jnp.sum(keys_local, axis=1)]
    unnamed x27 -> x22, local copies, waits for them, and re-layouts: 2.56 us -> 8.04 us
    squeeze x4 -> x0, local copies, waits for them, and re-layouts: 4.1 us -> none  [per_device(): result, unused = lax.scan(advance, start_state, stacked)]
  transfers between devices with their start and end apart: 1 -> 9, of which waited for: 0 -> 5; matrix products, arithmetic and copies ran while one was open for 8% -> 0% of each run, Pallas kernels for 0% -> 10%
where the time goes in v1:
time: 45.7 us; the launch traced here: 45.3 us
  Pallas kernels  16.8 us (37%)
  waiting for transfers between devices  9.56 us (21%)
  starting transfers between devices  9.46 us (21%)
  local copies, waits for them, and re-layouts  8.74 us (19%)
  between operations  0.72 us (2%)
    ppermute x9, waiting for transfers between devices, swap(): return lax.ppermute(x, 'seq', [(i, i ^ mask) for i in range(seq)])  9.56 us
    ppermute x9, starting transfers between devices, swap(): return lax.ppermute(x, 'seq', [(i, i ^ mask) for i in range(seq)])  9.46 us
    unnamed x22, local copies, waits for them, and re-layouts  8.04 us
    pallas_call x1, Pallas kernels, per_device(): pl.pallas_call(functools.partial(project_kernel, **sizes, rank=rank, log_...  4.74 us
    pallas_call x1, Pallas kernels, per_device(): pl.pallas_call(functools.partial(finish_kernel, **sizes, rank=rank, lengt...  4.51 us
    pallas_call x1, Pallas kernels, per_device(): pl.pallas_call(functools.partial(partner_kernel, **sizes, rank=rank, orde...  2.84 us
    pallas_call x1, Pallas kernels, per_device(): pl.pallas_call(functools.partial(own_kernel, **sizes, rank=rank), in_spec...  2.51 us
    pallas_call x1, Pallas kernels, per_device(): pl.pallas_call(functools.partial(near_kernel, **sizes), in_specs=[VMEM, V...  2.2 us
  transfers between devices with their start and end apart: 9, of which 5 were waited for; matrix products, arithmetic and copies ran while one was open for 0% of the time, Pallas kernels for 10%

profile of v1, /device:TPU:0, one launch (start us, length us, event | category | flops | bytes accessed | tf_op | source)
XLA Modules:
  0.0 45.3 jit_solution(3583607238956205637)
XLA Ops:
  0.6 0.7 %reshape.20.b_ref = f32[1,1152]{1,0:T(1,128)S(1)} reshape(f32[1152]{0:T(1024)} %param.12) | data formatting | bytes 9216 | tf_op jit(solution)/shard_map/reshape | solution.py:342
  1.3 0.0 copy-start
  1.3 3.0 %copy-done = bf16[3072,1152]{1,0:T(8,128)(2,1)S(1)} copy-done((bf16[3072,1152]{1,0:T(8,128)(2,1)S(1)}, bf16[3072,1152]{1,0:T(8,128)(2,1)}, u32[]{:S(2)}) %copy-start) | copy-done | bytes 7077912
  4.3 0.0 copy-start.2
  4.3 1.4 %copy-done.2 = bf16[2,128,3072]{2,1,0:T(8,128)(2,1)S(1)} copy-done((bf16[2,128,3072]{2,1,0:T(8,128)(2,1)S(1)}, bf16[2,128,3072]{2,1,0:T(8,128)(2,1)}, u32[]{:S(2)}) %copy-start.2) | copy-done | bytes 1572888
  5.7 0.0 copy-start.3
  5.8 0.8 %copy-done.3 = f32[3,128,32]{1,2,0:T(8,128)S(1)} copy-done((f32[3,128,32]{1,2,0:T(8,128)S(1)}, f32[3,128,32]{1,2,0:T(8,128)}, u32[]{:S(2)}) %copy-start.3) | copy-done | bytes 49176
  6.5 0.0 copy-start.5
  6.5 0.7 %copy-done.5 = f32[2,2,3,128]{3,1,2,0:T(2,128)S(1)} copy-done((f32[2,2,3,128]{3,1,2,0:T(2,128)S(1)}, f32[2,2,3,128]{3,1,2,0:T(2,128)}, u32[]{:S(2)}) %copy-start.5) | copy-done | bytes 6168
  7.2 0.0 copy-start.7
  7.2 0.8 %copy-done.7 = f32[3,128,32]{1,2,0:T(8,128)S(1)} copy-done((f32[3,128,32]{1,2,0:T(8,128)S(1)}, f32[3,128,32]{1,2,0:T(8,128)}, u32[]{:S(2)}) %copy-start.7) | copy-done | bytes 49176
  8.0 0.0 copy-start.9
  8.0 0.7 %copy-done.9 = f32[128]{0:T(128)S(1)} copy-done((f32[128]{0:T(128)S(1)}, f32[128]{0:T(128)}, u32[]{:S(2)}) %copy-start.9) | copy-done | bytes 536
  8.7 0.0 copy-start.10
  8.7 0.7 %copy-done.10 = f32[128]{0:T(128)S(1)} copy-done((f32[128]{0:T(128)S(1)}, f32[128]{0:T(128)}, u32[]{:S(2)}) %copy-start.10) | copy-done | bytes 536
  9.3 4.7 %project.1 = (bf16[1,144,384]{2,1,0:T(8,128)(2,1)S(1)}, bf16[256,256]{1,0:T(8,128)(2,1)S(1)}, f32[256,1152]{1,0:T(8,128)S(1)}) custom-call(bf16[256,3072]{1,0:T(8,128)(2,1)S(1)} %bitcast.8, bf16[3072,1152]{1,0:T(8,128)(2,1)S(1)} %copy-done, f32[1,1152]{1,0:T(1,128)S(1)} %reshape.20.b_ref, f32[1,128]{1,0:T(1,128)S(1)} %bitcast.15, f32[1,128]{1,0:T(1,128)S(1)} %bitcast.16, ...), custom_call_target="tpu_custom_call" | custom-call | tf_op jit(solution)/shard_map/project/pallas_call | solution.py:312
  14.1 0.0 copy-start.6
  14.1 4.0 %collective-permute-start.3 = (bf16[1,144,384]{2,1,0:T(8,128)(2,1)S(1)}, bf16[1,144,384]{2,1,0:T(8,128)(2,1)S(1)}, u32[]{:S(2)}, u32[]{:S(2)}) collective-permute-start(bf16[1,144,384]{2,1,0:T(8,128)(2,1)S(1)} %get-tuple-element.10.refs_0_), channel_id=1, source_target_pairs={{0,6},{1,7},{2,4},{3,5},{4,2},{5,3},{6,0},{7,1},{8,14},{9,15},{10,... | collective-permute-start | bytes 331784 | tf_op jit(solution)/shard_map/ppermute | solution.py:347
  18.2 0.4 collective-permute-start.2
  18.6 0.2 collective-permute-start.1
  18.8 2.9 %collective-permute-start = (bf16[256,256]{1,0:T(8,128)(2,1)S(1)}, bf16[256,256]{1,0:T(8,128)(2,1)S(1)}, u32[]{:S(2)}, u32[]{:S(2)}) collective-permute-start(bf16[256,256]{1,0:T(8,128)(2,1)S(1)} %get-tuple-element.9.query_ref), channel_id=1, source_target_pairs={{0,8},{1,9},{2,10},{3,11},{4,12},{5,13},{6,14},{7,15},{8,0},{9,1},... | collective-permute-start | bytes 393224 | tf_op jit(solution)/shard_map/ppermute | solution.py:347
  21.7 0.0 collective-permute-start.4
  21.7 0.3 collective-permute-done.3.refs_3_.refs_2_
  22.0 0.2 collective-permute-start.7
  22.2 4.3 %collective-permute-done.2.refs_2_.refs_1_ = bf16[1,144,384]{2,1,0:T(8,128)(2,1)S(1)} collective-permute-done((bf16[1,144,384]{2,1,0:T(8,128)(2,1)S(1)}, bf16[1,144,384]{2,1,0:T(8,128)(2,1)S(1)}, u32[]{:S(2)}, u32[]{:S(2)}) %collective-permute-start.2) | collective-permute-done | bytes 110624 | tf_op jit(solution)/shard_map/ppermute | solution.py:347
  26.6 0.0 collective-permute-start.6
  26.6 0.0 collective-permute-done.1.refs_1_.refs_0_
  26.6 0.5 %collective-permute-start.5 = (bf16[1,144,384]{2,1,0:T(8,128)(2,1)S(1)}, bf16[1,144,384]{2,1,0:T(8,128)(2,1)S(1)}, u32[]{:S(2)}, u32[]{:S(2)}) collective-permute-start(bf16[1,144,384]{2,1,0:T(8,128)(2,1)S(1)} %collective-permute-done.1.refs_1_.refs_0_), channel_id=1, source_target_pairs={{0,1},{1,0},{2,3},{3,2},{4,5},{5,4},{6,7},{7,6},{8,9},{9,8},{10,11... | collective-permute-start | bytes 331784 | tf_op jit(solution)/shard_map/ppermute | solution.py:347
  27.1 0.0 collective-permute-done.4.refs_4_.refs_3_
  27.1 0.0 collective-permute-done.query_ref
  27.1 0.0 collective-permute-done.7.refs_7_.refs_6_
  27.1 0.8 %collective-permute-done.6.refs_6_.refs_5_ = bf16[1,144,384]{2,1,0:T(8,128)(2,1)S(1)} collective-permute-done((bf16[1,144,384]{2,1,0:T(8,128)(2,1)S(1)}, bf16[1,144,384]{2,1,0:T(8,128)(2,1)S(1)}, u32[]{:S(2)}, u32[]{:S(2)}) %collective-permute-start.6) | collective-permute-done | bytes 110624 | tf_op jit(solution)/shard_map/ppermute | solution.py:347
  27.9 0.2 collective-permute-done.5.refs_5_.refs_4_
  28.0 2.8 %partner.1.half_ref = f32[272,128]{1,0:T(8,128)S(1)} custom-call(bf16[256,256]{1,0:T(8,128)(2,1)S(1)} %collective-permute-done.query_ref, bf16[1,144,384]{2,1,0:T(8,128)(2,1)S(1)} %get-tuple-element.10.refs_0_, bf16[1,144,384]{2,1,0:T(8,128)(2,1)S(1)} %collective-permute-done.1.refs_1_.refs_0_, ...), custom_call_target="tpu_custom_call" | custom-call | flops 805306368 | bytes 786432 | tf_op jit(solution)/shard_map/partner/pallas_call | solution.py:385
  30.9 1.2 %collective-permute-start.8 = (f32[272,128]{1,0:T(8,128)S(1)}, f32[272,128]{1,0:T(8,128)S(1)}, u32[]{:S(2)}, u32[]{:S(2)}) collective-permute-start(f32[272,128]{1,0:T(8,128)S(1)} %partner.1.half_ref), channel_id=1, source_target_pairs={{0,8},{1,9},{2,10},{3,11},{4,12},{5,13},{6,14},{7,15},{8,0},{9,1},... | collective-permute-start | bytes 417800 | tf_op jit(solution)/shard_map/ppermute | solution.py:347
  32.1 0.0 copy-done.6
  32.1 2.2 %near.1 = (f32[256,384]{1,0:T(8,128)S(1)}, f32[256,128]{1,0:T(8,128)S(1)}) custom-call(f32[256,1152]{1,0:T(8,128)S(1)} %get-tuple-element.11.qkv_ref, f32[2,3,2,128]{3,2,1,0:T(2,128)S(1)} %bitcast.12), custom_call_target="tpu_custom_call" | custom-call | flops 150994944 | bytes 1966080 | tf_op jit(solution)/shard_map/near/pallas_call | solution.py:362
  34.3 0.0 copy-start.1
  34.3 0.0 copy-start.4
  34.3 0.0 copy-start.8
  34.3 2.5 %own.1.own_ref = f32[256,128]{1,0:T(8,128)S(1)} custom-call(bf16[256,256]{1,0:T(8,128)(2,1)S(1)} %get-tuple-element.9.query_ref, bf16[1,144,384]{2,1,0:T(8,128)(2,1)S(1)} %collective-permute-done.1.refs_1_.refs_0_, bf16[1,144,384]{2,1,0:T(8,128)(2,1)S(1)} %collective-permute-done.2.refs_2_.refs_1_, ...), custom_call_target="tpu_custom_call" | custom-call | flops 805306368 | bytes 786432 | tf_op jit(solution)/shard_map/own/pallas_call | solution.py:395
  36.8 3.9 %collective-permute-done.8.back_ref = f32[272,128]{1,0:T(8,128)S(1)} collective-permute-done((f32[272,128]{1,0:T(8,128)S(1)}, f32[272,128]{1,0:T(8,128)S(1)}, u32[]{:S(2)}, u32[]{:S(2)}) %collective-permute-start.8) | collective-permute-done | bytes 139296 | tf_op jit(solution)/shard_map/ppermute | solution.py:347
  40.8 0.0 copy-done.1
  40.8 0.0 copy-done.4
  40.8 0.0 copy-done.8
  40.8 4.5 %finish.1 = (bf16[256,3072]{1,0:T(8,128)(2,1)}, f32[2,3,2,128]{3,2,1,0:T(2,128)}) custom-call(f32[272,128]{1,0:T(8,128)S(1)} %collective-permute-done.8.back_ref, f32[272,128]{1,0:T(8,128)S(1)} %partner.1.half_ref, f32[256,128]{1,0:T(8,128)S(1)} %own.1.own_ref, f32[256,384]{1,0:T(8,128)S(1)} %get-tuple-element.12.near_ref, ...), custom_call_target="tpu_custom_call" | custom-call | tf_op jit(solution)/shard_map/finish/pallas_call | solution.py:406
Async XLA Ops:
  1.3 3.0 %copy-start = (bf16[3072,1152]{1,0:T(8,128)(2,1)S(1)}, bf16[3072,1152]{1,0:T(8,128)(2,1)}, u32[]{:S(2)}) copy-start(bf16[3072,1152]{1,0:T(8,128)(2,1)} %w_ref.2) | copy-start | bytes 21233668
  4.3 1.4 %copy-start.2 = (bf16[2,128,3072]{2,1,0:T(8,128)(2,1)S(1)}, bf16[2,128,3072]{2,1,0:T(8,128)(2,1)}, u32[]{:S(2)}) copy-start(bf16[2,128,3072]{2,1,0:T(8,128)(2,1)} %param.10) | copy-start | bytes 4718596
  5.7 0.8 %copy-start.3 = (f32[3,128,32]{1,2,0:T(8,128)S(1)}, f32[3,128,32]{1,2,0:T(8,128)}, u32[]{:S(2)}) copy-start(f32[3,128,32]{1,2,0:T(8,128)} %param.16) | copy-start | bytes 147460
  6.5 0.7 %copy-start.5 = (f32[2,2,3,128]{3,1,2,0:T(2,128)S(1)}, f32[2,2,3,128]{3,1,2,0:T(2,128)}, u32[]{:S(2)}) copy-start(f32[2,2,3,128]{3,1,2,0:T(2,128)} %param.17) | copy-start | bytes 18436
  7.2 0.8 %copy-start.7 = (f32[3,128,32]{1,2,0:T(8,128)S(1)}, f32[3,128,32]{1,2,0:T(8,128)}, u32[]{:S(2)}) copy-start(f32[3,128,32]{1,2,0:T(8,128)} %param.15) | copy-start | bytes 147460
  8.0 0.7 %copy-start.9 = (f32[128]{0:T(128)S(1)}, f32[128]{0:T(128)}, u32[]{:S(2)}) copy-start(f32[128]{0:T(128)} %param.13) | copy-start | bytes 1540
  8.7 0.7 %copy-start.10 = (f32[128]{0:T(128)S(1)}, f32[128]{0:T(128)}, u32[]{:S(2)}) copy-start(f32[128]{0:T(128)} %param.14) | copy-start | bytes 1540
  14.1 18.0 %copy-start.6 = (f32[2,2,3,128]{3,1,2,0:T(2,128)S(1)}, f32[2,2,3,128]{3,1,2,0:T(2,128)}, u32[]{:S(2)}) copy-start(f32[2,2,3,128]{3,1,2,0:T(2,128)} %param.17) | copy-start | bytes 18436
  14.1 7.9 %collective-permute-start.3 = (bf16[1,144,384]{2,1,0:T(8,128)(2,1)S(1)}, bf16[1,144,384]{2,1,0:T(8,128)(2,1)S(1)}, u32[]{:S(2)}, u32[]{:S(2)}) collective-permute-start(bf16[1,144,384]{2,1,0:T(8,128)(2,1)S(1)} %get-tuple-element.10.refs_0_), channel_id=1, source_target_pairs={{0,6},{1,7},{2,4},{3,5},{4,2},{5,3},{6,0},{7,1},{8,14},{9,15},{10,... | collective-permute-start | bytes 331784 | tf_op jit(solution)/shard_map/ppermute | solution.py:347
  18.2 8.4 %collective-permute-start.2 = (bf16[1,144,384]{2,1,0:T(8,128)(2,1)S(1)}, bf16[1,144,384]{2,1,0:T(8,128)(2,1)S(1)}, u32[]{:S(2)}, u32[]{:S(2)}) collective-permute-start(bf16[1,144,384]{2,1,0:T(8,128)(2,1)S(1)} %get-tuple-element.10.refs_0_), channel_id=1, source_target_pairs={{0,4},{1,5},{2,6},{3,7},{4,0},{5,1},{6,2},{7,3},{8,12},{9,13},{10,... | collective-permute-start | bytes 331784 | tf_op jit(solution)/shard_map/ppermute | solution.py:347
  18.6 8.0 %collective-permute-start.1 = (bf16[1,144,384]{2,1,0:T(8,128)(2,1)S(1)}, bf16[1,144,384]{2,1,0:T(8,128)(2,1)S(1)}, u32[]{:S(2)}, u32[]{:S(2)}) collective-permute-start(bf16[1,144,384]{2,1,0:T(8,128)(2,1)S(1)} %get-tuple-element.10.refs_0_), channel_id=1, source_target_pairs={{0,2},{1,3},{2,0},{3,1},{4,6},{5,7},{6,4},{7,5},{8,10},{9,11},{10,... | collective-permute-start | bytes 331784 | tf_op jit(solution)/shard_map/ppermute | solution.py:347
  18.8 8.3 %collective-permute-start = (bf16[256,256]{1,0:T(8,128)(2,1)S(1)}, bf16[256,256]{1,0:T(8,128)(2,1)S(1)}, u32[]{:S(2)}, u32[]{:S(2)}) collective-permute-start(bf16[256,256]{1,0:T(8,128)(2,1)S(1)} %get-tuple-element.9.query_ref), channel_id=1, source_target_pairs={{0,8},{1,9},{2,10},{3,11},{4,12},{5,13},{6,14},{7,15},{8,0},{9,1},... | collective-permute-start | bytes 393224 | tf_op jit(solution)/shard_map/ppermute | solution.py:347
  21.7 5.4 %collective-permute-start.4 = (bf16[1,144,384]{2,1,0:T(8,128)(2,1)S(1)}, bf16[1,144,384]{2,1,0:T(8,128)(2,1)S(1)}, u32[]{:S(2)}, u32[]{:S(2)}) collective-permute-start(bf16[1,144,384]{2,1,0:T(8,128)(2,1)S(1)} %get-tuple-element.10.refs_0_), channel_id=1, source_target_pairs={{0,1},{1,0},{2,3},{3,2},{4,5},{5,4},{6,7},{7,6},{8,9},{9,8},{10,11... | collective-permute-start | bytes 331784 | tf_op jit(solution)/shard_map/ppermute | solution.py:347
  22.0 5.0 %collective-permute-start.7 = (bf16[1,144,384]{2,1,0:T(8,128)(2,1)S(1)}, bf16[1,144,384]{2,1,0:T(8,128)(2,1)S(1)}, u32[]{:S(2)}, u32[]{:S(2)}) collective-permute-start(bf16[1,144,384]{2,1,0:T(8,128)(2,1)S(1)} %collective-permute-done.3.refs_3_.refs_2_), channel_id=1, source_target_pairs={{0,1},{1,0},{2,3},{3,2},{4,5},{5,4},{6,7},{7,6},{8,9},{9,8},{10,11... | collective-permute-start | bytes 331784 | tf_op jit(solution)/shard_map/ppermute | solution.py:347
  26.6 1.3 %collective-permute-start.6 = (bf16[1,144,384]{2,1,0:T(8,128)(2,1)S(1)}, bf16[1,144,384]{2,1,0:T(8,128)(2,1)S(1)}, u32[]{:S(2)}, u32[]{:S(2)}) collective-permute-start(bf16[1,144,384]{2,1,0:T(8,128)(2,1)S(1)} %collective-permute-done.2.refs_2_.refs_1_), channel_id=1, source_target_pairs={{0,1},{1,0},{2,3},{3,2},{4,5},{5,4},{6,7},{7,6},{8,9},{9,8},{10,11... | collective-permute-start | bytes 331784 | tf_op jit(solution)/shard_map/ppermute | solution.py:347
  26.6 1.5 %collective-permute-start.5 = (bf16[1,144,384]{2,1,0:T(8,128)(2,1)S(1)}, bf16[1,144,384]{2,1,0:T(8,128)(2,1)S(1)}, u32[]{:S(2)}, u32[]{:S(2)}) collective-permute-start(bf16[1,144,384]{2,1,0:T(8,128)(2,1)S(1)} %collective-permute-done.1.refs_1_.refs_0_), channel_id=1, source_target_pairs={{0,1},{1,0},{2,3},{3,2},{4,5},{5,4},{6,7},{7,6},{8,9},{9,8},{10,11... | collective-permute-start | bytes 331784 | tf_op jit(solution)/shard_map/ppermute | solution.py:347
  30.9 9.9 %collective-permute-start.8 = (f32[272,128]{1,0:T(8,128)S(1)}, f32[272,128]{1,0:T(8,128)S(1)}, u32[]{:S(2)}, u32[]{:S(2)}) collective-permute-start(f32[272,128]{1,0:T(8,128)S(1)} %partner.1.half_ref), channel_id=1, source_target_pairs={{0,8},{1,9},{2,10},{3,11},{4,12},{5,13},{6,14},{7,15},{8,0},{9,1},... | collective-permute-start | bytes 417800 | tf_op jit(solution)/shard_map/ppermute | solution.py:347
  34.3 6.5 %copy-start.1 = (bf16[384,3072]{1,0:T(8,128)(2,1)S(1)}, bf16[384,3072]{1,0:T(8,128)(2,1)}, u32[]{:S(2)}) copy-start(bf16[384,3072]{1,0:T(8,128)(2,1)} %w_ref.3) | copy-start | bytes 7077892
  34.3 6.5 %copy-start.4 = (f32[3,128,32]{1,2,0:T(8,128)S(1)}, f32[3,128,32]{1,2,0:T(8,128)}, u32[]{:S(2)}) copy-start(f32[3,128,32]{1,2,0:T(8,128)} %param.16) | copy-start | bytes 147460
  34.3 6.5 %copy-start.8 = (s32[2,3]{1,0:T(2,128)S(1)}, s32[2,3]{1,0:T(2,128)}, u32[]{:S(2)}) copy-start(s32[2,3]{1,0:T(2,128)} %refresh_ref.1) | copy-start | bytes 76

commit v2 on v0

v2 whole, which is shorter than its diff:
```python
import functools
import math

import jax
import jax.numpy as jnp
from jax import lax
from jax.experimental import pallas as pl
from jax.experimental.pallas import tpu as pltpu
from jax.sharding import PartitionSpec as P

epsilon = 1e-06
log2_e = math.log2(math.e)
f32 = jnp.float32
bf16 = jnp.bfloat16
SUM_ROWS = 16
NT = (((1,), (1,)), ((), ()))
NN = (((1,), (0,)), ((), ()))


def dot(a, b, dims=NN):
    return lax.dot_general(a, b, dims, preferred_element_type=f32)


def split(x):
    high = x.astype(bf16)
    low = (x - high.astype(f32)).astype(bf16)
    return high, low


def dot3(a, b, dims=NN):
    return dot(a[0], b[0], dims) + (dot(a[0], b[1], dims) + dot(a[1], b[0], dims))


def pieces_of(x, count):
    out = []
    for _ in range(count):
        top = x.astype(bf16)
        out.append(top)
        x = x - top.astype(f32)
    return out


def lane_ids(rows, lanes):
    return lax.broadcasted_iota(jnp.int32, (rows, lanes), 1)


def key_lane(sample, head, rank):
    return head * rank if sample == 0 else (head + 1) * rank


def value_lane(sample, head, rank, heads):
    if head == 0:
        return heads * rank if sample == 0 else 0
    return ((heads - 1) * sample + head - 1) * rank


def free_lane(sample, rank):
    return 2 * rank if sample == 0 else rank


def within(lanes, start, count):
    return (lanes >= start) & (lanes < start + count)


def fill_basis(basis_h, basis_l, vb_ref, samples, heads, dim, rank):
    basis_h[...] = jnp.zeros_like(basis_h)
    basis_l[...] = jnp.zeros_like(basis_l)
    for h in range(heads):
        vh, vl = split(vb_ref[h])
        for b in range(samples):
            at = value_lane(b, h, rank, heads)
            basis_h[b, at : at + rank, h * dim : (h + 1) * dim] = vh
            basis_l[b, at : at + rank, h * dim : (h + 1) * dim] = vl


def project_kernel(
    images_hbm, w_hbm, b_hbm, qg_hbm, kg_hbm, kb_hbm, vb_hbm, centers_hbm,
    payload_ref, query_ref, qkv_ref,
    x_ref, w_ref, b_ref, qg_ref, kg_ref, kb_ref, vb_ref, centers_ref,
    acc_ref, tiles_h, tiles_l, last_h, last_l, sums_ref, big_sem, small_sem,
    *, samples, tokens, heads, dim, rank, log_factor,
):
    chunks, _, depth = x_ref.shape
    width = heads * dim

    def x_copy(c):
        columns = pl.ds(pl.multiple_of(c * depth, depth), depth)
        return pltpu.make_async_copy(images_hbm.at[:, columns], x_ref.at[c], big_sem.at[0, c])

    def w_copy(c):
        some = pl.ds(pl.multiple_of(c * depth, depth), depth)
        return pltpu.make_async_copy(w_hbm.at[some, :], w_ref.at[c], big_sem.at[1, c])

    small = [
        pltpu.make_async_copy(source, target, small_sem.at[i])
        for i, (source, target) in enumerate(
            [
                (kb_hbm, kb_ref), (vb_hbm, vb_ref), (b_hbm, b_ref),
                (qg_hbm, qg_ref), (kg_hbm, kg_ref), (centers_hbm, centers_ref),
            ]
        )
    ]
    for c in range(chunks):
        x_copy(c).start()
        w_copy(c).start()
        if c == 0:
            for copy in small:
                copy.start()
    tiles_h[...] = jnp.zeros_like(tiles_h)
    tiles_l[...] = jnp.zeros_like(tiles_l)
    last_h[...] = jnp.zeros_like(last_h)
    last_l[...] = jnp.zeros_like(last_l)
    sums_ref[...] = jnp.zeros_like(sums_ref)
    for copy in small:
        copy.wait()
    for h in range(heads):
        kh, kl = split(kb_ref[h])
        vh, vl = split(vb_ref[h])
        for b in range(samples):
            at = key_lane(b, h, rank)
            tiles_h[b, at : at + rank, h * dim : (h + 1) * dim] = kh
            tiles_l[b, at : at + rank, h * dim : (h + 1) * dim] = kl
            at = value_lane(b, h, rank, heads)
            if h == 0:
                tiles_h[b, at : at + rank, width : width + dim] = vh
                tiles_l[b, at : at + rank, width : width + dim] = vl
            else:
                last_h[at : at + rank, (h - 1) * dim : h * dim] = vh
                last_l[at : at + rank, (h - 1) * dim : h * dim] = vl
    for c in range(chunks):
        x_copy(c).wait()
        w_copy(c).wait()
        part = dot(x_ref[c], w_ref[c])
        if c == 0:
            acc_ref[...] = part
        else:
            acc_ref[...] += part

    def column(at):
        return acc_ref[:, at * dim : (at + 1) * dim] + b_ref[at : at + 1, :]

    def normed(at, gain):
        x = column(at)
        mean_square = jnp.mean(x * x, axis=-1, keepdims=True)
        return x * lax.rsqrt(mean_square + epsilon) * gain

    queries, keys, values = [], [], []
    for h in range(heads):
        q = normed(h, qg_ref[...])
        k = normed(heads + h, kg_ref[...])
        v = column(2 * heads + h)
        queries.append(q)
        keys.append(k)
        values.append(v)
        for b in range(samples):
            rows = slice(b * tokens, (b + 1) * tokens)
            row = (b * heads + h) * 2
            sums_ref[row : row + 1, :] = jnp.sum(k[rows], axis=0, keepdims=True)
            sums_ref[row + 1 : row + 2, :] = jnp.sum(v[rows], axis=0, keepdims=True)
    for p, piece in enumerate(pieces_of(sums_ref[...], 3)):
        payload_ref[0, tokens : tokens + SUM_ROWS, p * dim : (p + 1) * dim] = piece
    lasts, highs, lows = [], [], []
    for b in range(samples):
        rows = slice(b * tokens, (b + 1) * tokens)
        shifted = [keys[h][rows] - centers_ref[b, h, 0:1, :] for h in range(heads)]
        shifted += [values[h][rows] - centers_ref[b, h, 1:2, :] for h in range(heads)]
        main = split(jnp.concatenate(shifted[: heads + 1], axis=1))
        code = dot3(main, (tiles_h[b], tiles_l[b]), NT)
        payload_ref[0, :tokens, b * dim : (b + 1) * dim] = code.astype(bf16)
        tail = split(jnp.concatenate(shifted[heads + 1 :], axis=1))
        lasts.append(dot3(tail, (last_h[...], last_l[...]), NT))
        query = split(jnp.concatenate([q[rows] for q in queries], axis=1))
        query_code = dot3(query, (tiles_h[b, :, :width], tiles_l[b, :, :width]), NT) * log_factor
        high = query_code.astype(bf16).astype(f32)
        highs.append(high)
        lows.append(query_code - high)
    lanes = lane_ids(tokens, dim)
    last = jnp.where(lanes < (heads - 1) * rank, lasts[0], lasts[1])
    payload_ref[0, :tokens, samples * dim :] = last.astype(bf16)
    turned = pltpu.roll(lows[1], dim // 2, 1)
    query_ref[:, :dim] = jnp.where(lanes < heads * rank, highs[0], turned).astype(bf16)
    query_ref[:, dim : 2 * dim] = jnp.where(lanes < rank, turned, highs[1]).astype(bf16)
    query_ref[:, 2 * dim :] = jnp.where(lanes < heads * rank, lows[0], lows[1]).astype(bf16)
    for h in range(heads):
        qkv_ref[:, h * dim : (h + 1) * dim] = queries[h] * log_factor
        qkv_ref[:, width + h * dim : width + (h + 1) * dim] = keys[h]
        qkv_ref[:, 2 * width + h * dim : 2 * width + (h + 1) * dim] = values[h]


def near_kernel(qkv_ref, centers_ref, near_ref, stat_ref, *, samples, tokens, heads, dim):
    width = heads * dim
    lanes = lane_ids(tokens, dim)
    for b in range(samples):
        rows = slice(b * tokens, (b + 1) * tokens)
        stats = jnp.zeros((tokens, dim), f32)
        for h in range(heads):
            q = qkv_ref[rows, h * dim : (h + 1) * dim]
            k = split(qkv_ref[rows, width + h * dim : width + (h + 1) * dim])
            v = split(qkv_ref[rows, 2 * width + h * dim : 2 * width + (h + 1) * dim])
            scores = dot3(split(q), k, NT)
            row_max = jnp.max(scores, axis=-1, keepdims=True)
            weights = jnp.exp2(scores - row_max)
            row_sum = jnp.sum(weights, axis=-1, keepdims=True)
            near_ref[rows, h * dim : (h + 1) * dim] = dot3(split(weights), v) / row_sum
            center = jnp.sum(q * centers_ref[b, h, 0:1, :], axis=-1, keepdims=True)
            stats = jnp.where(lanes == h, row_max + jnp.log(row_sum) * log2_e, stats)
            stats = jnp.where(lanes == heads + h, center, stats)
        stat_ref[rows, :] = stats


def query_parts(query_ref, sample, heads, dim, rank):
    lanes = lane_ids(query_ref.shape[0], dim)
    if sample == 0:
        return query_ref[:, :dim].astype(f32), query_ref[:, 2 * dim :].astype(f32)
    first, second = query_ref[:, :dim].astype(f32), query_ref[:, dim : 2 * dim].astype(f32)
    turned = pltpu.roll(jnp.where(lanes < rank, second, first), dim // 2, 1)
    return second, jnp.where(lanes < heads * rank, turned, query_ref[:, 2 * dim :].astype(f32))


def code_attention(query_ref, tiles, b, *, samples, tokens, heads, dim, rank):
    lanes = lane_ids(tokens, dim)
    high, low = query_parts(query_ref, b, heads, dim, rank)
    stacked = []
    for h in range(heads):
        own = within(lanes, key_lane(b, h, rank), rank)
        both = [jnp.where(own, part, 0.0).astype(bf16) for part in (high, low)]
        stacked.append(jnp.concatenate(both, axis=1))
    left = jnp.concatenate(stacked, axis=0)
    scores, values = [], []
    for ref, i in tiles:
        code = ref[i, :tokens, b * dim : (b + 1) * dim]
        scores.append(dot(left, jnp.concatenate([code, code], axis=1), NT))
        values.append(jnp.concatenate([code, ref[i, :tokens, samples * dim :]], axis=1))
    best = scores[0]
    for part in scores[1:]:
        best = jnp.maximum(best, part)
    row_max = jnp.max(best, axis=-1, keepdims=True)
    total = jnp.zeros_like(best)
    weights = []
    for part in scores:
        weight = jnp.exp2(part - row_max).astype(bf16)
        total = total + weight.astype(f32)
        weights.append(weight)
    result = dot(jnp.concatenate(weights, axis=1), jnp.concatenate(values, axis=0))
    row_sum = jnp.sum(total, axis=-1, keepdims=True)
    result = result / row_sum
    log_sum = row_max + jnp.log(row_sum) * log2_e
    out = jnp.zeros((tokens, dim), f32)
    logs = []
    for h in range(heads):
        head_rows = slice(h * tokens, (h + 1) * tokens)
        part = result[head_rows, :dim] if h == 0 else result[head_rows, dim:]
        out = jnp.where(within(lanes, value_lane(b, h, rank, heads), rank), part, out)
        logs.append(log_sum[head_rows])
    return out, logs


def tree_sum(parts):
    while len(parts) > 1:
        parts = [parts[i] + parts[i + 1] for i in range(0, len(parts), 2)]
    return parts[0]


def tiles_of(refs):
    return [(ref, i) for ref in refs for i in range(ref.shape[0])]


def partner_kernel(query_ref, *refs, order, samples, tokens, heads, dim, rank):
    out_ref = refs[-1]
    tiles = tiles_of(refs[:-2])
    parts = []
    for place in order:
        ref, i = tiles[place]
        rows = slice(tokens, tokens + SUM_ROWS)
        pieces = [ref[i, rows, p * dim : (p + 1) * dim].astype(f32) for p in range(3)]
        parts.append(pieces[0] + (pieces[1] + pieces[2]))
    first = samples * tokens
    for p, piece in enumerate(pieces_of(tree_sum(parts), 2)):
        out_ref[first + p * SUM_ROWS : first + (p + 1) * SUM_ROWS, :] = piece
    lanes = lane_ids(tokens, dim)
    for b in range(samples):
        out, logs = code_attention(
            query_ref, tiles, b, samples=samples, tokens=tokens, heads=heads, dim=dim, rank=rank
        )
        for h in range(heads):
            for p, piece in enumerate(pieces_of(logs[h], 3)):
                out = jnp.where(lanes == free_lane(b, rank) + 3 * h + p, piece.astype(f32), out)
        out_ref[b * tokens : (b + 1) * tokens, :] = out.astype(bf16)


def own_kernel(
    query_ref, near_ref, stat_ref, centers_ref, vb_ref, *refs, samples, tokens, heads, dim, rank
):
    merged_ref, log_ref, basis_h, basis_l = refs[-4:]
    fill_basis(basis_h, basis_l, vb_ref, samples, heads, dim, rank)
    tiles = tiles_of(refs[:-4])
    lanes = lane_ids(tokens, dim)
    for b in range(samples):
        rows = slice(b * tokens, (b + 1) * tokens)
        out, logs = code_attention(
            query_ref, tiles, b, samples=samples, tokens=tokens, heads=heads, dim=dim, rank=rank
        )
        far = dot3(split(out), (basis_h[b], basis_l[b]))
        stats = stat_ref[rows, :]
        kept = jnp.zeros((tokens, dim), f32)
        for h in range(heads):
            columns = slice(h * dim, (h + 1) * dim)
            near_log = stats[:, h : h + 1]
            center = stats[:, heads + h : heads + h + 1]
            far_log = logs[h] + center
            top = jnp.maximum(near_log, far_log)
            near_part, far_part = jnp.exp2(near_log - top), jnp.exp2(far_log - top)
            whole = near_part + far_part
            merged = near_ref[rows, columns] * (near_part / whole)
            merged = merged + (far[:, columns] + centers_ref[b, h, 1:2, :]) * (far_part / whole)
            merged_ref[rows, columns] = merged
            kept = jnp.where(lanes == h, top + jnp.log(whole) * log2_e, kept)
            kept = jnp.where(lanes == heads + h, center, kept)
        log_ref[rows, :] = kept


def finish_kernel(
    back_ref, half_ref, merged_ref, log_ref, centers_ref, refresh_ref, vb_ref, w_ref,
    mixed_hbm, new_ref, attended_ref, basis_h, basis_l, mixed_ref, sem,
    *, samples, tokens, heads, dim, rank, length,
):
    fill_basis(basis_h, basis_l, vb_ref, samples, heads, dim, rank)
    for b in range(samples):
        rows = slice(b * tokens, (b + 1) * tokens)
        codes = back_ref[rows, :]
        far = dot(codes, basis_h[b]) + dot(codes, basis_l[b])
        extra = codes.astype(f32)
        logs = log_ref[rows, :]
        for h in range(heads):
            columns = slice(h * dim, (h + 1) * dim)
            spot = free_lane(b, rank) + 3 * h
            far_log = extra[:, spot : spot + 1] + (
                extra[:, spot + 1 : spot + 2] + extra[:, spot + 2 : spot + 3]
            )
            far_log = far_log + logs[:, heads + h : heads + h + 1]
            own_log = logs[:, h : h + 1]
            top = jnp.maximum(own_log, far_log)
            own_part, far_part = jnp.exp2(own_log - top), jnp.exp2(far_log - top)
            whole = own_part + far_part
            value = merged_ref[rows, columns] * (own_part / whole)
            value = value + (far[:, columns] + centers_ref[b, h, 1:2, :]) * (far_part / whole)
            attended_ref[rows, columns] = value.astype(bf16)
    chunks, _, columns = mixed_ref.shape
    copies = []
    for c in range(chunks):
        place = slice(c * columns, (c + 1) * columns)
        mixed_ref[c] = dot(attended_ref[...], w_ref[:, place]).astype(bf16)
        copy = pltpu.make_async_copy(mixed_ref.at[c], mixed_hbm.at[:, place], sem.at[c])
        copy.start()
        copies.append(copy)
    first = samples * tokens
    sums = [
        ref[first : first + SUM_ROWS, :].astype(f32)
        + ref[first + SUM_ROWS : first + 2 * SUM_ROWS, :].astype(f32)
        for ref in (half_ref, back_ref)
    ]
    fresh = (sums[0] + sums[1]) * (1.0 / length)
    for b in range(samples):
        for h in range(heads):
            for j in range(2):
                row = (b * heads + h) * 2 + j
                old = centers_ref[b, h, j : j + 1, :]
                new_ref[b, h, j : j + 1, :] = jnp.where(
                    refresh_ref[j, h] == 1, fresh[row : row + 1, :], old
                )
    for copy in copies:
        copy.wait()


VMEM = pl.BlockSpec(memory_space=pltpu.VMEM)
HBM = pl.BlockSpec(memory_space=pltpu.HBM)


def per_device(
    images, w_qkv, b_qkv, q_gain, k_gain, key_basis, value_basis, centers, refresh, w_out
):
    samples, tokens, model = images.shape
    heads, dim, rank = key_basis.shape
    seq = lax.axis_size("seq")
    rows = samples * tokens
    width = heads * dim
    sizes = dict(samples=samples, tokens=tokens, heads=heads, dim=dim)
    log_factor = log2_e / math.sqrt(dim)
    flat = images.reshape(rows, model)
    key_rows = key_basis.transpose(0, 2, 1)
    value_rows = value_basis.transpose(0, 2, 1)
    center_rows = centers.transpose(0, 2, 1, 3)
    chunks = 6
    depth = model // chunks
    shard = (1, tokens + SUM_ROWS, width)
    params = lambda mib: pltpu.CompilerParams(vmem_limit_bytes=mib * 2**20)

    payload, query, qkv = pl.pallas_call(
        functools.partial(project_kernel, **sizes, rank=rank, log_factor=log_factor),
        in_specs=[HBM] * 8,
        out_specs=[VMEM] * 3,
        out_shape=[
            jax.ShapeDtypeStruct(shard, bf16),
            jax.ShapeDtypeStruct((tokens, width), bf16),
            jax.ShapeDtypeStruct((rows, 3 * width), f32),
        ],
        scratch_shapes=[
            pltpu.VMEM((chunks, rows, depth), bf16),
            pltpu.VMEM((chunks, depth, 3 * width), bf16),
            pltpu.VMEM((3 * heads, dim), f32),
            pltpu.VMEM((1, dim), f32),
            pltpu.VMEM((1, dim), f32),
            pltpu.VMEM((heads, rank, dim), f32),
            pltpu.VMEM((heads, rank, dim), f32),
            pltpu.VMEM((samples, heads, 2, dim), f32),
            pltpu.VMEM((rows, 3 * width), f32),
            pltpu.VMEM((samples, dim, width + dim), bf16),
            pltpu.VMEM((samples, dim, width + dim), bf16),
            pltpu.VMEM((dim, width - dim), bf16),
            pltpu.VMEM((dim, width - dim), bf16),
            pltpu.VMEM((SUM_ROWS, dim), f32),
            pltpu.SemaphoreType.DMA((2, chunks)),
            pltpu.SemaphoreType.DMA((6,)),
        ],
        compiler_params=params(32),
        name="project",
    )(
        *(
            pltpu.with_memory_space_constraint(x, pltpu.HBM)
            for x in (
                flat, w_qkv, b_qkv.reshape(3 * heads, dim), q_gain.reshape(1, -1),
                k_gain.reshape(1, -1), key_rows, value_rows, center_rows,
            )
        )
    )

    def swap(x, mask):
        return lax.ppermute(x, "seq", [(i, i ^ mask) for i in range(seq)])

    far_mask = seq // 2
    bits = [m for m in (2**i for i in range(1, seq.bit_length() - 1)) if m < far_mask]
    query_far = swap(query, far_mask)
    held = [(payload, [0])]
    direct = sum(bits[:2])
    for mask in range(2, 2 * direct, 2):
        if mask & ~direct == 0:
            held.append((swap(payload, mask), [mask]))
    for bit in bits[2:]:
        block = jnp.concatenate([a for a, _ in held], axis=0)
        names = [m for _, ms in held for m in ms]
        held.append((swap(block, bit), [m ^ bit for m in names]))

    near, stats = pl.pallas_call(
        functools.partial(near_kernel, **sizes),
        in_specs=[VMEM, VMEM],
        out_specs=[VMEM, VMEM],
        out_shape=[
            jax.ShapeDtypeStruct((rows, width), f32),
            jax.ShapeDtypeStruct((rows, dim), f32),
        ],
        compiler_params=params(24),
        cost_estimate=pl.CostEstimate(
            flops=12 * rows * tokens * width, bytes_accessed=5 * rows * width * 4, transcendentals=0
        ),
        name="near",
    )(qkv, center_rows)

    held += [(swap(a, 1), [m ^ 1 for m in ms]) for a, ms in held]
    arrays = [a for a, _ in held]
    names = [m for _, ms in held for m in ms]
    order = tuple(names.index(m) for m in range(len(names)))
    cost = pl.CostEstimate(
        flops=8 * rows * tokens * len(names) * width,
        bytes_accessed=len(names) * 2 * tokens * width,
        transcendentals=0,
    )
    back = pl.pallas_call(
        functools.partial(partner_kernel, **sizes, rank=rank, order=order),
        in_specs=[VMEM] * (1 + len(arrays)) + [pl.BlockSpec(memory_space=pl.ANY)],
        out_specs=VMEM,
        out_shape=jax.ShapeDtypeStruct((rows + 2 * SUM_ROWS, dim), bf16),
        compiler_params=params(32),
        cost_estimate=cost,
        name="partner",
    )(query_far, *arrays, stats)
    returned = swap(back, far_mask)
    merged, logs = pl.pallas_call(
        functools.partial(own_kernel, **sizes, rank=rank),
        in_specs=[VMEM] * (4 + len(arrays)),
        out_specs=[VMEM, VMEM],
        out_shape=[
            jax.ShapeDtypeStruct((rows, width), f32),
            jax.ShapeDtypeStruct((rows, dim), f32),
        ],
        scratch_shapes=[
            pltpu.VMEM((samples, dim, width), bf16),
            pltpu.VMEM((samples, dim, width), bf16),
        ],
        compiler_params=params(32),
        cost_estimate=cost,
        name="own",
    )(query, near, stats, center_rows, value_rows, *arrays[1:])

    columns = 512
    mixed, new_centers = pl.pallas_call(
        functools.partial(finish_kernel, **sizes, rank=rank, length=tokens * seq),
        in_specs=[VMEM] * 5 + [pl.BlockSpec(memory_space=pltpu.SMEM), VMEM, VMEM],
        out_specs=[HBM, VMEM],
        out_shape=[
            jax.ShapeDtypeStruct((rows, model), bf16),
            jax.ShapeDtypeStruct((samples, heads, 2, dim), f32),
        ],
        scratch_shapes=[
            pltpu.VMEM((rows, width), bf16),
            pltpu.VMEM((samples, dim, width), bf16),
            pltpu.VMEM((samples, dim, width), bf16),
            pltpu.VMEM((model // columns, rows, columns), bf16),
            pltpu.SemaphoreType.DMA((model // columns,)),
        ],
        compiler_params=params(24),
        name="finish",
    )(returned, back, merged, logs, center_rows, refresh, value_rows, w_out)
    return (mixed.reshape(samples, tokens, model), new_centers.transpose(0, 2, 1, 3))


def solution(mesh):
    return jax.shard_map(
        per_device,
        mesh=mesh,
        in_specs=(
            P("groups", "seq", None),
            P(),
            P(),
            P(),
            P(),
            P(),
            P(),
            P("groups", None, None, None),
            P(),
            P(),
        ),
        out_specs=(P("groups", "seq", None), P("groups", None, None, None)),
        check_vma=False,
    )
```

time: 121 us -> 38.9 us (0.32)
  blocking collectives: 36.7 us -> 0 us
  matrix products: 35.6 us -> 0 us
  local copies, waits for them, and re-layouts: 22.8 us -> 0.02 us
  Pallas kernels: 0 us -> 18.3 us
  between operations: 14.3 us -> 0.71 us
  waiting for transfers between devices: 0.04 us -> 11.2 us
  other arithmetic: 10.5 us -> 0 us
  starting transfers between devices: 0.04 us -> 8.49 us
    psum x1 -> x0, blocking collectives: 36.7 us -> none  [per_device(): summed = lax.psum(local_sums, 'seq')]
    dot_general x22 -> x0, matrix products: 35.6 us -> none  [the longest x4 11.5 us: absorb(): jnp.einsum('bhqs,bhsd->bhqd', weights, value_rebuilt, precision=highest)]
    pallas_call x0 -> x5, Pallas kernels: none -> 18.3 us  [the longest x1 7.15 us: per_device(): pl.pallas_call(functools.partial(project_kernel, **sizes, rank=rank, log_...]
    ppermute x0 -> x9, waiting for transfers between devices: none -> 11.2 us  [swap(): return lax.ppermute(x, 'seq', [(i, i ^ mask) for i in range(seq)])]
    ppermute x0 -> x9, starting transfers between devices: none -> 8.49 us  [swap(): return lax.ppermute(x, 'seq', [(i, i ^ mask) for i in range(seq)])]
    reduce_sum x8 -> x0, other arithmetic: 6.22 us -> none  [the longest x1 2.55 us: per_device(): jnp.sum(keys_local, axis=1)]
    squeeze x4 -> x0, local copies, waits for them, and re-layouts: 4.1 us -> none  [per_device(): result, unused = lax.scan(advance, start_state, stacked)]
    another operation x1 -> x0, local copies, waits for them, and re-layouts: 3.85 us -> none  [per_device(): code_block.reshape(block_count, block_rows, sample_count - 0, 2, head_cou...]
  transfers between devices with their start and end apart: 1 -> 9, of which waited for: 0 -> 4; matrix products, arithmetic and copies ran while one was open for 8% -> 0% of each run, Pallas kernels for 0% -> 13%
where the time goes in v2:
time: 38.9 us; the launch traced here: 38.7 us
  Pallas kernels  18.3 us (47%)
  waiting for transfers between devices  11.2 us (29%)
  starting transfers between devices  8.49 us (22%)
  between operations  0.71 us (2%)
    ppermute x9, waiting for transfers between devices, swap(): return lax.ppermute(x, 'seq', [(i, i ^ mask) for i in range(seq)])  11.2 us
    ppermute x9, starting transfers between devices, swap(): return lax.ppermute(x, 'seq', [(i, i ^ mask) for i in range(seq)])  8.49 us
    pallas_call x1, Pallas kernels, per_device(): pl.pallas_call(functools.partial(project_kernel, **sizes, rank=rank, log_...  7.15 us
    pallas_call x1, Pallas kernels, per_device(): pl.pallas_call(functools.partial(finish_kernel, **sizes, rank=rank, lengt...  3.85 us
    pallas_call x1, Pallas kernels, per_device(): pl.pallas_call(functools.partial(own_kernel, **sizes, rank=rank), in_spec...  2.84 us
    pallas_call x1, Pallas kernels, per_device(): pl.pallas_call(functools.partial(partner_kernel, **sizes, rank=rank, orde...  2.27 us
    pallas_call x1, Pallas kernels, per_device(): pl.pallas_call(functools.partial(near_kernel, **sizes), in_specs=[VMEM, V...  2.21 us
  transfers between devices with their start and end apart: 9, of which 4 were waited for; matrix products, arithmetic and copies ran while one was open for 0% of the time, Pallas kernels for 13%

profile of v2, /device:TPU:0, one launch (start us, length us, event | category | flops | bytes accessed | tf_op | source)
XLA Modules:
  0.0 38.7 jit_solution(5033985571206116246)
XLA Ops:
  0.6 0.0 copy-start.2
  0.6 7.2 %project.1 = (bf16[1,144,384]{2,1,0:T(8,128)(2,1)S(1)}, bf16[128,384]{1,0:T(8,128)(2,1)S(1)}, f32[256,1152]{1,0:T(8,128)S(1)}) custom-call(bf16[256,3072]{1,0:T(8,128)(2,1)} %bitcast.16, bf16[3072,1152]{1,0:T(8,128)(2,1)} %w_hbm.1, f32[9,128]{1,0:T(8,128)} %bitcast.18, f32[1,128]{1,0:T(1,128)} %bitcast.19, f32[1,128]{1,0:T(1,128)} %bitcast.20, ...), custom_call_target="tpu_custom_call" | custom-call | tf_op jit(solution)/shard_map/project/pallas_call | solution.py:398
  7.8 4.0 %collective-permute-start.3 = (bf16[1,144,384]{2,1,0:T(8,128)(2,1)S(1)}, bf16[1,144,384]{2,1,0:T(8,128)(2,1)S(1)}, u32[]{:S(2)}, u32[]{:S(2)}) collective-permute-start(bf16[1,144,384]{2,1,0:T(8,128)(2,1)S(1)} %get-tuple-element.12.refs_0_), channel_id=1, source_target_pairs={{0,6},{1,7},{2,4},{3,5},{4,2},{5,3},{6,0},{7,1},{8,14},{9,15},{10,... | collective-permute-start | bytes 331784 | tf_op jit(solution)/shard_map/ppermute | solution.py:438
  11.8 0.4 %collective-permute-start.2 = (bf16[1,144,384]{2,1,0:T(8,128)(2,1)S(1)}, bf16[1,144,384]{2,1,0:T(8,128)(2,1)S(1)}, u32[]{:S(2)}, u32[]{:S(2)}) collective-permute-start(bf16[1,144,384]{2,1,0:T(8,128)(2,1)S(1)} %get-tuple-element.12.refs_0_), channel_id=1, source_target_pairs={{0,4},{1,5},{2,6},{3,7},{4,0},{5,1},{6,2},{7,3},{8,12},{9,13},{10,... | collective-permute-start | bytes 331784 | tf_op jit(solution)/shard_map/ppermute | solution.py:438
  12.3 0.2 collective-permute-start.1
  12.5 0.0 collective-permute-start.4
  12.5 3.2 %collective-permute-done.3.refs_3_.refs_2_ = bf16[1,144,384]{2,1,0:T(8,128)(2,1)S(1)} collective-permute-done((bf16[1,144,384]{2,1,0:T(8,128)(2,1)S(1)}, bf16[1,144,384]{2,1,0:T(8,128)(2,1)S(1)}, u32[]{:S(2)}, u32[]{:S(2)}) %collective-permute-start.3) | collective-permute-done | bytes 110624 | tf_op jit(solution)/shard_map/ppermute | solution.py:438
  15.7 0.0 collective-permute-start.7
  15.7 1.7 %collective-permute-done.2.refs_2_.refs_1_ = bf16[1,144,384]{2,1,0:T(8,128)(2,1)S(1)} collective-permute-done((bf16[1,144,384]{2,1,0:T(8,128)(2,1)S(1)}, bf16[1,144,384]{2,1,0:T(8,128)(2,1)S(1)}, u32[]{:S(2)}, u32[]{:S(2)}) %collective-permute-start.2) | collective-permute-done | bytes 110624 | tf_op jit(solution)/shard_map/ppermute | solution.py:438
  17.4 0.0 collective-permute-start.6
  17.4 0.0 collective-permute-done.1.refs_1_.refs_0_
  17.4 0.5 %collective-permute-start.5 = (bf16[1,144,384]{2,1,0:T(8,128)(2,1)S(1)}, bf16[1,144,384]{2,1,0:T(8,128)(2,1)S(1)}, u32[]{:S(2)}, u32[]{:S(2)}) collective-permute-start(bf16[1,144,384]{2,1,0:T(8,128)(2,1)S(1)} %collective-permute-done.1.refs_1_.refs_0_), channel_id=1, source_target_pairs={{0,1},{1,0},{2,3},{3,2},{4,5},{5,4},{6,7},{7,6},{8,9},{9,8},{10,11... | collective-permute-start | bytes 331784 | tf_op jit(solution)/shard_map/ppermute | solution.py:438
  18.0 2.6 %collective-permute-start = (bf16[128,384]{1,0:T(8,128)(2,1)S(1)}, bf16[128,384]{1,0:T(8,128)(2,1)S(1)}, u32[]{:S(2)}, u32[]{:S(2)}) collective-permute-start(bf16[128,384]{1,0:T(8,128)(2,1)S(1)} %get-tuple-element.11.query_ref), channel_id=1, source_target_pairs={{0,8},{1,9},{2,10},{3,11},{4,12},{5,13},{6,14},{7,15},{8,0},{9,1},... | collective-permute-start | bytes 294920 | tf_op jit(solution)/shard_map/ppermute | solution.py:438
  20.5 0.0 copy-done.2
  20.5 2.2 %near.1 = (f32[256,384]{1,0:T(8,128)S(1)}, f32[256,128]{1,0:T(8,128)S(1)}) custom-call(f32[256,1152]{1,0:T(8,128)S(1)} %get-tuple-element.13.qkv_ref, f32[2,3,2,128]{3,2,1,0:T(2,128)S(1)} %bitcast.13), custom_call_target="tpu_custom_call" | custom-call | flops 150994944 | bytes 1966080 | tf_op jit(solution)/shard_map/near/pallas_call | solution.py:453
  22.8 0.0 copy-start.1
  22.8 2.9 %collective-permute-done.query_ref = bf16[128,384]{1,0:T(8,128)(2,1)S(1)} collective-permute-done((bf16[128,384]{1,0:T(8,128)(2,1)S(1)}, bf16[128,384]{1,0:T(8,128)(2,1)S(1)}, u32[]{:S(2)}, u32[]{:S(2)}) %collective-permute-start) | collective-permute-done | bytes 98336 | tf_op jit(solution)/shard_map/ppermute | solution.py:438
  25.7 0.0 collective-permute-done.4.refs_4_.refs_3_
  25.7 0.0 collective-permute-done.7.refs_7_.refs_6_
  25.7 0.0 collective-permute-done.6.refs_6_.refs_5_
  25.7 0.0 collective-permute-done.5.refs_5_.refs_4_
  25.7 2.3 %partner.1.half_ref = bf16[288,128]{1,0:T(8,128)(2,1)S(1)} custom-call(bf16[128,384]{1,0:T(8,128)(2,1)S(1)} %collective-permute-done.query_ref, bf16[1,144,384]{2,1,0:T(8,128)(2,1)S(1)} %get-tuple-element.12.refs_0_, bf16[1,144,384]{2,1,0:T(8,128)(2,1)S(1)} %collective-permute-done.1.refs_1_.refs_0_, ...), custom_call_target="tpu_custom_call" | custom-call | flops 805306368 | bytes 786432 | tf_op jit(solution)/shard_map/partner/pallas_call | solution.py:477
  28.0 0.0 copy-start
  28.0 0.0 copy-start.3
  28.0 0.7 %collective-permute-start.8 = (bf16[288,128]{1,0:T(8,128)(2,1)S(1)}, bf16[288,128]{1,0:T(8,128)(2,1)S(1)}, u32[]{:S(2)}, u32[]{:S(2)}) collective-permute-start(bf16[288,128]{1,0:T(8,128)(2,1)S(1)} %partner.1.half_ref), channel_id=1, source_target_pairs={{0,8},{1,9},{2,10},{3,11},{4,12},{5,13},{6,14},{7,15},{8,0},{9,1},... | collective-permute-start | bytes 221192 | tf_op jit(solution)/shard_map/ppermute | solution.py:438
  28.7 0.0 copy-done.1
  28.7 2.8 %own.1 = (f32[256,384]{1,0:T(8,128)S(1)}, f32[256,128]{1,0:T(8,128)S(1)}) custom-call(bf16[128,384]{1,0:T(8,128)(2,1)S(1)} %get-tuple-element.11.query_ref, f32[256,384]{1,0:T(8,128)S(1)} %get-tuple-element.15.near_ref, f32[256,128]{1,0:T(8,128)S(1)} %get-tuple-element.14.refs_8_.stat_ref, f32[2,3,2,128]{3,2,1,0:T(2,128)S(1)} %bitcast.14, ...), custom_call_target="tpu_custom_call" | custom-call | flops 805306368 | bytes 786432 | tf_op jit(solution)/shard_map/own/pallas_call | solution.py:487
  31.5 3.3 %collective-permute-done.8.back_ref = bf16[288,128]{1,0:T(8,128)(2,1)S(1)} collective-permute-done((bf16[288,128]{1,0:T(8,128)(2,1)S(1)}, bf16[288,128]{1,0:T(8,128)(2,1)S(1)}, u32[]{:S(2)}, u32[]{:S(2)}) %collective-permute-start.8) | collective-permute-done | bytes 73760 | tf_op jit(solution)/shard_map/ppermute | solution.py:438
  34.9 0.0 copy-done
  34.9 0.0 copy-done.3
  34.9 3.8 %finish.1 = (bf16[256,3072]{1,0:T(8,128)(2,1)}, f32[2,3,2,128]{3,2,1,0:T(2,128)}) custom-call(bf16[288,128]{1,0:T(8,128)(2,1)S(1)} %collective-permute-done.8.back_ref, bf16[288,128]{1,0:T(8,128)(2,1)S(1)} %partner.1.half_ref, f32[256,384]{1,0:T(8,128)S(1)} %get-tuple-element.16.merged_ref, f32[256,128]{1,0:T(8,128)S(1)} %get-tuple-element.17.log_ref, ...), custom_call_target="tpu_custom_call" | custom-call | tf_op jit(solution)/shard_map/finish/pallas_call | solution.py:505
Async XLA Ops:
  0.6 19.9 %copy-start.2 = (f32[2,2,3,128]{3,1,2,0:T(2,128)S(1)}, f32[2,2,3,128]{3,1,2,0:T(2,128)}, u32[]{:S(2)}) copy-start(f32[2,2,3,128]{3,1,2,0:T(2,128)} %param.17) | copy-start | bytes 18436
  7.8 7.9 %collective-permute-start.3 = (bf16[1,144,384]{2,1,0:T(8,128)(2,1)S(1)}, bf16[1,144,384]{2,1,0:T(8,128)(2,1)S(1)}, u32[]{:S(2)}, u32[]{:S(2)}) collective-permute-start(bf16[1,144,384]{2,1,0:T(8,128)(2,1)S(1)} %get-tuple-element.12.refs_0_), channel_id=1, source_target_pairs={{0,6},{1,7},{2,4},{3,5},{4,2},{5,3},{6,0},{7,1},{8,14},{9,15},{10,... | collective-permute-start | bytes 331784 | tf_op jit(solution)/shard_map/ppermute | solution.py:438
  11.8 5.6 %collective-permute-start.2 = (bf16[1,144,384]{2,1,0:T(8,128)(2,1)S(1)}, bf16[1,144,384]{2,1,0:T(8,128)(2,1)S(1)}, u32[]{:S(2)}, u32[]{:S(2)}) collective-permute-start(bf16[1,144,384]{2,1,0:T(8,128)(2,1)S(1)} %get-tuple-element.12.refs_0_), channel_id=1, source_target_pairs={{0,4},{1,5},{2,6},{3,7},{4,0},{5,1},{6,2},{7,3},{8,12},{9,13},{10,... | collective-permute-start | bytes 331784 | tf_op jit(solution)/shard_map/ppermute | solution.py:438
  12.3 5.1 %collective-permute-start.1 = (bf16[1,144,384]{2,1,0:T(8,128)(2,1)S(1)}, bf16[1,144,384]{2,1,0:T(8,128)(2,1)S(1)}, u32[]{:S(2)}, u32[]{:S(2)}) collective-permute-start(bf16[1,144,384]{2,1,0:T(8,128)(2,1)S(1)} %get-tuple-element.12.refs_0_), channel_id=1, source_target_pairs={{0,2},{1,3},{2,0},{3,1},{4,6},{5,7},{6,4},{7,5},{8,10},{9,11},{10,... | collective-permute-start | bytes 331784 | tf_op jit(solution)/shard_map/ppermute | solution.py:438
  12.5 13.2 %collective-permute-start.4 = (bf16[1,144,384]{2,1,0:T(8,128)(2,1)S(1)}, bf16[1,144,384]{2,1,0:T(8,128)(2,1)S(1)}, u32[]{:S(2)}, u32[]{:S(2)}) collective-permute-start(bf16[1,144,384]{2,1,0:T(8,128)(2,1)S(1)} %get-tuple-element.12.refs_0_), channel_id=1, source_target_pairs={{0,1},{1,0},{2,3},{3,2},{4,5},{5,4},{6,7},{7,6},{8,9},{9,8},{10,11... | collective-permute-start | bytes 331784 | tf_op jit(solution)/shard_map/ppermute | solution.py:438
  15.7 9.9 %collective-permute-start.7 = (bf16[1,144,384]{2,1,0:T(8,128)(2,1)S(1)}, bf16[1,144,384]{2,1,0:T(8,128)(2,1)S(1)}, u32[]{:S(2)}, u32[]{:S(2)}) collective-permute-start(bf16[1,144,384]{2,1,0:T(8,128)(2,1)S(1)} %collective-permute-done.3.refs_3_.refs_2_), channel_id=1, source_target_pairs={{0,1},{1,0},{2,3},{3,2},{4,5},{5,4},{6,7},{7,6},{8,9},{9,8},{10,11... | collective-permute-start | bytes 331784 | tf_op jit(solution)/shard_map/ppermute | solution.py:438
  17.4 8.2 %collective-permute-start.6 = (bf16[1,144,384]{2,1,0:T(8,128)(2,1)S(1)}, bf16[1,144,384]{2,1,0:T(8,128)(2,1)S(1)}, u32[]{:S(2)}, u32[]{:S(2)}) collective-permute-start(bf16[1,144,384]{2,1,0:T(8,128)(2,1)S(1)} %collective-permute-done.2.refs_2_.refs_1_), channel_id=1, source_target_pairs={{0,1},{1,0},{2,3},{3,2},{4,5},{5,4},{6,7},{7,6},{8,9},{9,8},{10,11... | collective-permute-start | bytes 331784 | tf_op jit(solution)/shard_map/ppermute | solution.py:438
  17.4 8.2 %collective-permute-start.5 = (bf16[1,144,384]{2,1,0:T(8,128)(2,1)S(1)}, bf16[1,144,384]{2,1,0:T(8,128)(2,1)S(1)}, u32[]{:S(2)}, u32[]{:S(2)}) collective-permute-start(bf16[1,144,384]{2,1,0:T(8,128)(2,1)S(1)} %collective-permute-done.1.refs_1_.refs_0_), channel_id=1, source_target_pairs={{0,1},{1,0},{2,3},{3,2},{4,5},{5,4},{6,7},{7,6},{8,9},{9,8},{10,11... | collective-permute-start | bytes 331784 | tf_op jit(solution)/shard_map/ppermute | solution.py:438
  18.0 7.7 %collective-permute-start = (bf16[128,384]{1,0:T(8,128)(2,1)S(1)}, bf16[128,384]{1,0:T(8,128)(2,1)S(1)}, u32[]{:S(2)}, u32[]{:S(2)}) collective-permute-start(bf16[128,384]{1,0:T(8,128)(2,1)S(1)} %get-tuple-element.11.query_ref), channel_id=1, source_target_pairs={{0,8},{1,9},{2,10},{3,11},{4,12},{5,13},{6,14},{7,15},{8,0},{9,1},... | collective-permute-start | bytes 294920 | tf_op jit(solution)/shard_map/ppermute | solution.py:438
  22.8 5.9 %copy-start.1 = (f32[3,128,32]{1,2,0:T(8,128)S(1)}, f32[3,128,32]{1,2,0:T(8,128)}, u32[]{:S(2)}) copy-start(f32[3,128,32]{1,2,0:T(8,128)} %param.16) | copy-start | bytes 147460
  28.0 6.9 %copy-start = (bf16[384,3072]{1,0:T(8,128)(2,1)S(1)}, bf16[384,3072]{1,0:T(8,128)(2,1)}, u32[]{:S(2)}) copy-start(bf16[384,3072]{1,0:T(8,128)(2,1)} %w_ref.1) | copy-start | bytes 7077892
  28.0 6.9 %copy-start.3 = (s32[2,3]{1,0:T(2,128)S(1)}, s32[2,3]{1,0:T(2,128)}, u32[]{:S(2)}) copy-start(s32[2,3]{1,0:T(2,128)} %refresh_ref.1) | copy-start | bytes 76
  28.0 6.9 %collective-permute-start.8 = (bf16[288,128]{1,0:T(8,128)(2,1)S(1)}, bf16[288,128]{1,0:T(8,128)(2,1)S(1)}, u32[]{:S(2)}, u32[]{:S(2)}) collective-permute-start(bf16[288,128]{1,0:T(8,128)(2,1)S(1)} %partner.1.half_ref), channel_id=1, source_target_pairs={{0,8},{1,9},{2,10},{3,11},{4,12},{5,13},{6,14},{7,15},{8,0},{9,1},... | collective-permute-start | bytes 221192 | tf_op jit(solution)/shard_map/ppermute | solution.py:438

commit v3 on v2

--- a/solution.py
+++ b/solution.py
@@ -439,7 +439,6 @@
 
     far_mask = seq // 2
     bits = [m for m in (2**i for i in range(1, seq.bit_length() - 1)) if m < far_mask]
-    query_far = swap(query, far_mask)
     held = [(payload, [0])]
     direct = sum(bits[:2])
     for mask in range(2, 2 * direct, 2):
@@ -450,6 +449,8 @@
         names = [m for _, ms in held for m in ms]
         held.append((swap(block, bit), [m ^ bit for m in names]))
 
+    query_far = swap(query, far_mask)
+
     near, stats = pl.pallas_call(
         functools.partial(near_kernel, **sizes),
         in_specs=[VMEM, VMEM],
@@ -460,11 +461,14 @@
         ],
         compiler_params=params(24),
         cost_estimate=pl.CostEstimate(
-            flops=12 * rows * tokens * width, bytes_accessed=5 * rows * width * 4, transcendentals=0
+            flops=1200 * rows * tokens * width, bytes_accessed=50 * rows * width * 4, transcendentals=0
         ),
         name="near",
     )(qkv, center_rows)
 
+    for i in range(1, len(held)):
+        x, _, _ = lax.optimization_barrier((held[i][0], stats, query_far))
+        held[i] = (x, held[i][1])
     held += [(swap(a, 1), [m ^ 1 for m in ms]) for a, ms in held]
     arrays = [a for a, _ in held]
     names = [m for _, ms in held for m in ms]

time: 38.9 us -> 33.9 us (0.87)
  waiting for transfers between devices: 11.2 us -> 3.49 us
  starting transfers between devices: 8.49 us -> 11.2 us
    ppermute x9, waiting for transfers between devices: 11.2 us -> 3.49 us  [swap(): return lax.ppermute(x, 'seq', [(i, i ^ mask) for i in range(seq)])]
    ppermute x9, starting transfers between devices: 8.49 us -> 11.2 us  [swap(): return lax.ppermute(x, 'seq', [(i, i ^ mask) for i in range(seq)])]
  transfers between devices with their start and end apart: 9 -> 9, of which waited for: 4 -> 4; matrix products, arithmetic and copies ran while one was open for 0% -> 0% of each run, Pallas kernels for 13% -> 15%
where the time goes in v3:
time: 33.9 us; the launch traced here: 33.7 us
  Pallas kernels  18.3 us (54%)
  starting transfers between devices  11.2 us (33%)
  waiting for transfers between devices  3.49 us (10%)
  between operations  0.72 us (2%)
    ppermute x9, starting transfers between devices, swap(): return lax.ppermute(x, 'seq', [(i, i ^ mask) for i in range(seq)])  11.2 us
    pallas_call x1, Pallas kernels, per_device(): pl.pallas_call(functools.partial(project_kernel, **sizes, rank=rank, log_...  7.15 us
    pallas_call x1, Pallas kernels, per_device(): pl.pallas_call(functools.partial(finish_kernel, **sizes, rank=rank, lengt...  3.85 us
    ppermute x9, waiting for transfers between devices, swap(): return lax.ppermute(x, 'seq', [(i, i ^ mask) for i in range(seq)])  3.49 us
    pallas_call x1, Pallas kernels, per_device(): pl.pallas_call(functools.partial(own_kernel, **sizes, rank=rank), in_spec...  2.82 us
    pallas_call x1, Pallas kernels, per_device(): pl.pallas_call(functools.partial(partner_kernel, **sizes, rank=rank, orde...  2.28 us
    pallas_call x1, Pallas kernels, per_device(): pl.pallas_call(functools.partial(near_kernel, **sizes), in_specs=[VMEM, V...  2.21 us
  transfers between devices with their start and end apart: 9, of which 4 were waited for; matrix products, arithmetic and copies ran while one was open for 0% of the time, Pallas kernels for 15%

profile of v3, /device:TPU:0, one launch (start us, length us, event | category | flops | bytes accessed | tf_op | source)
XLA Modules:
  0.0 33.7 jit_solution(4330662286173416980)
XLA Ops:
  0.6 0.0 copy-start.2
  0.6 7.2 %project.1 = (bf16[1,144,384]{2,1,0:T(8,128)(2,1)S(1)}, bf16[128,384]{1,0:T(8,128)(2,1)S(1)}, f32[256,1152]{1,0:T(8,128)S(1)}) custom-call(bf16[256,3072]{1,0:T(8,128)(2,1)} %bitcast.16, bf16[3072,1152]{1,0:T(8,128)(2,1)} %w_hbm.1, f32[9,128]{1,0:T(8,128)} %bitcast.18, f32[1,128]{1,0:T(1,128)} %bitcast.19, f32[1,128]{1,0:T(1,128)} %bitcast.20, ...), custom_call_target="tpu_custom_call" | custom-call | tf_op jit(solution)/shard_map/project/pallas_call | solution.py:398
  7.8 0.5 %collective-permute-start.4 = (bf16[1,144,384]{2,1,0:T(8,128)(2,1)S(1)}, bf16[1,144,384]{2,1,0:T(8,128)(2,1)S(1)}, u32[]{:S(2)}, u32[]{:S(2)}) collective-permute-start(bf16[1,144,384]{2,1,0:T(8,128)(2,1)S(1)} %get-tuple-element.15.refs_0_), channel_id=1, source_target_pairs={{0,1},{1,0},{2,3},{3,2},{4,5},{5,4},{6,7},{7,6},{8,9},{9,8},{10,11... | collective-permute-start | bytes 331784 | tf_op jit(solution)/shard_map/ppermute | solution.py:438
  8.3 3.6 %collective-permute-start.3 = (bf16[1,144,384]{2,1,0:T(8,128)(2,1)S(1)}, bf16[1,144,384]{2,1,0:T(8,128)(2,1)S(1)}, u32[]{:S(2)}, u32[]{:S(2)}) collective-permute-start(bf16[1,144,384]{2,1,0:T(8,128)(2,1)S(1)} %get-tuple-element.15.refs_0_), channel_id=1, source_target_pairs={{0,6},{1,7},{2,4},{3,5},{4,2},{5,3},{6,0},{7,1},{8,14},{9,15},{10,... | collective-permute-start | bytes 331784 | tf_op jit(solution)/shard_map/ppermute | solution.py:438
  11.9 0.4 %collective-permute-start.2 = (bf16[1,144,384]{2,1,0:T(8,128)(2,1)S(1)}, bf16[1,144,384]{2,1,0:T(8,128)(2,1)S(1)}, u32[]{:S(2)}, u32[]{:S(2)}) collective-permute-start(bf16[1,144,384]{2,1,0:T(8,128)(2,1)S(1)} %get-tuple-element.15.refs_0_), channel_id=1, source_target_pairs={{0,4},{1,5},{2,6},{3,7},{4,0},{5,1},{6,2},{7,3},{8,12},{9,13},{10,... | collective-permute-start | bytes 331784 | tf_op jit(solution)/shard_map/ppermute | solution.py:438
  12.4 0.2 collective-permute-start.1
  12.6 2.9 %collective-permute-start = (bf16[128,384]{1,0:T(8,128)(2,1)S(1)}, bf16[128,384]{1,0:T(8,128)(2,1)S(1)}, u32[]{:S(2)}, u32[]{:S(2)}) collective-permute-start(bf16[128,384]{1,0:T(8,128)(2,1)S(1)} %get-tuple-element.14.query_ref), channel_id=1, source_target_pairs={{0,8},{1,9},{2,10},{3,11},{4,12},{5,13},{6,14},{7,15},{8,0},{9,1},... | collective-permute-start | bytes 294920 | tf_op jit(solution)/shard_map/ppermute | solution.py:438
  15.5 0.0 copy-done.2
  15.5 2.2 %near.1 = (f32[256,384]{1,0:T(8,128)S(1)}, f32[256,128]{1,0:T(8,128)S(1)}) custom-call(f32[256,1152]{1,0:T(8,128)S(1)} %get-tuple-element.16.qkv_ref, f32[2,3,2,128]{3,2,1,0:T(2,128)S(1)} %bitcast.13), custom_call_target="tpu_custom_call" | custom-call | flops 15099494400 | bytes 19660800 | tf_op jit(solution)/shard_map/near/pallas_call | solution.py:454
  17.7 0.0 copy-start.1
  17.7 1.7 %collective-permute-done.query_ref = bf16[128,384]{1,0:T(8,128)(2,1)S(1)} collective-permute-done((bf16[128,384]{1,0:T(8,128)(2,1)S(1)}, bf16[128,384]{1,0:T(8,128)(2,1)S(1)}, u32[]{:S(2)}, u32[]{:S(2)}) %collective-permute-start) | collective-permute-done | bytes 98336 | tf_op jit(solution)/shard_map/ppermute | solution.py:438
  19.4 0.0 collective-permute-done.3.refs_3_.refs_2_
  19.4 0.0 collective-permute-start.7
  19.4 0.9 %collective-permute-done.2.refs_2_.refs_1_ = bf16[1,144,384]{2,1,0:T(8,128)(2,1)S(1)} collective-permute-done((bf16[1,144,384]{2,1,0:T(8,128)(2,1)S(1)}, bf16[1,144,384]{2,1,0:T(8,128)(2,1)S(1)}, u32[]{:S(2)}, u32[]{:S(2)}) %collective-permute-start.2) | collective-permute-done | bytes 110624 | tf_op jit(solution)/shard_map/ppermute | solution.py:438
  20.2 0.0 collective-permute-start.6
  20.2 0.0 collective-permute-done.1.refs_1_.refs_0_
  20.2 0.5 %collective-permute-start.5 = (bf16[1,144,384]{2,1,0:T(8,128)(2,1)S(1)}, bf16[1,144,384]{2,1,0:T(8,128)(2,1)S(1)}, u32[]{:S(2)}, u32[]{:S(2)}) collective-permute-start(bf16[1,144,384]{2,1,0:T(8,128)(2,1)S(1)} %collective-permute-done.1.refs_1_.refs_0_), channel_id=1, source_target_pairs={{0,1},{1,0},{2,3},{3,2},{4,5},{5,4},{6,7},{7,6},{8,9},{9,8},{10,11... | collective-permute-start | bytes 331784 | tf_op jit(solution)/shard_map/ppermute | solution.py:438
  20.8 0.0 collective-permute-done.4.refs_4_.refs_3_
  20.8 0.0 collective-permute-done.7.refs_7_.refs_6_
  20.8 0.8 %collective-permute-done.6.refs_6_.refs_5_ = bf16[1,144,384]{2,1,0:T(8,128)(2,1)S(1)} collective-permute-done((bf16[1,144,384]{2,1,0:T(8,128)(2,1)S(1)}, bf16[1,144,384]{2,1,0:T(8,128)(2,1)S(1)}, u32[]{:S(2)}, u32[]{:S(2)}) %collective-permute-start.6) | collective-permute-done | bytes 110624 | tf_op jit(solution)/shard_map/ppermute | solution.py:438
  21.6 0.2 collective-permute-done.5.refs_5_.refs_4_
  21.7 2.3 %partner.1.half_ref = bf16[288,128]{1,0:T(8,128)(2,1)S(1)} custom-call(bf16[128,384]{1,0:T(8,128)(2,1)S(1)} %collective-permute-done.query_ref, bf16[1,144,384]{2,1,0:T(8,128)(2,1)S(1)} %get-tuple-element.15.refs_0_, bf16[1,144,384]{2,1,0:T(8,128)(2,1)S(1)} %collective-permute-done.1.refs_1_.refs_0_, ...), custom_call_target="tpu_custom_call" | custom-call | flops 805306368 | bytes 786432 | tf_op jit(solution)/shard_map/partner/pallas_call | solution.py:481
  24.0 0.0 copy-start
  24.0 0.0 copy-start.3
  24.0 3.0 %collective-permute-start.8 = (bf16[288,128]{1,0:T(8,128)(2,1)S(1)}, bf16[288,128]{1,0:T(8,128)(2,1)S(1)}, u32[]{:S(2)}, u32[]{:S(2)}) collective-permute-start(bf16[288,128]{1,0:T(8,128)(2,1)S(1)} %partner.1.half_ref), channel_id=1, source_target_pairs={{0,8},{1,9},{2,10},{3,11},{4,12},{5,13},{6,14},{7,15},{8,0},{9,1},... | collective-permute-start | bytes 221192 | tf_op jit(solution)/shard_map/ppermute | solution.py:438
  27.0 0.0 copy-done.1
  27.0 2.8 %own.1 = (f32[256,384]{1,0:T(8,128)S(1)}, f32[256,128]{1,0:T(8,128)S(1)}) custom-call(bf16[128,384]{1,0:T(8,128)(2,1)S(1)} %get-tuple-element.14.query_ref, f32[256,384]{1,0:T(8,128)S(1)} %get-tuple-element.21.near_ref, f32[256,128]{1,0:T(8,128)S(1)} %get-tuple-element.17.refs_8_.stat_ref, f32[2,3,2,128]{3,2,1,0:T(2,128)S(1)} %bitcast.14, ...), custom_call_target="tpu_custom_call" | custom-call | flops 805306368 | bytes 786432 | tf_op jit(solution)/shard_map/own/pallas_call | solution.py:491
  29.9 0.0 collective-permute-done.8.back_ref
  29.9 0.0 copy-done
  29.9 0.0 copy-done.3
  29.9 3.9 %finish.1 = (bf16[256,3072]{1,0:T(8,128)(2,1)}, f32[2,3,2,128]{3,2,1,0:T(2,128)}) custom-call(bf16[288,128]{1,0:T(8,128)(2,1)S(1)} %collective-permute-done.8.back_ref, bf16[288,128]{1,0:T(8,128)(2,1)S(1)} %partner.1.half_ref, f32[256,384]{1,0:T(8,128)S(1)} %get-tuple-element.22.merged_ref, f32[256,128]{1,0:T(8,128)S(1)} %get-tuple-element.23.log_ref, ...), custom_call_target="tpu_custom_call" | custom-call | tf_op jit(solution)/shard_map/finish/pallas_call | solution.py:509
Async XLA Ops:
  0.6 14.8 %copy-start.2 = (f32[2,2,3,128]{3,1,2,0:T(2,128)S(1)}, f32[2,2,3,128]{3,1,2,0:T(2,128)}, u32[]{:S(2)}) copy-start(f32[2,2,3,128]{3,1,2,0:T(2,128)} %param.17) | copy-start | bytes 18436
  7.8 13.0 %collective-permute-start.4 = (bf16[1,144,384]{2,1,0:T(8,128)(2,1)S(1)}, bf16[1,144,384]{2,1,0:T(8,128)(2,1)S(1)}, u32[]{:S(2)}, u32[]{:S(2)}) collective-permute-start(bf16[1,144,384]{2,1,0:T(8,128)(2,1)S(1)} %get-tuple-element.15.refs_0_), channel_id=1, source_target_pairs={{0,1},{1,0},{2,3},{3,2},{4,5},{5,4},{6,7},{7,6},{8,9},{9,8},{10,11... | collective-permute-start | bytes 331784 | tf_op jit(solution)/shard_map/ppermute | solution.py:438
  8.3 11.1 %collective-permute-start.3 = (bf16[1,144,384]{2,1,0:T(8,128)(2,1)S(1)}, bf16[1,144,384]{2,1,0:T(8,128)(2,1)S(1)}, u32[]{:S(2)}, u32[]{:S(2)}) collective-permute-start(bf16[1,144,384]{2,1,0:T(8,128)(2,1)S(1)} %get-tuple-element.15.refs_0_), channel_id=1, source_target_pairs={{0,6},{1,7},{2,4},{3,5},{4,2},{5,3},{6,0},{7,1},{8,14},{9,15},{10,... | collective-permute-start | bytes 331784 | tf_op jit(solution)/shard_map/ppermute | solution.py:438
  11.9 8.3 %collective-permute-start.2 = (bf16[1,144,384]{2,1,0:T(8,128)(2,1)S(1)}, bf16[1,144,384]{2,1,0:T(8,128)(2,1)S(1)}, u32[]{:S(2)}, u32[]{:S(2)}) collective-permute-start(bf16[1,144,384]{2,1,0:T(8,128)(2,1)S(1)} %get-tuple-element.15.refs_0_), channel_id=1, source_target_pairs={{0,4},{1,5},{2,6},{3,7},{4,0},{5,1},{6,2},{7,3},{8,12},{9,13},{10,... | collective-permute-start | bytes 331784 | tf_op jit(solution)/shard_map/ppermute | solution.py:438
  12.4 7.9 %collective-permute-start.1 = (bf16[1,144,384]{2,1,0:T(8,128)(2,1)S(1)}, bf16[1,144,384]{2,1,0:T(8,128)(2,1)S(1)}, u32[]{:S(2)}, u32[]{:S(2)}) collective-permute-start(bf16[1,144,384]{2,1,0:T(8,128)(2,1)S(1)} %get-tuple-element.15.refs_0_), channel_id=1, source_target_pairs={{0,2},{1,3},{2,0},{3,1},{4,6},{5,7},{6,4},{7,5},{8,10},{9,11},{10,... | collective-permute-start | bytes 331784 | tf_op jit(solution)/shard_map/ppermute | solution.py:438
  12.6 6.8 %collective-permute-start = (bf16[128,384]{1,0:T(8,128)(2,1)S(1)}, bf16[128,384]{1,0:T(8,128)(2,1)S(1)}, u32[]{:S(2)}, u32[]{:S(2)}) collective-permute-start(bf16[128,384]{1,0:T(8,128)(2,1)S(1)} %get-tuple-element.14.query_ref), channel_id=1, source_target_pairs={{0,8},{1,9},{2,10},{3,11},{4,12},{5,13},{6,14},{7,15},{8,0},{9,1},... | collective-permute-start | bytes 294920 | tf_op jit(solution)/shard_map/ppermute | solution.py:438
  17.7 9.3 %copy-start.1 = (f32[3,128,32]{1,2,0:T(8,128)S(1)}, f32[3,128,32]{1,2,0:T(8,128)}, u32[]{:S(2)}) copy-start(f32[3,128,32]{1,2,0:T(8,128)} %param.16) | copy-start | bytes 147460
  19.4 1.4 %collective-permute-start.7 = (bf16[1,144,384]{2,1,0:T(8,128)(2,1)S(1)}, bf16[1,144,384]{2,1,0:T(8,128)(2,1)S(1)}, u32[]{:S(2)}, u32[]{:S(2)}) collective-permute-start(bf16[1,144,384]{2,1,0:T(8,128)(2,1)S(1)} %collective-permute-done.3.refs_3_.refs_2_), channel_id=1, source_target_pairs={{0,1},{1,0},{2,3},{3,2},{4,5},{5,4},{6,7},{7,6},{8,9},{9,8},{10,11... | collective-permute-start | bytes 331784 | tf_op jit(solution)/shard_map/ppermute | solution.py:438
  20.2 1.3 %collective-permute-start.6 = (bf16[1,144,384]{2,1,0:T(8,128)(2,1)S(1)}, bf16[1,144,384]{2,1,0:T(8,128)(2,1)S(1)}, u32[]{:S(2)}, u32[]{:S(2)}) collective-permute-start(bf16[1,144,384]{2,1,0:T(8,128)(2,1)S(1)} %collective-permute-done.2.refs_2_.refs_1_), channel_id=1, source_target_pairs={{0,1},{1,0},{2,3},{3,2},{4,5},{5,4},{6,7},{7,6},{8,9},{9,8},{10,11... | collective-permute-start | bytes 331784 | tf_op jit(solution)/shard_map/ppermute | solution.py:438
  20.2 1.5 %collective-permute-start.5 = (bf16[1,144,384]{2,1,0:T(8,128)(2,1)S(1)}, bf16[1,144,384]{2,1,0:T(8,128)(2,1)S(1)}, u32[]{:S(2)}, u32[]{:S(2)}) collective-permute-start(bf16[1,144,384]{2,1,0:T(8,128)(2,1)S(1)} %collective-permute-done.1.refs_1_.refs_0_), channel_id=1, source_target_pairs={{0,1},{1,0},{2,3},{3,2},{4,5},{5,4},{6,7},{7,6},{8,9},{9,8},{10,11... | collective-permute-start | bytes 331784 | tf_op jit(solution)/shard_map/ppermute | solution.py:438
  24.0 5.9 %copy-start = (bf16[384,3072]{1,0:T(8,128)(2,1)S(1)}, bf16[384,3072]{1,0:T(8,128)(2,1)}, u32[]{:S(2)}) copy-start(bf16[384,3072]{1,0:T(8,128)(2,1)} %w_ref.1) | copy-start | bytes 7077892
  24.0 5.9 %copy-start.3 = (s32[2,3]{1,0:T(2,128)S(1)}, s32[2,3]{1,0:T(2,128)}, u32[]{:S(2)}) copy-start(s32[2,3]{1,0:T(2,128)} %refresh_ref.1) | copy-start | bytes 76
  24.0 5.8 %collective-permute-start.8 = (bf16[288,128]{1,0:T(8,128)(2,1)S(1)}, bf16[288,128]{1,0:T(8,128)(2,1)S(1)}, u32[]{:S(2)}, u32[]{:S(2)}) collective-permute-start(bf16[288,128]{1,0:T(8,128)(2,1)S(1)} %partner.1.half_ref), channel_id=1, source_target_pairs={{0,8},{1,9},{2,10},{3,11},{4,12},{5,13},{6,14},{7,15},{8,0},{9,1},... | collective-permute-start | bytes 221192 | tf_op jit(solution)/shard_map/ppermute | solution.py:438

commit v4 on v3

--- a/solution.py
+++ b/solution.py
@@ -77,7 +77,7 @@
     images_hbm, w_hbm, b_hbm, qg_hbm, kg_hbm, kb_hbm, vb_hbm, centers_hbm,
     payload_ref, query_ref, qkv_ref,
     x_ref, w_ref, b_ref, qg_ref, kg_ref, kb_ref, vb_ref, centers_ref,
-    acc_ref, tiles_h, tiles_l, last_h, last_l, sums_ref, big_sem, small_sem,
+    acc_ref, main_ref, tail_ref, sums_ref, big_sem, small_sem,
     *, samples, tokens, heads, dim, rank, log_factor,
 ):
     chunks, _, depth = x_ref.shape
@@ -103,30 +103,11 @@
     for c in range(chunks):
         x_copy(c).start()
         w_copy(c).start()
-        if c == 0:
-            for copy in small:
-                copy.start()
-    tiles_h[...] = jnp.zeros_like(tiles_h)
-    tiles_l[...] = jnp.zeros_like(tiles_l)
-    last_h[...] = jnp.zeros_like(last_h)
-    last_l[...] = jnp.zeros_like(last_l)
+    for copy in small:
+        copy.start()
+    main_ref[...] = jnp.zeros_like(main_ref)
+    tail_ref[...] = jnp.zeros_like(tail_ref)
     sums_ref[...] = jnp.zeros_like(sums_ref)
-    for copy in small:
-        copy.wait()
-    for h in range(heads):
-        kh, kl = split(kb_ref[h])
-        vh, vl = split(vb_ref[h])
-        for b in range(samples):
-            at = key_lane(b, h, rank)
-            tiles_h[b, at : at + rank, h * dim : (h + 1) * dim] = kh
-            tiles_l[b, at : at + rank, h * dim : (h + 1) * dim] = kl
-            at = value_lane(b, h, rank, heads)
-            if h == 0:
-                tiles_h[b, at : at + rank, width : width + dim] = vh
-                tiles_l[b, at : at + rank, width : width + dim] = vl
-            else:
-                last_h[at : at + rank, (h - 1) * dim : h * dim] = vh
-                last_l[at : at + rank, (h - 1) * dim : h * dim] = vl
     for c in range(chunks):
         x_copy(c).wait()
         w_copy(c).wait()
@@ -136,6 +117,19 @@
         else:
             acc_ref[...] += part
 
+    for copy in small:
+        copy.wait()
+    half = dim // 2
+    for h in range(heads):
+        for p, (k, v) in enumerate(zip(split(kb_ref[h]), split(vb_ref[h]))):
+            at = p * dim + key_lane(0, h, rank)
+            main_ref[at : at + rank, h * dim : (h + 1) * dim] = k
+            at = value_lane(0, h, rank, heads)
+            if h == 0:
+                main_ref[p * dim + at : p * dim + at + rank, width:] = v
+            else:
+                at = p * half + at
+                tail_ref[at : at + rank, (h - 1) * dim : h * dim] = v
     def column(at):
         return acc_ref[:, at * dim : (at + 1) * dim] + b_ref[at : at + 1, :]
 
@@ -159,36 +153,63 @@
             sums_ref[row + 1 : row + 2, :] = jnp.sum(v[rows], axis=0, keepdims=True)
     for p, piece in enumerate(pieces_of(sums_ref[...], 3)):
         payload_ref[0, tokens : tokens + SUM_ROWS, p * dim : (p + 1) * dim] = piece
-    lasts, highs, lows = [], [], []
-    for b in range(samples):
-        rows = slice(b * tokens, (b + 1) * tokens)
-        shifted = [keys[h][rows] - centers_ref[b, h, 0:1, :] for h in range(heads)]
-        shifted += [values[h][rows] - centers_ref[b, h, 1:2, :] for h in range(heads)]
-        main = split(jnp.concatenate(shifted[: heads + 1], axis=1))
-        code = dot3(main, (tiles_h[b], tiles_l[b]), NT)
-        payload_ref[0, :tokens, b * dim : (b + 1) * dim] = code.astype(bf16)
-        tail = split(jnp.concatenate(shifted[heads + 1 :], axis=1))
-        lasts.append(dot3(tail, (last_h[...], last_l[...]), NT))
-        query = split(jnp.concatenate([q[rows] for q in queries], axis=1))
-        query_code = dot3(query, (tiles_h[b, :, :width], tiles_l[b, :, :width]), NT) * log_factor
-        high = query_code.astype(bf16).astype(f32)
-        highs.append(high)
-        lows.append(query_code - high)
+    def by_sample(j):
+        rows = [centers_ref[b, h, j : j + 1, :] for b in range(samples) for h in range(heads)]
+        return [
+            jnp.concatenate(
+                [jnp.broadcast_to(rows[b * heads + h], (tokens, dim)) for b in range(samples)], axis=0
+            )
+            for h in range(heads)
+        ]
+
+    key_centers, value_centers = by_sample(0), by_sample(1)
+    shifted = [keys[h] - key_centers[h] for h in range(heads)]
+    shifted += [values[h] - value_centers[h] for h in range(heads)]
+
+    def coded(x, columns):
+        high, low = split(x)
+        both = dot(high, main_ref[:, columns], NT)
+        return both[:, :dim] + (both[:, dim:] + dot(low, main_ref[:dim, columns], NT))
+
+    code = coded(jnp.concatenate(shifted[: heads + 1], axis=1), slice(0, width + dim))
+    query_code = coded(jnp.concatenate(queries, axis=1), slice(0, width)) * log_factor
+    high, low = split(jnp.concatenate(shifted[heads + 1 :], axis=1))
+    both = dot(high, tail_ref[...], NT)
+    tail = both + pltpu.roll(both, half, 1) + dot(low, tail_ref[...], NT)
+    payload_ref[0, :tokens, :dim] = code[:tokens].astype(bf16)
+    payload_ref[0, :tokens, dim : 2 * dim] = pltpu.roll(code[tokens:], rank, 1).astype(bf16)
     lanes = lane_ids(tokens, dim)
-    last = jnp.where(lanes < (heads - 1) * rank, lasts[0], lasts[1])
+    last = jnp.where(lanes < half, tail[:tokens], pltpu.roll(tail[tokens:], half, 1))
     payload_ref[0, :tokens, samples * dim :] = last.astype(bf16)
-    turned = pltpu.roll(lows[1], dim // 2, 1)
-    query_ref[:, :dim] = jnp.where(lanes < heads * rank, highs[0], turned).astype(bf16)
-    query_ref[:, dim : 2 * dim] = jnp.where(lanes < rank, turned, highs[1]).astype(bf16)
-    query_ref[:, 2 * dim :] = jnp.where(lanes < heads * rank, lows[0], lows[1]).astype(bf16)
+    high_0 = query_code[:tokens].astype(bf16).astype(f32)
+    low_0 = query_code[:tokens] - high_0
+    query_1 = pltpu.roll(query_code[tokens:], rank, 1)
+    high_1 = query_1.astype(bf16).astype(f32)
+    low_1 = query_1 - high_1
+    turned = pltpu.roll(low_1, half, 1)
+    query_ref[:, :dim] = jnp.where(lanes < heads * rank, high_0, turned).astype(bf16)
+    query_ref[:, dim : 2 * dim] = jnp.where(lanes < rank, turned, high_1).astype(bf16)
+    query_ref[:, 2 * dim :] = jnp.where(lanes < heads * rank, low_0, low_1).astype(bf16)
     for h in range(heads):
         qkv_ref[:, h * dim : (h + 1) * dim] = queries[h] * log_factor
         qkv_ref[:, width + h * dim : width + (h + 1) * dim] = keys[h]
         qkv_ref[:, 2 * width + h * dim : 2 * width + (h + 1) * dim] = values[h]
 
 
-def near_kernel(qkv_ref, centers_ref, near_ref, stat_ref, *, samples, tokens, heads, dim):
+def near_kernel(
+    qkv_ref, centers_ref, refresh_ref, vb_ref, near_ref, stat_ref, basis_h, basis_l, old_ref,
+    *, samples, tokens, heads, dim, rank,
+):
     width = heads * dim
+    fill_basis(basis_h, basis_l, vb_ref, samples, heads, dim, rank)
+    old_ref[...] = jnp.zeros_like(old_ref)
+    for b in range(samples):
+        for h in range(heads):
+            for j in range(2):
+                row = (b * heads + h) * 2 + j
+                keep = jnp.where(refresh_ref[j, h] == 1, 0.0, 1.0)
+                old_ref[row : row + 1, :] = centers_ref[b, h, j : j + 1, :]
+                old_ref[SUM_ROWS + row : SUM_ROWS + row + 1, :] = jnp.full((1, dim), keep, f32)
     lanes = lane_ids(tokens, dim)
     for b in range(samples):
         rows = slice(b * tokens, (b + 1) * tokens)
@@ -289,11 +310,11 @@
 
 
 def own_kernel(
-    query_ref, near_ref, stat_ref, centers_ref, vb_ref, *refs, samples, tokens, heads, dim, rank
+    query_ref, near_ref, stat_ref, old_ref, basis_h, basis_l, *refs,
+    samples, tokens, heads, dim, rank,
 ):
-    merged_ref, log_ref, basis_h, basis_l = refs[-4:]
-    fill_basis(basis_h, basis_l, vb_ref, samples, heads, dim, rank)
-    tiles = tiles_of(refs[:-4])
+    merged_ref, log_ref = refs[-2:]
+    tiles = tiles_of(refs[:-2])
     lanes = lane_ids(tokens, dim)
     for b in range(samples):
         rows = slice(b * tokens, (b + 1) * tokens)
@@ -312,7 +333,8 @@
             near_part, far_part = jnp.exp2(near_log - top), jnp.exp2(far_log - top)
             whole = near_part + far_part
             merged = near_ref[rows, columns] * (near_part / whole)
-            merged = merged + (far[:, columns] + centers_ref[b, h, 1:2, :]) * (far_part / whole)
+            row = (b * heads + h) * 2 + 1
+            merged = merged + (far[:, columns] + old_ref[row : row + 1, :]) * (far_part / whole)
             merged_ref[rows, columns] = merged
             kept = jnp.where(lanes == h, top + jnp.log(whole) * log2_e, kept)
             kept = jnp.where(lanes == heads + h, center, kept)
@@ -320,11 +342,26 @@
 
 
 def finish_kernel(
-    back_ref, half_ref, merged_ref, log_ref, centers_ref, refresh_ref, vb_ref, w_ref,
-    mixed_hbm, new_ref, attended_ref, basis_h, basis_l, mixed_ref, sem,
+    back_ref, half_ref, merged_ref, log_ref, old_ref, basis_h, basis_l, w_ref,
+    mixed_hbm, new_hbm, attended_ref, mixed_ref, new_ref, sem, new_sem,
     *, samples, tokens, heads, dim, rank, length,
 ):
-    fill_basis(basis_h, basis_l, vb_ref, samples, heads, dim, rank)
+    first = samples * tokens
+    sums = [
+        ref[first : first + SUM_ROWS, :].astype(f32)
+        + ref[first + SUM_ROWS : first + 2 * SUM_ROWS, :].astype(f32)
+        for ref in (half_ref, back_ref)
+    ]
+    fresh = (sums[0] + sums[1]) * (1.0 / length)
+    fresh = jnp.where(old_ref[SUM_ROWS:, :] > 0.5, old_ref[:SUM_ROWS, :], fresh)
+    for b in range(samples):
+        for h in range(heads):
+            row = (b * heads + h) * 2
+            new_ref[b, h] = fresh[row : row + 2, :]
+    new_copy = pltpu.make_async_copy(new_ref, new_hbm, new_sem.at[0])
+    new_copy.start()
+    chunks, columns = mixed_ref.shape[1], mixed_ref.shape[3]
+    copies = []
     for b in range(samples):
         rows = slice(b * tokens, (b + 1) * tokens)
         codes = back_ref[rows, :]
@@ -332,7 +369,7 @@
         extra = codes.astype(f32)
         logs = log_ref[rows, :]
         for h in range(heads):
-            columns = slice(h * dim, (h + 1) * dim)
+            head = slice(h * dim, (h + 1) * dim)
             spot = free_lane(b, rank) + 3 * h
             far_log = extra[:, spot : spot + 1] + (
                 extra[:, spot + 1 : spot + 2] + extra[:, spot + 2 : spot + 3]
@@ -342,33 +379,19 @@
             top = jnp.maximum(own_log, far_log)
             own_part, far_part = jnp.exp2(own_log - top), jnp.exp2(far_log - top)
             whole = own_part + far_part
-            value = merged_ref[rows, columns] * (own_part / whole)
-            value = value + (far[:, columns] + centers_ref[b, h, 1:2, :]) * (far_part / whole)
-            attended_ref[rows, columns] = value.astype(bf16)
-    chunks, _, columns = mixed_ref.shape
-    copies = []
-    for c in range(chunks):
-        place = slice(c * columns, (c + 1) * columns)
-        mixed_ref[c] = dot(attended_ref[...], w_ref[:, place]).astype(bf16)
-        copy = pltpu.make_async_copy(mixed_ref.at[c], mixed_hbm.at[:, place], sem.at[c])
-        copy.start()
-        copies.append(copy)
-    first = samples * tokens
-    sums = [
-        ref[first : first + SUM_ROWS, :].astype(f32)
-        + ref[first + SUM_ROWS : first + 2 * SUM_ROWS, :].astype(f32)
-        for ref in (half_ref, back_ref)
-    ]
-    fresh = (sums[0] + sums[1]) * (1.0 / length)
-    for b in range(samples):
-        for h in range(heads):
-            for j in range(2):
-                row = (b * heads + h) * 2 + j
-                old = centers_ref[b, h, j : j + 1, :]
-                new_ref[b, h, j : j + 1, :] = jnp.where(
-                    refresh_ref[j, h] == 1, fresh[row : row + 1, :], old
-                )
-    for copy in copies:
+            row = (b * heads + h) * 2 + 1
+            value = merged_ref[rows, head] * (own_part / whole)
+            value = value + (far[:, head] + old_ref[row : row + 1, :]) * (far_part / whole)
+            attended_ref[rows, head] = value.astype(bf16)
+        for c in range(chunks):
+            place = slice(c * columns, (c + 1) * columns)
+            mixed_ref[b, c] = dot(attended_ref[rows, :], w_ref[:, place]).astype(bf16)
+            copy = pltpu.make_async_copy(
+                mixed_ref.at[b, c], mixed_hbm.at[rows, place], sem.at[b, c]
+            )
+            copy.start()
+            copies.append(copy)
+    for copy in copies + [new_copy]:
         copy.wait()
 
 
@@ -390,7 +413,7 @@
     key_rows = key_basis.transpose(0, 2, 1)
     value_rows = value_basis.transpose(0, 2, 1)
     center_rows = centers.transpose(0, 2, 1, 3)
-    chunks = 6
+    chunks = 3
     depth = model // chunks
     shard = (1, tokens + SUM_ROWS, width)
     params = lambda mib: pltpu.CompilerParams(vmem_limit_bytes=mib * 2**20)
@@ -414,9 +437,7 @@
             pltpu.VMEM((heads, rank, dim), f32),
             pltpu.VMEM((samples, heads, 2, dim), f32),
             pltpu.VMEM((rows, 3 * width), f32),
-            pltpu.VMEM((samples, dim, width + dim), bf16),
-            pltpu.VMEM((samples, dim, width + dim), bf16),
-            pltpu.VMEM((dim, width - dim), bf16),
+            pltpu.VMEM((2 * dim, width + dim), bf16),
             pltpu.VMEM((dim, width - dim), bf16),
             pltpu.VMEM((SUM_ROWS, dim), f32),
             pltpu.SemaphoreType.DMA((2, chunks)),
@@ -451,23 +472,26 @@
 
     query_far = swap(query, far_mask)
 
-    near, stats = pl.pallas_call(
-        functools.partial(near_kernel, **sizes),
-        in_specs=[VMEM, VMEM],
-        out_specs=[VMEM, VMEM],
+    near, stats, basis_high, basis_low, old = pl.pallas_call(
+        functools.partial(near_kernel, **sizes, rank=rank),
+        in_specs=[VMEM, VMEM, pl.BlockSpec(memory_space=pltpu.SMEM), VMEM],
+        out_specs=[VMEM] * 5,
         out_shape=[
             jax.ShapeDtypeStruct((rows, width), f32),
             jax.ShapeDtypeStruct((rows, dim), f32),
+            jax.ShapeDtypeStruct((samples, dim, width), bf16),
+            jax.ShapeDtypeStruct((samples, dim, width), bf16),
+            jax.ShapeDtypeStruct((2 * SUM_ROWS, dim), f32),
         ],
         compiler_params=params(24),
         cost_estimate=pl.CostEstimate(
             flops=1200 * rows * tokens * width, bytes_accessed=50 * rows * width * 4, transcendentals=0
         ),
         name="near",
-    )(qkv, center_rows)
+    )(qkv, center_rows, refresh, value_rows)
 
     for i in range(1, len(held)):
-        x, _, _ = lax.optimization_barrier((held[i][0], stats, query_far))
+        x, _, _ = lax.optimization_barrier((held[i][0], stats, query_far if i == 1 else stats))
         held[i] = (x, held[i][1])
     held += [(swap(a, 1), [m ^ 1 for m in ms]) for a, ms in held]
     arrays = [a for a, _ in held]
@@ -490,40 +514,36 @@
     returned = swap(back, far_mask)
     merged, logs = pl.pallas_call(
         functools.partial(own_kernel, **sizes, rank=rank),
-        in_specs=[VMEM] * (4 + len(arrays)),
-        out_specs=[VMEM, VMEM],
+        in_specs=[VMEM] * (5 + len(arrays)),
+        out_specs=[VMEM] * 2,
         out_shape=[
             jax.ShapeDtypeStruct((rows, width), f32),
             jax.ShapeDtypeStruct((rows, dim), f32),
         ],
-        scratch_shapes=[
-            pltpu.VMEM((samples, dim, width), bf16),
-            pltpu.VMEM((samples, dim, width), bf16),
-        ],
         compiler_params=params(32),
         cost_estimate=cost,
         name="own",
-    )(query, near, stats, center_rows, value_rows, *arrays[1:])
-
-    columns = 512
+    )(query, near, stats, old, basis_high, basis_low, *arrays[1:])
+
+    columns = 768
     mixed, new_centers = pl.pallas_call(
         functools.partial(finish_kernel, **sizes, rank=rank, length=tokens * seq),
-        in_specs=[VMEM] * 5 + [pl.BlockSpec(memory_space=pltpu.SMEM), VMEM, VMEM],
-        out_specs=[HBM, VMEM],
+        in_specs=[VMEM] * 8,
+        out_specs=[HBM, HBM],
         out_shape=[
             jax.ShapeDtypeStruct((rows, model), bf16),
             jax.ShapeDtypeStruct((samples, heads, 2, dim), f32),
         ],
         scratch_shapes=[
             pltpu.VMEM((rows, width), bf16),
-            pltpu.VMEM((samples, dim, width), bf16),
-            pltpu.VMEM((samples, dim, width), bf16),
-            pltpu.VMEM((model // columns, rows, columns), bf16),
-            pltpu.SemaphoreType.DMA((model // columns,)),
+            pltpu.VMEM((samples, model // columns, tokens, columns), bf16),
+            pltpu.VMEM((samples, heads, 2, dim), f32),
+            pltpu.SemaphoreType.DMA((samples, model // columns)),
+            pltpu.SemaphoreType.DMA((1,)),
         ],
         compiler_params=params(24),
         name="finish",
-    )(returned, back, merged, logs, center_rows, refresh, value_rows, w_out)
+    )(returned, back, merged, logs, old, basis_high, basis_low, w_out)
     return (mixed.reshape(samples, tokens, model), new_centers.transpose(0, 2, 1, 3))
 
 

time: 33.9 us -> 30.5 us (0.90)
  Pallas kernels: 18.3 us -> 15.9 us
  starting transfers between devices: 11.2 us -> 10.7 us
  waiting for transfers between devices: 3.49 us -> 3.03 us
    pallas_call x1, Pallas kernels: 7.15 us -> 5.38 us  [per_device(): pl.pallas_call(functools.partial(project_kernel, **sizes, rank=rank, log_...]
    pallas_call x1, Pallas kernels: 3.85 us -> 2.61 us  [per_device(): pl.pallas_call(functools.partial(finish_kernel, **sizes, rank=rank, lengt...]
    pallas_call x1, Pallas kernels: 2.21 us -> 2.79 us  [per_device(): pl.pallas_call(functools.partial(near_kernel, **sizes, rank=rank), in_spe...]
    ppermute x9, waiting for transfers between devices: 3.49 us -> 3.03 us  [swap(): return lax.ppermute(x, 'seq', [(i, i ^ mask) for i in range(seq)])]
    ppermute x9, starting transfers between devices: 11.2 us -> 10.7 us  [swap(): return lax.ppermute(x, 'seq', [(i, i ^ mask) for i in range(seq)])]
  transfers between devices with their start and end apart: 9 -> 9, of which waited for: 4 -> 4; matrix products, arithmetic and copies ran while one was open for 0% -> 0% of each run, Pallas kernels for 15% -> 18%
where the time goes in v4:
time: 30.5 us; the launch traced here: 30.4 us
  Pallas kernels  15.9 us (52%)
  starting transfers between devices  10.7 us (35%)
  waiting for transfers between devices  3.03 us (10%)
  between operations  0.72 us (2%)
    ppermute x9, starting transfers between devices, swap(): return lax.ppermute(x, 'seq', [(i, i ^ mask) for i in range(seq)])  10.7 us
    pallas_call x1, Pallas kernels, per_device(): pl.pallas_call(functools.partial(project_kernel, **sizes, rank=rank, log_...  5.38 us
    ppermute x9, waiting for transfers between devices, swap(): return lax.ppermute(x, 'seq', [(i, i ^ mask) for i in range(seq)])  3.03 us
    pallas_call x1, Pallas kernels, per_device(): pl.pallas_call(functools.partial(own_kernel, **sizes, rank=rank), in_spec...  2.81 us
    pallas_call x1, Pallas kernels, per_device(): pl.pallas_call(functools.partial(near_kernel, **sizes, rank=rank), in_spe...  2.79 us
    pallas_call x1, Pallas kernels, per_device(): pl.pallas_call(functools.partial(finish_kernel, **sizes, rank=rank, lengt...  2.61 us
    pallas_call x1, Pallas kernels, per_device(): pl.pallas_call(functools.partial(partner_kernel, **sizes, rank=rank, orde...  2.27 us
  transfers between devices with their start and end apart: 9, of which 4 were waited for; matrix products, arithmetic and copies ran while one was open for 0% of the time, Pallas kernels for 18%

profile of v4, /device:TPU:0, one launch (start us, length us, event | category | flops | bytes accessed | tf_op | source)
XLA Modules:
  0.0 30.4 jit_solution(9141025339189390620)
XLA Ops:
  0.6 0.0 copy-start.1
  0.6 0.0 copy-start.2
  0.7 0.0 copy-start.3
  0.7 5.4 %project.1 = (bf16[1,144,384]{2,1,0:T(8,128)(2,1)S(1)}, bf16[128,384]{1,0:T(8,128)(2,1)S(1)}, f32[256,1152]{1,0:T(8,128)S(1)}) custom-call(bf16[256,3072]{1,0:T(8,128)(2,1)} %bitcast.13, bf16[3072,1152]{1,0:T(8,128)(2,1)} %w_hbm.1, f32[9,128]{1,0:T(8,128)} %bitcast.15, f32[1,128]{1,0:T(1,128)} %bitcast.16, f32[1,128]{1,0:T(1,128)} %bitcast.17, ...), custom_call_target="tpu_custom_call" | custom-call | tf_op jit(solution)/shard_map/project/pallas_call | solution.py:421
  6.1 0.5 %collective-permute-start.4 = (bf16[1,144,384]{2,1,0:T(8,128)(2,1)S(1)}, bf16[1,144,384]{2,1,0:T(8,128)(2,1)S(1)}, u32[]{:S(2)}, u32[]{:S(2)}) collective-permute-start(bf16[1,144,384]{2,1,0:T(8,128)(2,1)S(1)} %get-tuple-element.18.refs_0_), channel_id=1, source_target_pairs={{0,1},{1,0},{2,3},{3,2},{4,5},{5,4},{6,7},{7,6},{8,9},{9,8},{10,11... | collective-permute-start | bytes 331784 | tf_op jit(solution)/shard_map/ppermute | solution.py:459
  6.6 3.6 %collective-permute-start.3 = (bf16[1,144,384]{2,1,0:T(8,128)(2,1)S(1)}, bf16[1,144,384]{2,1,0:T(8,128)(2,1)S(1)}, u32[]{:S(2)}, u32[]{:S(2)}) collective-permute-start(bf16[1,144,384]{2,1,0:T(8,128)(2,1)S(1)} %get-tuple-element.18.refs_0_), channel_id=1, source_target_pairs={{0,6},{1,7},{2,4},{3,5},{4,2},{5,3},{6,0},{7,1},{8,14},{9,15},{10,... | collective-permute-start | bytes 331784 | tf_op jit(solution)/shard_map/ppermute | solution.py:459
  10.2 0.4 %collective-permute-start.2 = (bf16[1,144,384]{2,1,0:T(8,128)(2,1)S(1)}, bf16[1,144,384]{2,1,0:T(8,128)(2,1)S(1)}, u32[]{:S(2)}, u32[]{:S(2)}) collective-permute-start(bf16[1,144,384]{2,1,0:T(8,128)(2,1)S(1)} %get-tuple-element.18.refs_0_), channel_id=1, source_target_pairs={{0,4},{1,5},{2,6},{3,7},{4,0},{5,1},{6,2},{7,3},{8,12},{9,13},{10,... | collective-permute-start | bytes 331784 | tf_op jit(solution)/shard_map/ppermute | solution.py:459
  10.6 0.2 collective-permute-start.1
  10.8 2.9 %collective-permute-start = (bf16[128,384]{1,0:T(8,128)(2,1)S(1)}, bf16[128,384]{1,0:T(8,128)(2,1)S(1)}, u32[]{:S(2)}, u32[]{:S(2)}) collective-permute-start(bf16[128,384]{1,0:T(8,128)(2,1)S(1)} %get-tuple-element.17.query_ref), channel_id=1, source_target_pairs={{0,8},{1,9},{2,10},{3,11},{4,12},{5,13},{6,14},{7,15},{8,0},{9,1},... | collective-permute-start | bytes 294920 | tf_op jit(solution)/shard_map/ppermute | solution.py:459
  13.7 0.0 copy-done.1
  13.7 0.0 copy-done.2
  13.7 0.0 copy-done.3
  13.7 2.8 %near.1 = (f32[256,384]{1,0:T(8,128)S(1)}, f32[256,128]{1,0:T(8,128)S(1)}, bf16[2,128,384]{2,1,0:T(8,128)(2,1)S(1)}, bf16[2,128,384]{2,1,0:T(8,128)(2,1)S(1)}, f32[32,128]{1,0:T(8,128)S(1)}) custom-call(f32[256,1152]{1,0:T(8,128)S(1)} %get-tuple-element.19.qkv_ref, f32[2,3,2,128]{3,2,1,0:T(2,128)S(1)} %bitcast.12, s32[2,3]{1,0:T(2,128)S(1)} %copy-done.3, ...), custom_call_target="tpu_custom_call" | custom-call | flops 15099494400 | bytes 19660800 | tf_op jit(solution)/shard_map/near/pallas_call | solution.py:475
  16.5 0.0 collective-permute-done.3.refs_3_.refs_2_
  16.5 0.1 collective-permute-start.7
  16.6 1.9 %collective-permute-done.2.refs_2_.refs_1_ = bf16[1,144,384]{2,1,0:T(8,128)(2,1)S(1)} collective-permute-done((bf16[1,144,384]{2,1,0:T(8,128)(2,1)S(1)}, bf16[1,144,384]{2,1,0:T(8,128)(2,1)S(1)}, u32[]{:S(2)}, u32[]{:S(2)}) %collective-permute-start.2) | collective-permute-done | bytes 110624 | tf_op jit(solution)/shard_map/ppermute | solution.py:459
  18.5 0.0 collective-permute-start.6
  18.5 0.0 collective-permute-done.query_ref
  18.5 0.0 collective-permute-done.1.refs_1_.refs_0_
  18.5 0.5 %collective-permute-start.5 = (bf16[1,144,384]{2,1,0:T(8,128)(2,1)S(1)}, bf16[1,144,384]{2,1,0:T(8,128)(2,1)S(1)}, u32[]{:S(2)}, u32[]{:S(2)}) collective-permute-start(bf16[1,144,384]{2,1,0:T(8,128)(2,1)S(1)} %collective-permute-done.1.refs_1_.refs_0_), channel_id=1, source_target_pairs={{0,1},{1,0},{2,3},{3,2},{4,5},{5,4},{6,7},{7,6},{8,9},{9,8},{10,11... | collective-permute-start | bytes 331784 | tf_op jit(solution)/shard_map/ppermute | solution.py:459
  19.0 0.0 collective-permute-done.4.refs_4_.refs_3_
  19.0 0.0 collective-permute-done.7.refs_7_.refs_6_
  19.0 0.8 %collective-permute-done.6.refs_6_.refs_5_ = bf16[1,144,384]{2,1,0:T(8,128)(2,1)S(1)} collective-permute-done((bf16[1,144,384]{2,1,0:T(8,128)(2,1)S(1)}, bf16[1,144,384]{2,1,0:T(8,128)(2,1)S(1)}, u32[]{:S(2)}, u32[]{:S(2)}) %collective-permute-start.6) | collective-permute-done | bytes 110624 | tf_op jit(solution)/shard_map/ppermute | solution.py:459
  19.8 0.2 collective-permute-done.5.refs_5_.refs_4_
  20.0 2.3 %partner.1.half_ref = bf16[288,128]{1,0:T(8,128)(2,1)S(1)} custom-call(bf16[128,384]{1,0:T(8,128)(2,1)S(1)} %collective-permute-done.query_ref, bf16[1,144,384]{2,1,0:T(8,128)(2,1)S(1)} %get-tuple-element.18.refs_0_, bf16[1,144,384]{2,1,0:T(8,128)(2,1)S(1)} %collective-permute-done.1.refs_1_.refs_0_, ...), custom_call_target="tpu_custom_call" | custom-call | flops 805306368 | bytes 786432 | tf_op jit(solution)/shard_map/partner/pallas_call | solution.py:505
  22.2 0.0 copy-start
  22.3 2.5 %collective-permute-start.8 = (bf16[288,128]{1,0:T(8,128)(2,1)S(1)}, bf16[288,128]{1,0:T(8,128)(2,1)S(1)}, u32[]{:S(2)}, u32[]{:S(2)}) collective-permute-start(bf16[288,128]{1,0:T(8,128)(2,1)S(1)} %partner.1.half_ref), channel_id=1, source_target_pairs={{0,8},{1,9},{2,10},{3,11},{4,12},{5,13},{6,14},{7,15},{8,0},{9,1},... | collective-permute-start | bytes 221192 | tf_op jit(solution)/shard_map/ppermute | solution.py:459
  24.7 2.8 %own.1 = (f32[256,384]{1,0:T(8,128)S(1)}, f32[256,128]{1,0:T(8,128)S(1)}) custom-call(bf16[128,384]{1,0:T(8,128)(2,1)S(1)} %get-tuple-element.17.query_ref, f32[256,384]{1,0:T(8,128)S(1)} %get-tuple-element.24.near_ref, f32[256,128]{1,0:T(8,128)S(1)} %get-tuple-element.20.refs_8_.stat_ref, f32[32,128]{1,0:T(8,128)S(1)} %get-tuple-element.25.old_ref, ...), custom_call_target="tpu_custom_call" | custom-call | flops 805306368 | bytes 786432 | tf_op jit(solution)/shard_map/own/pallas_call | solution.py:515
  27.6 0.2 collective-permute-done.8.back_ref
  27.8 0.0 copy-done
  27.8 2.6 %finish.1 = (bf16[256,3072]{1,0:T(8,128)(2,1)}, f32[2,3,2,128]{3,2,1,0:T(2,128)}) custom-call(bf16[288,128]{1,0:T(8,128)(2,1)S(1)} %collective-permute-done.8.back_ref, bf16[288,128]{1,0:T(8,128)(2,1)S(1)} %partner.1.half_ref, f32[256,384]{1,0:T(8,128)S(1)} %get-tuple-element.28.merged_ref, f32[256,128]{1,0:T(8,128)S(1)} %get-tuple-element.29.log_ref, ...), custom_call_target="tpu_custom_call" | custom-call | tf_op jit(solution)/shard_map/finish/pallas_call | solution.py:529
Async XLA Ops:
  0.6 13.1 %copy-start.1 = (f32[3,128,32]{1,2,0:T(8,128)S(1)}, f32[3,128,32]{1,2,0:T(8,128)}, u32[]{:S(2)}) copy-start(f32[3,128,32]{1,2,0:T(8,128)} %param.16) | copy-start | bytes 147460
  0.6 13.1 %copy-start.2 = (f32[2,2,3,128]{3,1,2,0:T(2,128)S(1)}, f32[2,2,3,128]{3,1,2,0:T(2,128)}, u32[]{:S(2)}) copy-start(f32[2,2,3,128]{3,1,2,0:T(2,128)} %param.17) | copy-start | bytes 18436
  0.7 13.1 %copy-start.3 = (s32[2,3]{1,0:T(2,128)S(1)}, s32[2,3]{1,0:T(2,128)}, u32[]{:S(2)}) copy-start(s32[2,3]{1,0:T(2,128)} %refresh_ref.1) | copy-start | bytes 76
  6.1 13.0 %collective-permute-start.4 = (bf16[1,144,384]{2,1,0:T(8,128)(2,1)S(1)}, bf16[1,144,384]{2,1,0:T(8,128)(2,1)S(1)}, u32[]{:S(2)}, u32[]{:S(2)}) collective-permute-start(bf16[1,144,384]{2,1,0:T(8,128)(2,1)S(1)} %get-tuple-element.18.refs_0_), channel_id=1, source_target_pairs={{0,1},{1,0},{2,3},{3,2},{4,5},{5,4},{6,7},{7,6},{8,9},{9,8},{10,11... | collective-permute-start | bytes 331784 | tf_op jit(solution)/shard_map/ppermute | solution.py:459
  6.6 10.0 %collective-permute-start.3 = (bf16[1,144,384]{2,1,0:T(8,128)(2,1)S(1)}, bf16[1,144,384]{2,1,0:T(8,128)(2,1)S(1)}, u32[]{:S(2)}, u32[]{:S(2)}) collective-permute-start(bf16[1,144,384]{2,1,0:T(8,128)(2,1)S(1)} %get-tuple-element.18.refs_0_), channel_id=1, source_target_pairs={{0,6},{1,7},{2,4},{3,5},{4,2},{5,3},{6,0},{7,1},{8,14},{9,15},{10,... | collective-permute-start | bytes 331784 | tf_op jit(solution)/shard_map/ppermute | solution.py:459
  10.2 8.3 %collective-permute-start.2 = (bf16[1,144,384]{2,1,0:T(8,128)(2,1)S(1)}, bf16[1,144,384]{2,1,0:T(8,128)(2,1)S(1)}, u32[]{:S(2)}, u32[]{:S(2)}) collective-permute-start(bf16[1,144,384]{2,1,0:T(8,128)(2,1)S(1)} %get-tuple-element.18.refs_0_), channel_id=1, source_target_pairs={{0,4},{1,5},{2,6},{3,7},{4,0},{5,1},{6,2},{7,3},{8,12},{9,13},{10,... | collective-permute-start | bytes 331784 | tf_op jit(solution)/shard_map/ppermute | solution.py:459
  10.6 7.9 %collective-permute-start.1 = (bf16[1,144,384]{2,1,0:T(8,128)(2,1)S(1)}, bf16[1,144,384]{2,1,0:T(8,128)(2,1)S(1)}, u32[]{:S(2)}, u32[]{:S(2)}) collective-permute-start(bf16[1,144,384]{2,1,0:T(8,128)(2,1)S(1)} %get-tuple-element.18.refs_0_), channel_id=1, source_target_pairs={{0,2},{1,3},{2,0},{3,1},{4,6},{5,7},{6,4},{7,5},{8,10},{9,11},{10,... | collective-permute-start | bytes 331784 | tf_op jit(solution)/shard_map/ppermute | solution.py:459
  10.8 7.7 %collective-permute-start = (bf16[128,384]{1,0:T(8,128)(2,1)S(1)}, bf16[128,384]{1,0:T(8,128)(2,1)S(1)}, u32[]{:S(2)}, u32[]{:S(2)}) collective-permute-start(bf16[128,384]{1,0:T(8,128)(2,1)S(1)} %get-tuple-element.17.query_ref), channel_id=1, source_target_pairs={{0,8},{1,9},{2,10},{3,11},{4,12},{5,13},{6,14},{7,15},{8,0},{9,1},... | collective-permute-start | bytes 294920 | tf_op jit(solution)/shard_map/ppermute | solution.py:459
  16.5 2.5 %collective-permute-start.7 = (bf16[1,144,384]{2,1,0:T(8,128)(2,1)S(1)}, bf16[1,144,384]{2,1,0:T(8,128)(2,1)S(1)}, u32[]{:S(2)}, u32[]{:S(2)}) collective-permute-start(bf16[1,144,384]{2,1,0:T(8,128)(2,1)S(1)} %collective-permute-done.3.refs_3_.refs_2_), channel_id=1, source_target_pairs={{0,1},{1,0},{2,3},{3,2},{4,5},{5,4},{6,7},{7,6},{8,9},{9,8},{10,11... | collective-permute-start | bytes 331784 | tf_op jit(solution)/shard_map/ppermute | solution.py:459
  18.5 1.3 %collective-permute-start.6 = (bf16[1,144,384]{2,1,0:T(8,128)(2,1)S(1)}, bf16[1,144,384]{2,1,0:T(8,128)(2,1)S(1)}, u32[]{:S(2)}, u32[]{:S(2)}) collective-permute-start(bf16[1,144,384]{2,1,0:T(8,128)(2,1)S(1)} %collective-permute-done.2.refs_2_.refs_1_), channel_id=1, source_target_pairs={{0,1},{1,0},{2,3},{3,2},{4,5},{5,4},{6,7},{7,6},{8,9},{9,8},{10,11... | collective-permute-start | bytes 331784 | tf_op jit(solution)/shard_map/ppermute | solution.py:459
  18.5 1.5 %collective-permute-start.5 = (bf16[1,144,384]{2,1,0:T(8,128)(2,1)S(1)}, bf16[1,144,384]{2,1,0:T(8,128)(2,1)S(1)}, u32[]{:S(2)}, u32[]{:S(2)}) collective-permute-start(bf16[1,144,384]{2,1,0:T(8,128)(2,1)S(1)} %collective-permute-done.1.refs_1_.refs_0_), channel_id=1, source_target_pairs={{0,1},{1,0},{2,3},{3,2},{4,5},{5,4},{6,7},{7,6},{8,9},{9,8},{10,11... | collective-permute-start | bytes 331784 | tf_op jit(solution)/shard_map/ppermute | solution.py:459
  22.2 5.5 %copy-start = (bf16[384,3072]{1,0:T(8,128)(2,1)S(1)}, bf16[384,3072]{1,0:T(8,128)(2,1)}, u32[]{:S(2)}) copy-start(bf16[384,3072]{1,0:T(8,128)(2,1)} %w_ref.1) | copy-start | bytes 7077892
  22.3 5.5 %collective-permute-start.8 = (bf16[288,128]{1,0:T(8,128)(2,1)S(1)}, bf16[288,128]{1,0:T(8,128)(2,1)S(1)}, u32[]{:S(2)}, u32[]{:S(2)}) collective-permute-start(bf16[288,128]{1,0:T(8,128)(2,1)S(1)} %partner.1.half_ref), channel_id=1, source_target_pairs={{0,8},{1,9},{2,10},{3,11},{4,12},{5,13},{6,14},{7,15},{8,0},{9,1},... | collective-permute-start | bytes 221192 | tf_op jit(solution)/shard_map/ppermute | solution.py:459

commit v5 on v4

--- a/solution.py
+++ b/solution.py
@@ -56,6 +56,14 @@
 
 def free_lane(sample, rank):
     return 2 * rank if sample == 0 else rank
+
+
+def log_lane(sample, head, piece, rank):
+    return free_lane(sample, rank) + 8 * piece + head
+
+
+def sum_lane(sample, rank):
+    return free_lane(sample, rank) + 20
 
 
 def within(lanes, start, count):
@@ -78,18 +86,18 @@
     payload_ref, query_ref, qkv_ref,
     x_ref, w_ref, b_ref, qg_ref, kg_ref, kb_ref, vb_ref, centers_ref,
     acc_ref, main_ref, tail_ref, sums_ref, big_sem, small_sem,
-    *, samples, tokens, heads, dim, rank, log_factor,
+    *, samples, tokens, heads, dim, rank, log_factor, cuts,
 ):
-    chunks, _, depth = x_ref.shape
     width = heads * dim
+    places = [slice(first, last) for first, last in zip(cuts[:-1], cuts[1:])]
 
     def x_copy(c):
-        columns = pl.ds(pl.multiple_of(c * depth, depth), depth)
-        return pltpu.make_async_copy(images_hbm.at[:, columns], x_ref.at[c], big_sem.at[0, c])
+        p = places[c]
+        return pltpu.make_async_copy(images_hbm.at[:, p], x_ref.at[:, p], big_sem.at[0, c])
 
     def w_copy(c):
-        some = pl.ds(pl.multiple_of(c * depth, depth), depth)
-        return pltpu.make_async_copy(w_hbm.at[some, :], w_ref.at[c], big_sem.at[1, c])
+        p = places[c]
+        return pltpu.make_async_copy(w_hbm.at[p, :], w_ref.at[p, :], big_sem.at[1, c])
 
     small = [
         pltpu.make_async_copy(source, target, small_sem.at[i])
@@ -100,36 +108,41 @@
             ]
         )
     ]
-    for c in range(chunks):
+    for copy in small:
+        copy.start()
+    for c in range(len(places)):
         x_copy(c).start()
         w_copy(c).start()
-    for copy in small:
-        copy.start()
     main_ref[...] = jnp.zeros_like(main_ref)
     tail_ref[...] = jnp.zeros_like(tail_ref)
     sums_ref[...] = jnp.zeros_like(sums_ref)
-    for c in range(chunks):
+    half = dim // 2
+
+    def build():
+        for copy in small:
+            copy.wait()
+        for h in range(heads):
+            for p, (k, v) in enumerate(zip(split(kb_ref[h]), split(vb_ref[h]))):
+                at = p * dim + key_lane(0, h, rank)
+                main_ref[at : at + rank, h * dim : (h + 1) * dim] = k
+                at = value_lane(0, h, rank, heads)
+                if h == 0:
+                    main_ref[p * dim + at : p * dim + at + rank, width:] = v
+                else:
+                    at = p * half + at
+                    tail_ref[at : at + rank, (h - 1) * dim : h * dim] = v
+
+    for c, place in enumerate(places):
+        if c == len(places) - 1:
+            build()
         x_copy(c).wait()
         w_copy(c).wait()
-        part = dot(x_ref[c], w_ref[c])
+        part = dot(x_ref[:, place], w_ref[place, :])
         if c == 0:
             acc_ref[...] = part
         else:
             acc_ref[...] += part
 
-    for copy in small:
-        copy.wait()
-    half = dim // 2
-    for h in range(heads):
-        for p, (k, v) in enumerate(zip(split(kb_ref[h]), split(vb_ref[h]))):
-            at = p * dim + key_lane(0, h, rank)
-            main_ref[at : at + rank, h * dim : (h + 1) * dim] = k
-            at = value_lane(0, h, rank, heads)
-            if h == 0:
-                main_ref[p * dim + at : p * dim + at + rank, width:] = v
-            else:
-                at = p * half + at
-                tail_ref[at : at + rank, (h - 1) * dim : h * dim] = v
     def column(at):
         return acc_ref[:, at * dim : (at + 1) * dim] + b_ref[at : at + 1, :]
 
@@ -247,11 +260,15 @@
         both = [jnp.where(own, part, 0.0).astype(bf16) for part in (high, low)]
         stacked.append(jnp.concatenate(both, axis=1))
     left = jnp.concatenate(stacked, axis=0)
-    scores, values = [], []
+    scores, values, codes = [], [], []
     for ref, i in tiles:
         code = ref[i, :tokens, b * dim : (b + 1) * dim]
-        scores.append(dot(left, jnp.concatenate([code, code], axis=1), NT))
+        codes.append(jnp.concatenate([code, code], axis=1))
         values.append(jnp.concatenate([code, ref[i, :tokens, samples * dim :]], axis=1))
+    for i in range(0, len(codes), 2):
+        some = codes[i : i + 2]
+        both = dot(left, jnp.concatenate(some, axis=0), NT)
+        scores += [both[:, j * tokens : (j + 1) * tokens] for j in range(len(some))]
     best = scores[0]
     for part in scores[1:]:
         best = jnp.maximum(best, part)
@@ -286,8 +303,26 @@
     return [(ref, i) for ref in refs for i in range(ref.shape[0])]
 
 
-def partner_kernel(query_ref, *refs, order, samples, tokens, heads, dim, rank):
-    out_ref = refs[-1]
+def early_kernel(query_ref, *refs, samples, tokens, heads, dim, rank):
+    out_ref, log_ref = refs[-2:]
+    tiles = tiles_of(refs[:-2])
+    lanes = lane_ids(tokens, dim)
+    for b in range(samples):
+        rows = slice(b * tokens, (b + 1) * tokens)
+        out, logs = code_attention(
+            query_ref, tiles, b, samples=samples, tokens=tokens, heads=heads, dim=dim, rank=rank
+        )
+        kept = jnp.zeros((tokens, dim), f32)
+        for h in range(heads):
+            kept = jnp.where(lanes == h, logs[h], kept)
+        out_ref[rows, :] = out
+        log_ref[rows, :] = kept
+
+
+def partner_kernel(
+    query_ref, part_ref, part_log_ref, *refs, order, late, samples, tokens, heads, dim, rank
+):
+    out_ref, half_ref = refs[-2:]
     tiles = tiles_of(refs[:-2])
     parts = []
     for place in order:
@@ -295,18 +330,33 @@
         rows = slice(tokens, tokens + SUM_ROWS)
         pieces = [ref[i, rows, p * dim : (p + 1) * dim].astype(f32) for p in range(3)]
         parts.append(pieces[0] + (pieces[1] + pieces[2]))
-    first = samples * tokens
-    for p, piece in enumerate(pieces_of(tree_sum(parts), 2)):
-        out_ref[first + p * SUM_ROWS : first + (p + 1) * SUM_ROWS, :] = piece
+    pieces = [piece.astype(f32) for piece in pieces_of(tree_sum(parts), 2)]
+    half_ref[...] = pieces[0] + pieces[1]
+    empty = jnp.zeros((tokens - SUM_ROWS, dim), f32)
+    turned = [jnp.concatenate([piece, empty], axis=0).T for piece in pieces]
     lanes = lane_ids(tokens, dim)
     for b in range(samples):
+        rows = slice(b * tokens, (b + 1) * tokens)
         out, logs = code_attention(
-            query_ref, tiles, b, samples=samples, tokens=tokens, heads=heads, dim=dim, rank=rank
+            query_ref, tiles[-late:], b,
+            samples=samples, tokens=tokens, heads=heads, dim=dim, rank=rank,
         )
+        before, before_logs = part_ref[rows, :], part_log_ref[rows, :]
+        scale = jnp.zeros((tokens, dim), f32)
+        for h in range(heads):
+            before_log = before_logs[:, h : h + 1]
+            top = jnp.maximum(logs[h], before_log)
+            new, old = jnp.exp2(logs[h] - top), jnp.exp2(before_log - top)
+            whole = new + old
+            scale = jnp.where(within(lanes, value_lane(b, h, rank, heads), rank), new / whole, scale)
+            logs[h] = top + jnp.log(whole) * log2_e
+        out = before + (out - before) * scale
         for h in range(heads):
             for p, piece in enumerate(pieces_of(logs[h], 3)):
-                out = jnp.where(lanes == free_lane(b, rank) + 3 * h + p, piece.astype(f32), out)
-        out_ref[b * tokens : (b + 1) * tokens, :] = out.astype(bf16)
+                out = jnp.where(lanes == log_lane(b, h, p, rank), piece.astype(f32), out)
+        at = sum_lane(b, rank)
+        out = jnp.where(within(lanes, at, 2 * samples * heads), pltpu.roll(turned[b], at, 1), out)
+        out_ref[rows, :] = out.astype(bf16)
 
 
 def own_kernel(
@@ -336,8 +386,8 @@
             row = (b * heads + h) * 2 + 1
             merged = merged + (far[:, columns] + old_ref[row : row + 1, :]) * (far_part / whole)
             merged_ref[rows, columns] = merged
-            kept = jnp.where(lanes == h, top + jnp.log(whole) * log2_e, kept)
-            kept = jnp.where(lanes == heads + h, center, kept)
+            log = top + jnp.log(whole) * log2_e - center
+            kept = jnp.where(lanes == log_lane(b, h, 0, rank), log, kept)
         log_ref[rows, :] = kept
 
 
@@ -346,43 +396,24 @@
     mixed_hbm, new_hbm, attended_ref, mixed_ref, new_ref, sem, new_sem,
     *, samples, tokens, heads, dim, rank, length,
 ):
-    first = samples * tokens
-    sums = [
-        ref[first : first + SUM_ROWS, :].astype(f32)
-        + ref[first + SUM_ROWS : first + 2 * SUM_ROWS, :].astype(f32)
-        for ref in (half_ref, back_ref)
-    ]
-    fresh = (sums[0] + sums[1]) * (1.0 / length)
-    fresh = jnp.where(old_ref[SUM_ROWS:, :] > 0.5, old_ref[:SUM_ROWS, :], fresh)
-    for b in range(samples):
-        for h in range(heads):
-            row = (b * heads + h) * 2
-            new_ref[b, h] = fresh[row : row + 2, :]
-    new_copy = pltpu.make_async_copy(new_ref, new_hbm, new_sem.at[0])
-    new_copy.start()
     chunks, columns = mixed_ref.shape[1], mixed_ref.shape[3]
     copies = []
+    sums = jnp.zeros((tokens, dim), f32)
     for b in range(samples):
         rows = slice(b * tokens, (b + 1) * tokens)
         codes = back_ref[rows, :]
+        extra = codes.astype(f32)
+        sums = sums + pltpu.roll(extra, dim - sum_lane(b, rank), 1)
+        far_log = extra + (pltpu.roll(extra, dim - 8, 1) + pltpu.roll(extra, dim - 16, 1))
+        share = 1.0 / (1.0 + jnp.exp2(log_ref[rows, :] - far_log))
         far = dot(codes, basis_h[b]) + dot(codes, basis_l[b])
-        extra = codes.astype(f32)
-        logs = log_ref[rows, :]
         for h in range(heads):
             head = slice(h * dim, (h + 1) * dim)
-            spot = free_lane(b, rank) + 3 * h
-            far_log = extra[:, spot : spot + 1] + (
-                extra[:, spot + 1 : spot + 2] + extra[:, spot + 2 : spot + 3]
-            )
-            far_log = far_log + logs[:, heads + h : heads + h + 1]
-            own_log = logs[:, h : h + 1]
-            top = jnp.maximum(own_log, far_log)
-            own_part, far_part = jnp.exp2(own_log - top), jnp.exp2(far_log - top)
-            whole = own_part + far_part
+            at = log_lane(b, h, 0, rank)
             row = (b * heads + h) * 2 + 1
-            value = merged_ref[rows, head] * (own_part / whole)
-            value = value + (far[:, head] + old_ref[row : row + 1, :]) * (far_part / whole)
-            attended_ref[rows, head] = value.astype(bf16)
+            near = merged_ref[rows, head]
+            value = far[:, head] + old_ref[row : row + 1, :] - near
+            attended_ref[rows, head] = (near + value * share[:, at : at + 1]).astype(bf16)
         for c in range(chunks):
             place = slice(c * columns, (c + 1) * columns)
             mixed_ref[b, c] = dot(attended_ref[rows, :], w_ref[:, place]).astype(bf16)
@@ -391,7 +422,15 @@
             )
             copy.start()
             copies.append(copy)
-    for copy in copies + [new_copy]:
+    fresh = (half_ref[...] + sums.T[:SUM_ROWS, :]) * (1.0 / length)
+    fresh = jnp.where(old_ref[SUM_ROWS:, :] > 0.5, old_ref[:SUM_ROWS, :], fresh)
+    for b in range(samples):
+        for h in range(heads):
+            row = (b * heads + h) * 2
+            new_ref[b, h] = fresh[row : row + 2, :]
+    copies.append(pltpu.make_async_copy(new_ref, new_hbm, new_sem.at[0]))
+    copies[-1].start()
+    for copy in copies:
         copy.wait()
 
 
@@ -413,13 +452,12 @@
     key_rows = key_basis.transpose(0, 2, 1)
     value_rows = value_basis.transpose(0, 2, 1)
     center_rows = centers.transpose(0, 2, 1, 3)
-    chunks = 3
-    depth = model // chunks
+    cuts = tuple(model * i // 3 for i in range(4))
     shard = (1, tokens + SUM_ROWS, width)
     params = lambda mib: pltpu.CompilerParams(vmem_limit_bytes=mib * 2**20)
 
     payload, query, qkv = pl.pallas_call(
-        functools.partial(project_kernel, **sizes, rank=rank, log_factor=log_factor),
+        functools.partial(project_kernel, **sizes, rank=rank, log_factor=log_factor, cuts=cuts),
         in_specs=[HBM] * 8,
         out_specs=[VMEM] * 3,
         out_shape=[
@@ -428,8 +466,8 @@
             jax.ShapeDtypeStruct((rows, 3 * width), f32),
         ],
         scratch_shapes=[
-            pltpu.VMEM((chunks, rows, depth), bf16),
-            pltpu.VMEM((chunks, depth, 3 * width), bf16),
+            pltpu.VMEM((rows, model), bf16),
+            pltpu.VMEM((model, 3 * width), bf16),
             pltpu.VMEM((3 * heads, dim), f32),
             pltpu.VMEM((1, dim), f32),
             pltpu.VMEM((1, dim), f32),
@@ -440,7 +478,7 @@
             pltpu.VMEM((2 * dim, width + dim), bf16),
             pltpu.VMEM((dim, width - dim), bf16),
             pltpu.VMEM((SUM_ROWS, dim), f32),
-            pltpu.SemaphoreType.DMA((2, chunks)),
+            pltpu.SemaphoreType.DMA((2, len(cuts) - 1)),
             pltpu.SemaphoreType.DMA((6,)),
         ],
         compiler_params=params(32),
@@ -491,26 +529,46 @@
     )(qkv, center_rows, refresh, value_rows)
 
     for i in range(1, len(held)):
-        x, _, _ = lax.optimization_barrier((held[i][0], stats, query_far if i == 1 else stats))
+        x, _ = lax.optimization_barrier((held[i][0], stats))
         held[i] = (x, held[i][1])
-    held += [(swap(a, 1), [m ^ 1 for m in ms]) for a, ms in held]
+    held.insert(1, (swap(payload, 1), [1]))
+    early = [a for a, _ in held]
+    held += [(swap(a, 1), [m ^ 1 for m in ms]) for a, ms in held[2:]]
     arrays = [a for a, _ in held]
     names = [m for _, ms in held for m in ms]
     order = tuple(names.index(m) for m in range(len(names)))
-    cost = pl.CostEstimate(
-        flops=8 * rows * tokens * len(names) * width,
-        bytes_accessed=len(names) * 2 * tokens * width,
-        transcendentals=0,
-    )
-    back = pl.pallas_call(
-        functools.partial(partner_kernel, **sizes, rank=rank, order=order),
-        in_specs=[VMEM] * (1 + len(arrays)) + [pl.BlockSpec(memory_space=pl.ANY)],
-        out_specs=VMEM,
-        out_shape=jax.ShapeDtypeStruct((rows + 2 * SUM_ROWS, dim), bf16),
+    count_early = sum(a.shape[0] for a in early)
+
+    def cost(shards):
+        return pl.CostEstimate(
+            flops=8 * rows * tokens * shards * width,
+            bytes_accessed=shards * 2 * tokens * width,
+            transcendentals=0,
+        )
+
+    part, part_log = pl.pallas_call(
+        functools.partial(early_kernel, **sizes, rank=rank),
+        in_specs=[VMEM] * (1 + len(early)),
+        out_specs=[VMEM] * 2,
+        out_shape=[jax.ShapeDtypeStruct((rows, dim), f32)] * 2,
         compiler_params=params(32),
-        cost_estimate=cost,
+        cost_estimate=cost(count_early),
+        name="early",
+    )(query_far, *early)
+    back, half = pl.pallas_call(
+        functools.partial(
+            partner_kernel, **sizes, rank=rank, order=order, late=len(names) - count_early
+        ),
+        in_specs=[VMEM] * (3 + len(arrays)),
+        out_specs=[VMEM] * 2,
+        out_shape=[
+            jax.ShapeDtypeStruct((rows, dim), bf16),
+            jax.ShapeDtypeStruct((SUM_ROWS, dim), f32),
+        ],
+        compiler_params=params(32),
+        cost_estimate=cost(len(names)),
         name="partner",
-    )(query_far, *arrays, stats)
+    )(query_far, part, part_log, *arrays)
     returned = swap(back, far_mask)
     merged, logs = pl.pallas_call(
         functools.partial(own_kernel, **sizes, rank=rank),
@@ -521,7 +579,7 @@
             jax.ShapeDtypeStruct((rows, dim), f32),
         ],
         compiler_params=params(32),
-        cost_estimate=cost,
+        cost_estimate=cost(len(names)),
         name="own",
     )(query, near, stats, old, basis_high, basis_low, *arrays[1:])
 
@@ -543,7 +601,7 @@
         ],
         compiler_params=params(24),
         name="finish",
-    )(returned, back, merged, logs, old, basis_high, basis_low, w_out)
+    )(returned, half, merged, logs, old, basis_high, basis_low, w_out)
     return (mixed.reshape(samples, tokens, model), new_centers.transpose(0, 2, 1, 3))
 
 

time: 30.5 us -> 29.1 us (0.954)
  the two profiles are of different devices: /device:TPU:0 before, /device:TPU:6 now
where the time goes in v5:
time: 29.1 us; the launch traced here: 29 us
  Pallas kernels  15.4 us (53%)
  starting transfers between devices  7.6 us (26%)
  waiting for transfers between devices  5.22 us (18%)
  between operations  0.74 us (3%)
    ppermute x9, starting transfers between devices, swap(): return lax.ppermute(x, 'seq', [(i, i ^ mask) for i in range(seq)])  7.6 us
    ppermute x9, waiting for transfers between devices, swap(): return lax.ppermute(x, 'seq', [(i, i ^ mask) for i in range(seq)])  5.22 us
    pallas_call x1, Pallas kernels, per_device(): pl.pallas_call(functools.partial(project_kernel, **sizes, rank=rank, log_...  5.21 us
    pallas_call x1, Pallas kernels, per_device(): pl.pallas_call(functools.partial(near_kernel, **sizes, rank=rank), in_spe...  2.78 us
    pallas_call x1, Pallas kernels, per_device(): pl.pallas_call(functools.partial(own_kernel, **sizes, rank=rank), in_spec...  2.74 us
    pallas_call x1, Pallas kernels, per_device(): pl.pallas_call(functools.partial(finish_kernel, **sizes, rank=rank, lengt...  2.14 us
    pallas_call x1, Pallas kernels, per_device(): pl.pallas_call(functools.partial(early_kernel, **sizes, rank=rank), in_sp...  1.28 us
    pallas_call x1, Pallas kernels, per_device(): pl.pallas_call(functools.partial(partner_kernel, **sizes, rank=rank, orde...  1.24 us
  transfers between devices with their start and end apart: 9, of which 2 were waited for; matrix products, arithmetic and copies ran while one was open for 0% of the time, Pallas kernels for 23%

profile of v5, /device:TPU:6, one launch (start us, length us, event | category | flops | bytes accessed | tf_op | source)
XLA Modules:
  0.0 29.0 jit_solution(8928057187247881890)
XLA Ops:
  0.6 0.0 copy-start.1
  0.6 0.0 copy-start.2
  0.7 0.0 copy-start.3
  0.7 5.2 %project.1 = (bf16[1,144,384]{2,1,0:T(8,128)(2,1)S(1)}, bf16[128,384]{1,0:T(8,128)(2,1)S(1)}, f32[256,1152]{1,0:T(8,128)S(1)}) custom-call(bf16[256,3072]{1,0:T(8,128)(2,1)} %bitcast.13, bf16[3072,1152]{1,0:T(8,128)(2,1)} %w_hbm.1, f32[9,128]{1,0:T(8,128)} %bitcast.15, f32[1,128]{1,0:T(1,128)} %bitcast.16, f32[1,128]{1,0:T(1,128)} %bitcast.17, ...), custom_call_target="tpu_custom_call" | custom-call | tf_op jit(solution)/shard_map/project/pallas_call | solution.py:459
  5.9 1.6 %collective-permute-start.4 = (bf16[1,144,384]{2,1,0:T(8,128)(2,1)S(1)}, bf16[1,144,384]{2,1,0:T(8,128)(2,1)S(1)}, u32[]{:S(2)}, u32[]{:S(2)}) collective-permute-start(bf16[1,144,384]{2,1,0:T(8,128)(2,1)S(1)} %get-tuple-element.22.refs_0_), channel_id=1, source_target_pairs={{0,6},{1,7},{2,4},{3,5},{4,2},{5,3},{6,0},{7,1},{8,14},{9,15},{10,... | collective-permute-start | bytes 331784 | tf_op jit(solution)/shard_map/ppermute | solution.py:497
  7.5 0.4 %collective-permute-start.3 = (bf16[1,144,384]{2,1,0:T(8,128)(2,1)S(1)}, bf16[1,144,384]{2,1,0:T(8,128)(2,1)S(1)}, u32[]{:S(2)}, u32[]{:S(2)}) collective-permute-start(bf16[1,144,384]{2,1,0:T(8,128)(2,1)S(1)} %get-tuple-element.22.refs_0_), channel_id=1, source_target_pairs={{0,4},{1,5},{2,6},{3,7},{4,0},{5,1},{6,2},{7,3},{8,12},{9,13},{10,... | collective-permute-start | bytes 331784 | tf_op jit(solution)/shard_map/ppermute | solution.py:497
  7.9 1.5 %collective-permute-start.2 = (bf16[1,144,384]{2,1,0:T(8,128)(2,1)S(1)}, bf16[1,144,384]{2,1,0:T(8,128)(2,1)S(1)}, u32[]{:S(2)}, u32[]{:S(2)}) collective-permute-start(bf16[1,144,384]{2,1,0:T(8,128)(2,1)S(1)} %get-tuple-element.22.refs_0_), channel_id=1, source_target_pairs={{0,2},{1,3},{2,0},{3,1},{4,6},{5,7},{6,4},{7,5},{8,10},{9,11},{10,... | collective-permute-start | bytes 331784 | tf_op jit(solution)/shard_map/ppermute | solution.py:497
  9.4 0.0 collective-permute-start.1
  9.4 2.6 %collective-permute-start = (bf16[128,384]{1,0:T(8,128)(2,1)S(1)}, bf16[128,384]{1,0:T(8,128)(2,1)S(1)}, u32[]{:S(2)}, u32[]{:S(2)}) collective-permute-start(bf16[128,384]{1,0:T(8,128)(2,1)S(1)} %get-tuple-element.21.query_ref), channel_id=1, source_target_pairs={{0,8},{1,9},{2,10},{3,11},{4,12},{5,13},{6,14},{7,15},{8,0},{9,1},... | collective-permute-start | bytes 294920 | tf_op jit(solution)/shard_map/ppermute | solution.py:497
  12.0 0.0 copy-done.1
  12.0 0.0 copy-done.2
  12.0 0.0 copy-done.3
  12.0 2.8 %near.1 = (f32[256,384]{1,0:T(8,128)S(1)}, f32[256,128]{1,0:T(8,128)S(1)}, bf16[2,128,384]{2,1,0:T(8,128)(2,1)S(1)}, bf16[2,128,384]{2,1,0:T(8,128)(2,1)S(1)}, f32[32,128]{1,0:T(8,128)S(1)}) custom-call(f32[256,1152]{1,0:T(8,128)S(1)} %get-tuple-element.23.qkv_ref, f32[2,3,2,128]{3,2,1,0:T(2,128)S(1)} %bitcast.12, s32[2,3]{1,0:T(2,128)S(1)} %copy-done.3, ...), custom_call_target="tpu_custom_call" | custom-call | flops 15099494400 | bytes 19660800 | tf_op jit(solution)/shard_map/near/pallas_call | solution.py:513
  14.8 0.0 collective-permute-done.4.refs_4_.refs_3_
  14.8 0.3 %collective-permute-start.7 = (bf16[1,144,384]{2,1,0:T(8,128)(2,1)S(1)}, bf16[1,144,384]{2,1,0:T(8,128)(2,1)S(1)}, u32[]{:S(2)}, u32[]{:S(2)}) collective-permute-start(bf16[1,144,384]{2,1,0:T(8,128)(2,1)S(1)} %collective-permute-done.4.refs_4_.refs_3_), channel_id=1, source_target_pairs={{0,1},{1,0},{2,3},{3,2},{4,5},{5,4},{6,7},{7,6},{8,9},{9,8},{10,11... | collective-permute-start | bytes 331784 | tf_op jit(solution)/shard_map/ppermute | solution.py:497
  15.1 0.0 collective-permute-done.3.refs_3_.refs_2_
  15.1 0.3 collective-permute-start.6
  15.4 0.0 collective-permute-done.2.refs_2_.refs_1_
  15.4 0.2 collective-permute-start.5
  15.7 2.0 %collective-permute-done.query_ref = bf16[128,384]{1,0:T(8,128)(2,1)S(1)} collective-permute-done((bf16[128,384]{1,0:T(8,128)(2,1)S(1)}, bf16[128,384]{1,0:T(8,128)(2,1)S(1)}, u32[]{:S(2)}, u32[]{:S(2)}) %collective-permute-start) | collective-permute-done | bytes 98336 | tf_op jit(solution)/shard_map/ppermute | solution.py:497
  17.7 0.0 collective-permute-done.1.refs_1_.refs_0_
  17.7 1.3 %early.1 = (f32[256,128]{1,0:T(8,128)S(1)}, f32[256,128]{1,0:T(8,128)S(1)}) custom-call(bf16[128,384]{1,0:T(8,128)(2,1)S(1)} %collective-permute-done.query_ref, bf16[1,144,384]{2,1,0:T(8,128)(2,1)S(1)} %get-tuple-element.22.refs_0_, bf16[1,144,384]{2,1,0:T(8,128)(2,1)S(1)} %collective-permute-done.1.refs_1_.refs_0_, ...), custom_call_target="tpu_custom_call" | custom-call | flops 503316480 | bytes 491520 | tf_op jit(solution)/shard_map/early/pallas_call | solution.py:549
  19.0 0.0 collective-permute-done.7.refs_7_.refs_6_
  19.0 0.0 collective-permute-done.6.refs_6_.refs_5_
  19.0 0.0 collective-permute-done.5.refs_5_.refs_4_
  19.0 1.2 %partner.1 = (bf16[256,128]{1,0:T(8,128)(2,1)S(1)}, f32[16,128]{1,0:T(8,128)S(1)}) custom-call(bf16[128,384]{1,0:T(8,128)(2,1)S(1)} %collective-permute-done.query_ref, f32[256,128]{1,0:T(8,128)S(1)} %get-tuple-element.28.part_ref, f32[256,128]{1,0:T(8,128)S(1)} %get-tuple-element.29.part_log_ref, bf16[1,144,384]{2,1,0:T(8,128)(2,1)S(1)} %get-tuple-element.22.refs_0_, ...), custom_call_target="tpu_custom_call" | custom-call | flops 805306368 | bytes 786432 | tf_op jit(solution)/shard_map/partner/pallas_call | solution.py:558
  20.2 0.0 copy-start
  20.2 0.6 %collective-permute-start.8 = (bf16[256,128]{1,0:T(8,128)(2,1)S(1)}, bf16[256,128]{1,0:T(8,128)(2,1)S(1)}, u32[]{:S(2)}, u32[]{:S(2)}) collective-permute-start(bf16[256,128]{1,0:T(8,128)(2,1)S(1)} %get-tuple-element.30), channel_id=1, source_target_pairs={{0,8},{1,9},{2,10},{3,11},{4,12},{5,13},{6,14},{7,15},{8,0},{9,1},... | collective-permute-start | bytes 196616 | tf_op jit(solution)/shard_map/ppermute | solution.py:497
  20.9 2.7 %own.1 = (f32[256,384]{1,0:T(8,128)S(1)}, f32[256,128]{1,0:T(8,128)S(1)}) custom-call(bf16[128,384]{1,0:T(8,128)(2,1)S(1)} %get-tuple-element.21.query_ref, f32[256,384]{1,0:T(8,128)S(1)} %get-tuple-element.32.near_ref, f32[256,128]{1,0:T(8,128)S(1)} %get-tuple-element.24.stat_ref, f32[32,128]{1,0:T(8,128)S(1)} %get-tuple-element.33.old_ref, ...), custom_call_target="tpu_custom_call" | custom-call | flops 805306368 | bytes 786432 | tf_op jit(solution)/shard_map/own/pallas_call | solution.py:573
  23.6 3.2 %collective-permute-done.8.back_ref = bf16[256,128]{1,0:T(8,128)(2,1)S(1)} collective-permute-done((bf16[256,128]{1,0:T(8,128)(2,1)S(1)}, bf16[256,128]{1,0:T(8,128)(2,1)S(1)}, u32[]{:S(2)}, u32[]{:S(2)}) %collective-permute-start.8) | collective-permute-done | bytes 65568 | tf_op jit(solution)/shard_map/ppermute | solution.py:497
  26.8 0.0 copy-done
  26.8 2.1 %finish.1 = (bf16[256,3072]{1,0:T(8,128)(2,1)}, f32[2,3,2,128]{3,2,1,0:T(2,128)}) custom-call(bf16[256,128]{1,0:T(8,128)(2,1)S(1)} %collective-permute-done.8.back_ref, f32[16,128]{1,0:T(8,128)S(1)} %get-tuple-element.31.half_ref, f32[256,384]{1,0:T(8,128)S(1)} %get-tuple-element.36.merged_ref, f32[256,128]{1,0:T(8,128)S(1)} %get-tuple-element.37.log_ref, ...), custom_call_target="tpu_custom_call" | custom-call | tf_op jit(solution)/shard_map/finish/pallas_call | solution.py:587
Async XLA Ops:
  0.6 11.4 %copy-start.1 = (f32[3,128,32]{1,2,0:T(8,128)S(1)}, f32[3,128,32]{1,2,0:T(8,128)}, u32[]{:S(2)}) copy-start(f32[3,128,32]{1,2,0:T(8,128)} %param.16) | copy-start | bytes 147460
  0.6 11.4 %copy-start.2 = (f32[2,2,3,128]{3,1,2,0:T(2,128)S(1)}, f32[2,2,3,128]{3,1,2,0:T(2,128)}, u32[]{:S(2)}) copy-start(f32[2,2,3,128]{3,1,2,0:T(2,128)} %param.17) | copy-start | bytes 18436
  0.7 11.4 %copy-start.3 = (s32[2,3]{1,0:T(2,128)S(1)}, s32[2,3]{1,0:T(2,128)}, u32[]{:S(2)}) copy-start(s32[2,3]{1,0:T(2,128)} %refresh_ref.1) | copy-start | bytes 76
  5.9 9.0 %collective-permute-start.4 = (bf16[1,144,384]{2,1,0:T(8,128)(2,1)S(1)}, bf16[1,144,384]{2,1,0:T(8,128)(2,1)S(1)}, u32[]{:S(2)}, u32[]{:S(2)}) collective-permute-start(bf16[1,144,384]{2,1,0:T(8,128)(2,1)S(1)} %get-tuple-element.22.refs_0_), channel_id=1, source_target_pairs={{0,6},{1,7},{2,4},{3,5},{4,2},{5,3},{6,0},{7,1},{8,14},{9,15},{10,... | collective-permute-start | bytes 331784 | tf_op jit(solution)/shard_map/ppermute | solution.py:497
  7.5 7.7 %collective-permute-start.3 = (bf16[1,144,384]{2,1,0:T(8,128)(2,1)S(1)}, bf16[1,144,384]{2,1,0:T(8,128)(2,1)S(1)}, u32[]{:S(2)}, u32[]{:S(2)}) collective-permute-start(bf16[1,144,384]{2,1,0:T(8,128)(2,1)S(1)} %get-tuple-element.22.refs_0_), channel_id=1, source_target_pairs={{0,4},{1,5},{2,6},{3,7},{4,0},{5,1},{6,2},{7,3},{8,12},{9,13},{10,... | collective-permute-start | bytes 331784 | tf_op jit(solution)/shard_map/ppermute | solution.py:497
  7.9 7.5 %collective-permute-start.2 = (bf16[1,144,384]{2,1,0:T(8,128)(2,1)S(1)}, bf16[1,144,384]{2,1,0:T(8,128)(2,1)S(1)}, u32[]{:S(2)}, u32[]{:S(2)}) collective-permute-start(bf16[1,144,384]{2,1,0:T(8,128)(2,1)S(1)} %get-tuple-element.22.refs_0_), channel_id=1, source_target_pairs={{0,2},{1,3},{2,0},{3,1},{4,6},{5,7},{6,4},{7,5},{8,10},{9,11},{10,... | collective-permute-start | bytes 331784 | tf_op jit(solution)/shard_map/ppermute | solution.py:497
  9.4 8.2 %collective-permute-start.1 = (bf16[1,144,384]{2,1,0:T(8,128)(2,1)S(1)}, bf16[1,144,384]{2,1,0:T(8,128)(2,1)S(1)}, u32[]{:S(2)}, u32[]{:S(2)}) collective-permute-start(bf16[1,144,384]{2,1,0:T(8,128)(2,1)S(1)} %get-tuple-element.22.refs_0_), channel_id=1, source_target_pairs={{0,1},{1,0},{2,3},{3,2},{4,5},{5,4},{6,7},{7,6},{8,9},{9,8},{10,11... | collective-permute-start | bytes 331784 | tf_op jit(solution)/shard_map/ppermute | solution.py:497
  9.4 8.2 %collective-permute-start = (bf16[128,384]{1,0:T(8,128)(2,1)S(1)}, bf16[128,384]{1,0:T(8,128)(2,1)S(1)}, u32[]{:S(2)}, u32[]{:S(2)}) collective-permute-start(bf16[128,384]{1,0:T(8,128)(2,1)S(1)} %get-tuple-element.21.query_ref), channel_id=1, source_target_pairs={{0,8},{1,9},{2,10},{3,11},{4,12},{5,13},{6,14},{7,15},{8,0},{9,1},... | collective-permute-start | bytes 294920 | tf_op jit(solution)/shard_map/ppermute | solution.py:497
  14.8 4.1 %collective-permute-start.7 = (bf16[1,144,384]{2,1,0:T(8,128)(2,1)S(1)}, bf16[1,144,384]{2,1,0:T(8,128)(2,1)S(1)}, u32[]{:S(2)}, u32[]{:S(2)}) collective-permute-start(bf16[1,144,384]{2,1,0:T(8,128)(2,1)S(1)} %collective-permute-done.4.refs_4_.refs_3_), channel_id=1, source_target_pairs={{0,1},{1,0},{2,3},{3,2},{4,5},{5,4},{6,7},{7,6},{8,9},{9,8},{10,11... | collective-permute-start | bytes 331784 | tf_op jit(solution)/shard_map/ppermute | solution.py:497
  15.1 3.8 %collective-permute-start.6 = (bf16[1,144,384]{2,1,0:T(8,128)(2,1)S(1)}, bf16[1,144,384]{2,1,0:T(8,128)(2,1)S(1)}, u32[]{:S(2)}, u32[]{:S(2)}) collective-permute-start(bf16[1,144,384]{2,1,0:T(8,128)(2,1)S(1)} %collective-permute-done.3.refs_3_.refs_2_), channel_id=1, source_target_pairs={{0,1},{1,0},{2,3},{3,2},{4,5},{5,4},{6,7},{7,6},{8,9},{9,8},{10,11... | collective-permute-start | bytes 331784 | tf_op jit(solution)/shard_map/ppermute | solution.py:497
  15.4 3.5 %collective-permute-start.5 = (bf16[1,144,384]{2,1,0:T(8,128)(2,1)S(1)}, bf16[1,144,384]{2,1,0:T(8,128)(2,1)S(1)}, u32[]{:S(2)}, u32[]{:S(2)}) collective-permute-start(bf16[1,144,384]{2,1,0:T(8,128)(2,1)S(1)} %collective-permute-done.2.refs_2_.refs_1_), channel_id=1, source_target_pairs={{0,1},{1,0},{2,3},{3,2},{4,5},{5,4},{6,7},{7,6},{8,9},{9,8},{10,11... | collective-permute-start | bytes 331784 | tf_op jit(solution)/shard_map/ppermute | solution.py:497
  20.2 6.6 %copy-start = (bf16[384,3072]{1,0:T(8,128)(2,1)S(1)}, bf16[384,3072]{1,0:T(8,128)(2,1)}, u32[]{:S(2)}) copy-start(bf16[384,3072]{1,0:T(8,128)(2,1)} %w_ref.1) | copy-start | bytes 7077892
  20.2 6.6 %collective-permute-start.8 = (bf16[256,128]{1,0:T(8,128)(2,1)S(1)}, bf16[256,128]{1,0:T(8,128)(2,1)S(1)}, u32[]{:S(2)}, u32[]{:S(2)}) collective-permute-start(bf16[256,128]{1,0:T(8,128)(2,1)S(1)} %get-tuple-element.30), channel_id=1, source_target_pairs={{0,8},{1,9},{2,10},{3,11},{4,12},{5,13},{6,14},{7,15},{8,0},{9,1},... | collective-permute-start | bytes 196616 | tf_op jit(solution)/shard_map/ppermute | solution.py:497

commit v6 on v5

--- a/solution.py
+++ b/solution.py
@@ -210,7 +210,7 @@
 
 
 def near_kernel(
-    qkv_ref, centers_ref, refresh_ref, vb_ref, near_ref, stat_ref, basis_h, basis_l, old_ref,
+    qkv_ref, centers_ref, refresh_ref, vb_ref, near_ref, rel_ref, basis_h, basis_l, old_ref,
     *, samples, tokens, heads, dim, rank,
 ):
     width = heads * dim
@@ -223,23 +223,21 @@
                 keep = jnp.where(refresh_ref[j, h] == 1, 0.0, 1.0)
                 old_ref[row : row + 1, :] = centers_ref[b, h, j : j + 1, :]
                 old_ref[SUM_ROWS + row : SUM_ROWS + row + 1, :] = jnp.full((1, dim), keep, f32)
-    lanes = lane_ids(tokens, dim)
     for b in range(samples):
         rows = slice(b * tokens, (b + 1) * tokens)
-        stats = jnp.zeros((tokens, dim), f32)
-        for h in range(heads):
-            q = qkv_ref[rows, h * dim : (h + 1) * dim]
+        for h in range(heads):
+            head = slice(h * dim, (h + 1) * dim)
+            q = qkv_ref[rows, head]
             k = split(qkv_ref[rows, width + h * dim : width + (h + 1) * dim])
             v = split(qkv_ref[rows, 2 * width + h * dim : 2 * width + (h + 1) * dim])
             scores = dot3(split(q), k, NT)
             row_max = jnp.max(scores, axis=-1, keepdims=True)
             weights = jnp.exp2(scores - row_max)
             row_sum = jnp.sum(weights, axis=-1, keepdims=True)
-            near_ref[rows, h * dim : (h + 1) * dim] = dot3(split(weights), v) / row_sum
+            near_ref[rows, head] = dot3(split(weights), v) / row_sum
             center = jnp.sum(q * centers_ref[b, h, 0:1, :], axis=-1, keepdims=True)
-            stats = jnp.where(lanes == h, row_max + jnp.log(row_sum) * log2_e, stats)
-            stats = jnp.where(lanes == heads + h, center, stats)
-        stat_ref[rows, :] = stats
+            rel = row_max + jnp.log(row_sum) * log2_e - center
+            rel_ref[rows, head] = jnp.broadcast_to(rel, (tokens, dim))
 
 
 def query_parts(query_ref, sample, heads, dim, rank):
@@ -251,46 +249,65 @@
     return second, jnp.where(lanes < heads * rank, turned, query_ref[:, 2 * dim :].astype(f32))
 
 
-def code_attention(query_ref, tiles, b, *, samples, tokens, heads, dim, rank):
+def code_attention(query_ref, tiles, *, samples, tokens, heads, dim, rank):
     lanes = lane_ids(tokens, dim)
-    high, low = query_parts(query_ref, b, heads, dim, rank)
-    stacked = []
+    scores, values = [], []
+    for b in range(samples):
+        high, low = query_parts(query_ref, b, heads, dim, rank)
+        stacked = []
+        for h in range(heads):
+            own = within(lanes, key_lane(b, h, rank), rank)
+            both = [jnp.where(own, part, 0.0).astype(bf16) for part in (high, low)]
+            stacked.append(jnp.concatenate(both, axis=1))
+        left = jnp.concatenate(stacked, axis=0)
+        codes = [ref[i, :tokens, b * dim : (b + 1) * dim] for ref, i in tiles]
+        values.append(jnp.concatenate(codes, axis=0))
+        parts = []
+        for i in range(0, len(codes), 2):
+            some = jnp.concatenate(codes[i : i + 2], axis=0)
+            both = dot(left, jnp.concatenate([some, some], axis=1), NT)
+            parts += [both[:, j * tokens : (j + 1) * tokens] for j in range(len(codes[i : i + 2]))]
+        scores.append(parts)
+    rest = jnp.concatenate([ref[i, :tokens, samples * dim :] for ref, i in tiles], axis=0)
+    weights, scales, logs = [], [], []
+    for b in range(samples):
+        best = scores[b][0]
+        for part in scores[b][1:]:
+            best = jnp.maximum(best, part)
+        row_max = jnp.max(best, axis=-1, keepdims=True)
+        total = jnp.zeros_like(best)
+        parts = []
+        for part in scores[b]:
+            weight = jnp.exp2(part - row_max).astype(bf16)
+            total = total + weight.astype(f32)
+            parts.append(weight)
+        row_sum = jnp.sum(total, axis=-1, keepdims=True)
+        weights.append(jnp.concatenate(parts, axis=1))
+        scales.append(1.0 / row_sum)
+        log = row_max + jnp.log(row_sum) * log2_e
+        logs.append([log[h * tokens : (h + 1) * tokens] for h in range(heads)])
+    outs = []
+    for b in range(samples):
+        results = [dot(weights[b][:tokens], values[b])]
+        others = dot(weights[b][tokens:], rest)
+        results += [others[h * tokens : (h + 1) * tokens] for h in range(heads - 1)]
+        out = jnp.zeros((tokens, dim), f32)
+        for h in range(heads):
+            part = results[h] * scales[b][h * tokens : (h + 1) * tokens]
+            out = jnp.where(within(lanes, value_lane(b, h, rank, heads), rank), part, out)
+        outs.append(out)
+    return outs, logs
+
+
+def spread(b, logs, tokens, heads, dim, rank):
+    lanes = lane_ids(tokens, dim)
+    out = jnp.zeros((tokens, dim), f32)
     for h in range(heads):
-        own = within(lanes, key_lane(b, h, rank), rank)
-        both = [jnp.where(own, part, 0.0).astype(bf16) for part in (high, low)]
-        stacked.append(jnp.concatenate(both, axis=1))
-    left = jnp.concatenate(stacked, axis=0)
-    scores, values, codes = [], [], []
-    for ref, i in tiles:
-        code = ref[i, :tokens, b * dim : (b + 1) * dim]
-        codes.append(jnp.concatenate([code, code], axis=1))
-        values.append(jnp.concatenate([code, ref[i, :tokens, samples * dim :]], axis=1))
-    for i in range(0, len(codes), 2):
-        some = codes[i : i + 2]
-        both = dot(left, jnp.concatenate(some, axis=0), NT)
-        scores += [both[:, j * tokens : (j + 1) * tokens] for j in range(len(some))]
-    best = scores[0]
-    for part in scores[1:]:
-        best = jnp.maximum(best, part)
-    row_max = jnp.max(best, axis=-1, keepdims=True)
-    total = jnp.zeros_like(best)
-    weights = []
-    for part in scores:
-        weight = jnp.exp2(part - row_max).astype(bf16)
-        total = total + weight.astype(f32)
-        weights.append(weight)
-    result = dot(jnp.concatenate(weights, axis=1), jnp.concatenate(values, axis=0))
-    row_sum = jnp.sum(total, axis=-1, keepdims=True)
-    result = result / row_sum
-    log_sum = row_max + jnp.log(row_sum) * log2_e
-    out = jnp.zeros((tokens, dim), f32)
-    logs = []
-    for h in range(heads):
-        head_rows = slice(h * tokens, (h + 1) * tokens)
-        part = result[head_rows, :dim] if h == 0 else result[head_rows, dim:]
-        out = jnp.where(within(lanes, value_lane(b, h, rank, heads), rank), part, out)
-        logs.append(log_sum[head_rows])
-    return out, logs
+        place = within(lanes, value_lane(b, h, rank, heads), rank)
+        for p in range(3):
+            place = place | (lanes == log_lane(b, h, p, rank))
+        out = jnp.where(place, logs[h], out)
+    return out
 
 
 def tree_sum(parts):
@@ -307,16 +324,14 @@
     out_ref, log_ref = refs[-2:]
     tiles = tiles_of(refs[:-2])
     lanes = lane_ids(tokens, dim)
+    outs, all_logs = code_attention(
+        query_ref, tiles, samples=samples, tokens=tokens, heads=heads, dim=dim, rank=rank
+    )
     for b in range(samples):
         rows = slice(b * tokens, (b + 1) * tokens)
-        out, logs = code_attention(
-            query_ref, tiles, b, samples=samples, tokens=tokens, heads=heads, dim=dim, rank=rank
-        )
-        kept = jnp.zeros((tokens, dim), f32)
-        for h in range(heads):
-            kept = jnp.where(lanes == h, logs[h], kept)
+        out, logs = outs[b], all_logs[b]
         out_ref[rows, :] = out
-        log_ref[rows, :] = kept
+        log_ref[rows, :] = spread(b, logs, tokens, heads, dim, rank)
 
 
 def partner_kernel(
@@ -335,58 +350,52 @@
     empty = jnp.zeros((tokens - SUM_ROWS, dim), f32)
     turned = [jnp.concatenate([piece, empty], axis=0).T for piece in pieces]
     lanes = lane_ids(tokens, dim)
+    outs, all_logs = code_attention(
+        query_ref, tiles[-late:], samples=samples, tokens=tokens, heads=heads, dim=dim, rank=rank
+    )
     for b in range(samples):
         rows = slice(b * tokens, (b + 1) * tokens)
-        out, logs = code_attention(
-            query_ref, tiles[-late:], b,
-            samples=samples, tokens=tokens, heads=heads, dim=dim, rank=rank,
-        )
-        before, before_logs = part_ref[rows, :], part_log_ref[rows, :]
-        scale = jnp.zeros((tokens, dim), f32)
-        for h in range(heads):
-            before_log = before_logs[:, h : h + 1]
-            top = jnp.maximum(logs[h], before_log)
-            new, old = jnp.exp2(logs[h] - top), jnp.exp2(before_log - top)
-            whole = new + old
-            scale = jnp.where(within(lanes, value_lane(b, h, rank, heads), rank), new / whole, scale)
-            logs[h] = top + jnp.log(whole) * log2_e
-        out = before + (out - before) * scale
-        for h in range(heads):
-            for p, piece in enumerate(pieces_of(logs[h], 3)):
-                out = jnp.where(lanes == log_lane(b, h, p, rank), piece.astype(f32), out)
+        out, logs = outs[b], all_logs[b]
+        before, before_log = part_ref[rows, :], part_log_ref[rows, :]
+        log = spread(b, logs, tokens, heads, dim, rank)
+        top = jnp.maximum(log, before_log)
+        new = jnp.exp2(log - top)
+        whole = new + jnp.exp2(before_log - top)
+        out = before + (out - before) * (new / whole)
+        log = top + jnp.log(whole) * log2_e
+        for p, piece in enumerate(pieces_of(log, 3)):
+            place = within(lanes, log_lane(b, 0, p, rank), heads)
+            out = jnp.where(place, piece.astype(f32), out)
         at = sum_lane(b, rank)
         out = jnp.where(within(lanes, at, 2 * samples * heads), pltpu.roll(turned[b], at, 1), out)
         out_ref[rows, :] = out.astype(bf16)
 
 
 def own_kernel(
-    query_ref, near_ref, stat_ref, old_ref, basis_h, basis_l, *refs,
+    query_ref, near_ref, rel_ref, old_ref, basis_h, basis_l, *refs,
     samples, tokens, heads, dim, rank,
 ):
     merged_ref, log_ref = refs[-2:]
     tiles = tiles_of(refs[:-2])
     lanes = lane_ids(tokens, dim)
+    outs, all_logs = code_attention(
+        query_ref, tiles, samples=samples, tokens=tokens, heads=heads, dim=dim, rank=rank
+    )
     for b in range(samples):
         rows = slice(b * tokens, (b + 1) * tokens)
-        out, logs = code_attention(
-            query_ref, tiles, b, samples=samples, tokens=tokens, heads=heads, dim=dim, rank=rank
-        )
+        out, logs = outs[b], all_logs[b]
         far = dot3(split(out), (basis_h[b], basis_l[b]))
-        stats = stat_ref[rows, :]
         kept = jnp.zeros((tokens, dim), f32)
         for h in range(heads):
             columns = slice(h * dim, (h + 1) * dim)
-            near_log = stats[:, h : h + 1]
-            center = stats[:, heads + h : heads + h + 1]
-            far_log = logs[h] + center
-            top = jnp.maximum(near_log, far_log)
-            near_part, far_part = jnp.exp2(near_log - top), jnp.exp2(far_log - top)
-            whole = near_part + far_part
-            merged = near_ref[rows, columns] * (near_part / whole)
+            near, rel = near_ref[rows, columns], rel_ref[rows, columns]
+            top = jnp.maximum(rel, logs[h])
+            far_part = jnp.exp2(logs[h] - top)
+            whole = jnp.exp2(rel - top) + far_part
             row = (b * heads + h) * 2 + 1
-            merged = merged + (far[:, columns] + old_ref[row : row + 1, :]) * (far_part / whole)
-            merged_ref[rows, columns] = merged
-            log = top + jnp.log(whole) * log2_e - center
+            value = far[:, columns] + old_ref[row : row + 1, :] - near
+            merged_ref[rows, columns] = near + value * (far_part / whole)
+            log = top + jnp.log(whole) * log2_e
             kept = jnp.where(lanes == log_lane(b, h, 0, rank), log, kept)
         log_ref[rows, :] = kept
 
@@ -510,13 +519,13 @@
 
     query_far = swap(query, far_mask)
 
-    near, stats, basis_high, basis_low, old = pl.pallas_call(
+    near, rel, basis_high, basis_low, old = pl.pallas_call(
         functools.partial(near_kernel, **sizes, rank=rank),
         in_specs=[VMEM, VMEM, pl.BlockSpec(memory_space=pltpu.SMEM), VMEM],
         out_specs=[VMEM] * 5,
         out_shape=[
             jax.ShapeDtypeStruct((rows, width), f32),
-            jax.ShapeDtypeStruct((rows, dim), f32),
+            jax.ShapeDtypeStruct((rows, width), f32),
             jax.ShapeDtypeStruct((samples, dim, width), bf16),
             jax.ShapeDtypeStruct((samples, dim, width), bf16),
             jax.ShapeDtypeStruct((2 * SUM_ROWS, dim), f32),
@@ -529,7 +538,7 @@
     )(qkv, center_rows, refresh, value_rows)
 
     for i in range(1, len(held)):
-        x, _ = lax.optimization_barrier((held[i][0], stats))
+        x, _ = lax.optimization_barrier((held[i][0], rel))
         held[i] = (x, held[i][1])
     held.insert(1, (swap(payload, 1), [1]))
     early = [a for a, _ in held]
@@ -581,7 +590,7 @@
         compiler_params=params(32),
         cost_estimate=cost(len(names)),
         name="own",
-    )(query, near, stats, old, basis_high, basis_low, *arrays[1:])
+    )(query, near, rel, old, basis_high, basis_low, *arrays[1:])
 
     columns = 768
     mixed, new_centers = pl.pallas_call(

time: 29.1 us -> 28.4 us (0.976)
  Pallas kernels: 15.4 us -> 13.6 us
  waiting for transfers between devices: 5.22 us -> 6.3 us
    ppermute x9, waiting for transfers between devices: 5.22 us -> 6.3 us  [swap(): return lax.ppermute(x, 'seq', [(i, i ^ mask) for i in range(seq)])]
    pallas_call x1, Pallas kernels: 2.74 us -> 1.65 us  [per_device(): pl.pallas_call(functools.partial(own_kernel, **sizes, rank=rank), in_spec...]
    pallas_call x1, Pallas kernels: 1.24 us -> 0.79 us  [per_device(): pl.pallas_call(functools.partial(partner_kernel, **sizes, rank=rank, orde...]
    pallas_call x1, Pallas kernels: 1.28 us -> 0.98 us  [per_device(): pl.pallas_call(functools.partial(early_kernel, **sizes, rank=rank), in_sp...]
  transfers between devices with their start and end apart: 9 -> 9, of which waited for: 2 -> 2; matrix products, arithmetic and copies ran while one was open for 0% -> 0% of each run, Pallas kernels for 23% -> 19%
where the time goes in v6:
time: 28.4 us; the launch traced here: 28.2 us
  Pallas kernels  13.6 us (48%)
  starting transfers between devices  7.6 us (27%)
  waiting for transfers between devices  6.3 us (22%)
  between operations  0.74 us (3%)
    ppermute x9, starting transfers between devices, swap(): return lax.ppermute(x, 'seq', [(i, i ^ mask) for i in range(seq)])  7.6 us
    ppermute x9, waiting for transfers between devices, swap(): return lax.ppermute(x, 'seq', [(i, i ^ mask) for i in range(seq)])  6.3 us
    pallas_call x1, Pallas kernels, per_device(): pl.pallas_call(functools.partial(project_kernel, **sizes, rank=rank, log_...  5.21 us
    pallas_call x1, Pallas kernels, per_device(): pl.pallas_call(functools.partial(near_kernel, **sizes, rank=rank), in_spe...  2.78 us
    pallas_call x1, Pallas kernels, per_device(): pl.pallas_call(functools.partial(finish_kernel, **sizes, rank=rank, lengt...  2.14 us
    pallas_call x1, Pallas kernels, per_device(): pl.pallas_call(functools.partial(own_kernel, **sizes, rank=rank), in_spec...  1.65 us
    pallas_call x1, Pallas kernels, per_device(): pl.pallas_call(functools.partial(early_kernel, **sizes, rank=rank), in_sp...  0.98 us
    pallas_call x1, Pallas kernels, per_device(): pl.pallas_call(functools.partial(partner_kernel, **sizes, rank=rank, orde...  0.79 us
  transfers between devices with their start and end apart: 9, of which 2 were waited for; matrix products, arithmetic and copies ran while one was open for 0% of the time, Pallas kernels for 19%

profile of v6, /device:TPU:6, one launch (start us, length us, event | category | flops | bytes accessed | tf_op | source)
XLA Modules:
  0.0 28.2 jit_solution(2571691832496166587)
XLA Ops:
  0.6 0.0 copy-start.1
  0.6 0.0 copy-start.2
  0.7 0.0 copy-start.3
  0.7 5.2 %project.1 = (bf16[1,144,384]{2,1,0:T(8,128)(2,1)S(1)}, bf16[128,384]{1,0:T(8,128)(2,1)S(1)}, f32[256,1152]{1,0:T(8,128)S(1)}) custom-call(bf16[256,3072]{1,0:T(8,128)(2,1)} %bitcast.13, bf16[3072,1152]{1,0:T(8,128)(2,1)} %w_hbm.1, f32[9,128]{1,0:T(8,128)} %bitcast.15, f32[1,128]{1,0:T(1,128)} %bitcast.16, f32[1,128]{1,0:T(1,128)} %bitcast.17, ...), custom_call_target="tpu_custom_call" | custom-call | tf_op jit(solution)/shard_map/project/pallas_call | solution.py:468
  5.9 1.6 %collective-permute-start.4 = (bf16[1,144,384]{2,1,0:T(8,128)(2,1)S(1)}, bf16[1,144,384]{2,1,0:T(8,128)(2,1)S(1)}, u32[]{:S(2)}, u32[]{:S(2)}) collective-permute-start(bf16[1,144,384]{2,1,0:T(8,128)(2,1)S(1)} %get-tuple-element.22.refs_0_), channel_id=1, source_target_pairs={{0,6},{1,7},{2,4},{3,5},{4,2},{5,3},{6,0},{7,1},{8,14},{9,15},{10,... | collective-permute-start | bytes 331784 | tf_op jit(solution)/shard_map/ppermute | solution.py:506
  7.5 0.4 %collective-permute-start.3 = (bf16[1,144,384]{2,1,0:T(8,128)(2,1)S(1)}, bf16[1,144,384]{2,1,0:T(8,128)(2,1)S(1)}, u32[]{:S(2)}, u32[]{:S(2)}) collective-permute-start(bf16[1,144,384]{2,1,0:T(8,128)(2,1)S(1)} %get-tuple-element.22.refs_0_), channel_id=1, source_target_pairs={{0,4},{1,5},{2,6},{3,7},{4,0},{5,1},{6,2},{7,3},{8,12},{9,13},{10,... | collective-permute-start | bytes 331784 | tf_op jit(solution)/shard_map/ppermute | solution.py:506
  7.9 1.5 %collective-permute-start.2 = (bf16[1,144,384]{2,1,0:T(8,128)(2,1)S(1)}, bf16[1,144,384]{2,1,0:T(8,128)(2,1)S(1)}, u32[]{:S(2)}, u32[]{:S(2)}) collective-permute-start(bf16[1,144,384]{2,1,0:T(8,128)(2,1)S(1)} %get-tuple-element.22.refs_0_), channel_id=1, source_target_pairs={{0,2},{1,3},{2,0},{3,1},{4,6},{5,7},{6,4},{7,5},{8,10},{9,11},{10,... | collective-permute-start | bytes 331784 | tf_op jit(solution)/shard_map/ppermute | solution.py:506
  9.4 0.0 collective-permute-start.1
  9.4 2.6 %collective-permute-start = (bf16[128,384]{1,0:T(8,128)(2,1)S(1)}, bf16[128,384]{1,0:T(8,128)(2,1)S(1)}, u32[]{:S(2)}, u32[]{:S(2)}) collective-permute-start(bf16[128,384]{1,0:T(8,128)(2,1)S(1)} %get-tuple-element.21.query_ref), channel_id=1, source_target_pairs={{0,8},{1,9},{2,10},{3,11},{4,12},{5,13},{6,14},{7,15},{8,0},{9,1},... | collective-permute-start | bytes 294920 | tf_op jit(solution)/shard_map/ppermute | solution.py:506
  12.0 0.0 copy-done.1
  12.0 0.0 copy-done.2
  12.0 0.0 copy-done.3
  12.0 2.8 %near.1 = (f32[256,384]{1,0:T(8,128)S(1)}, f32[256,384]{1,0:T(8,128)S(1)}, bf16[2,128,384]{2,1,0:T(8,128)(2,1)S(1)}, bf16[2,128,384]{2,1,0:T(8,128)(2,1)S(1)}, f32[32,128]{1,0:T(8,128)S(1)}) custom-call(f32[256,1152]{1,0:T(8,128)S(1)} %get-tuple-element.23.qkv_ref, f32[2,3,2,128]{3,2,1,0:T(2,128)S(1)} %bitcast.12, s32[2,3]{1,0:T(2,128)S(1)} %copy-done.3, ...), custom_call_target="tpu_custom_call" | custom-call | flops 15099494400 | bytes 19660800 | tf_op jit(solution)/shard_map/near/pallas_call | solution.py:522
  14.8 0.0 collective-permute-done.4.refs_4_.refs_3_
  14.8 0.3 %collective-permute-start.7 = (bf16[1,144,384]{2,1,0:T(8,128)(2,1)S(1)}, bf16[1,144,384]{2,1,0:T(8,128)(2,1)S(1)}, u32[]{:S(2)}, u32[]{:S(2)}) collective-permute-start(bf16[1,144,384]{2,1,0:T(8,128)(2,1)S(1)} %collective-permute-done.4.refs_4_.refs_3_), channel_id=1, source_target_pairs={{0,1},{1,0},{2,3},{3,2},{4,5},{5,4},{6,7},{7,6},{8,9},{9,8},{10,11... | collective-permute-start | bytes 331784 | tf_op jit(solution)/shard_map/ppermute | solution.py:506
  15.1 0.0 collective-permute-done.3.refs_3_.refs_2_
  15.1 0.3 collective-permute-start.6
  15.4 0.0 collective-permute-done.2.refs_2_.refs_1_
  15.4 0.2 collective-permute-start.5
  15.7 2.0 %collective-permute-done.query_ref = bf16[128,384]{1,0:T(8,128)(2,1)S(1)} collective-permute-done((bf16[128,384]{1,0:T(8,128)(2,1)S(1)}, bf16[128,384]{1,0:T(8,128)(2,1)S(1)}, u32[]{:S(2)}, u32[]{:S(2)}) %collective-permute-start) | collective-permute-done | bytes 98336 | tf_op jit(solution)/shard_map/ppermute | solution.py:506
  17.7 0.0 collective-permute-done.1.refs_1_.refs_0_
  17.7 1.0 %early.1 = (f32[256,128]{1,0:T(8,128)S(1)}, f32[256,128]{1,0:T(8,128)S(1)}) custom-call(bf16[128,384]{1,0:T(8,128)(2,1)S(1)} %collective-permute-done.query_ref, bf16[1,144,384]{2,1,0:T(8,128)(2,1)S(1)} %get-tuple-element.22.refs_0_, bf16[1,144,384]{2,1,0:T(8,128)(2,1)S(1)} %collective-permute-done.1.refs_1_.refs_0_, ...), custom_call_target="tpu_custom_call" | custom-call | flops 503316480 | bytes 491520 | tf_op jit(solution)/shard_map/early/pallas_call | solution.py:558
  18.6 0.0 collective-permute-done.7.refs_7_.refs_6_
  18.7 0.0 collective-permute-done.6.refs_6_.refs_5_
  18.7 0.0 collective-permute-done.5.refs_5_.refs_4_
  18.7 0.8 %partner.1 = (bf16[256,128]{1,0:T(8,128)(2,1)S(1)}, f32[16,128]{1,0:T(8,128)S(1)}) custom-call(bf16[128,384]{1,0:T(8,128)(2,1)S(1)} %collective-permute-done.query_ref, f32[256,128]{1,0:T(8,128)S(1)} %get-tuple-element.28.part_ref, f32[256,128]{1,0:T(8,128)S(1)} %get-tuple-element.29.part_log_ref, bf16[1,144,384]{2,1,0:T(8,128)(2,1)S(1)} %get-tuple-element.22.refs_0_, ...), custom_call_target="tpu_custom_call" | custom-call | flops 805306368 | bytes 786432 | tf_op jit(solution)/shard_map/partner/pallas_call | solution.py:567
  19.5 0.0 copy-start
  19.5 0.6 %collective-permute-start.8 = (bf16[256,128]{1,0:T(8,128)(2,1)S(1)}, bf16[256,128]{1,0:T(8,128)(2,1)S(1)}, u32[]{:S(2)}, u32[]{:S(2)}) collective-permute-start(bf16[256,128]{1,0:T(8,128)(2,1)S(1)} %get-tuple-element.30), channel_id=1, source_target_pairs={{0,8},{1,9},{2,10},{3,11},{4,12},{5,13},{6,14},{7,15},{8,0},{9,1},... | collective-permute-start | bytes 196616 | tf_op jit(solution)/shard_map/ppermute | solution.py:506
  20.1 1.7 %own.1 = (f32[256,384]{1,0:T(8,128)S(1)}, f32[256,128]{1,0:T(8,128)S(1)}) custom-call(bf16[128,384]{1,0:T(8,128)(2,1)S(1)} %get-tuple-element.21.query_ref, f32[256,384]{1,0:T(8,128)S(1)} %get-tuple-element.32.near_ref, f32[256,384]{1,0:T(8,128)S(1)} %get-tuple-element.24.rel_ref, f32[32,128]{1,0:T(8,128)S(1)} %get-tuple-element.33.old_ref, ...), custom_call_target="tpu_custom_call" | custom-call | flops 805306368 | bytes 786432 | tf_op jit(solution)/shard_map/own/pallas_call | solution.py:582
  21.8 4.3 %collective-permute-done.8.back_ref = bf16[256,128]{1,0:T(8,128)(2,1)S(1)} collective-permute-done((bf16[256,128]{1,0:T(8,128)(2,1)S(1)}, bf16[256,128]{1,0:T(8,128)(2,1)S(1)}, u32[]{:S(2)}, u32[]{:S(2)}) %collective-permute-start.8) | collective-permute-done | bytes 65568 | tf_op jit(solution)/shard_map/ppermute | solution.py:506
  26.1 0.0 copy-done
  26.1 2.1 %finish.1 = (bf16[256,3072]{1,0:T(8,128)(2,1)}, f32[2,3,2,128]{3,2,1,0:T(2,128)}) custom-call(bf16[256,128]{1,0:T(8,128)(2,1)S(1)} %collective-permute-done.8.back_ref, f32[16,128]{1,0:T(8,128)S(1)} %get-tuple-element.31.half_ref, f32[256,384]{1,0:T(8,128)S(1)} %get-tuple-element.36.merged_ref, f32[256,128]{1,0:T(8,128)S(1)} %get-tuple-element.37.log_ref, ...), custom_call_target="tpu_custom_call" | custom-call | tf_op jit(solution)/shard_map/finish/pallas_call | solution.py:596
Async XLA Ops:
  0.6 11.4 %copy-start.1 = (f32[3,128,32]{1,2,0:T(8,128)S(1)}, f32[3,128,32]{1,2,0:T(8,128)}, u32[]{:S(2)}) copy-start(f32[3,128,32]{1,2,0:T(8,128)} %param.16) | copy-start | bytes 147460
  0.6 11.4 %copy-start.2 = (f32[2,2,3,128]{3,1,2,0:T(2,128)S(1)}, f32[2,2,3,128]{3,1,2,0:T(2,128)}, u32[]{:S(2)}) copy-start(f32[2,2,3,128]{3,1,2,0:T(2,128)} %param.17) | copy-start | bytes 18436
  0.7 11.4 %copy-start.3 = (s32[2,3]{1,0:T(2,128)S(1)}, s32[2,3]{1,0:T(2,128)}, u32[]{:S(2)}) copy-start(s32[2,3]{1,0:T(2,128)} %refresh_ref.1) | copy-start | bytes 76
  5.9 8.9 %collective-permute-start.4 = (bf16[1,144,384]{2,1,0:T(8,128)(2,1)S(1)}, bf16[1,144,384]{2,1,0:T(8,128)(2,1)S(1)}, u32[]{:S(2)}, u32[]{:S(2)}) collective-permute-start(bf16[1,144,384]{2,1,0:T(8,128)(2,1)S(1)} %get-tuple-element.22.refs_0_), channel_id=1, source_target_pairs={{0,6},{1,7},{2,4},{3,5},{4,2},{5,3},{6,0},{7,1},{8,14},{9,15},{10,... | collective-permute-start | bytes 331784 | tf_op jit(solution)/shard_map/ppermute | solution.py:506
  7.5 7.7 %collective-permute-start.3 = (bf16[1,144,384]{2,1,0:T(8,128)(2,1)S(1)}, bf16[1,144,384]{2,1,0:T(8,128)(2,1)S(1)}, u32[]{:S(2)}, u32[]{:S(2)}) collective-permute-start(bf16[1,144,384]{2,1,0:T(8,128)(2,1)S(1)} %get-tuple-element.22.refs_0_), channel_id=1, source_target_pairs={{0,4},{1,5},{2,6},{3,7},{4,0},{5,1},{6,2},{7,3},{8,12},{9,13},{10,... | collective-permute-start | bytes 331784 | tf_op jit(solution)/shard_map/ppermute | solution.py:506
  7.9 7.5 %collective-permute-start.2 = (bf16[1,144,384]{2,1,0:T(8,128)(2,1)S(1)}, bf16[1,144,384]{2,1,0:T(8,128)(2,1)S(1)}, u32[]{:S(2)}, u32[]{:S(2)}) collective-permute-start(bf16[1,144,384]{2,1,0:T(8,128)(2,1)S(1)} %get-tuple-element.22.refs_0_), channel_id=1, source_target_pairs={{0,2},{1,3},{2,0},{3,1},{4,6},{5,7},{6,4},{7,5},{8,10},{9,11},{10,... | collective-permute-start | bytes 331784 | tf_op jit(solution)/shard_map/ppermute | solution.py:506
  9.4 8.2 %collective-permute-start.1 = (bf16[1,144,384]{2,1,0:T(8,128)(2,1)S(1)}, bf16[1,144,384]{2,1,0:T(8,128)(2,1)S(1)}, u32[]{:S(2)}, u32[]{:S(2)}) collective-permute-start(bf16[1,144,384]{2,1,0:T(8,128)(2,1)S(1)} %get-tuple-element.22.refs_0_), channel_id=1, source_target_pairs={{0,1},{1,0},{2,3},{3,2},{4,5},{5,4},{6,7},{7,6},{8,9},{9,8},{10,11... | collective-permute-start | bytes 331784 | tf_op jit(solution)/shard_map/ppermute | solution.py:506
  9.4 8.2 %collective-permute-start = (bf16[128,384]{1,0:T(8,128)(2,1)S(1)}, bf16[128,384]{1,0:T(8,128)(2,1)S(1)}, u32[]{:S(2)}, u32[]{:S(2)}) collective-permute-start(bf16[128,384]{1,0:T(8,128)(2,1)S(1)} %get-tuple-element.21.query_ref), channel_id=1, source_target_pairs={{0,8},{1,9},{2,10},{3,11},{4,12},{5,13},{6,14},{7,15},{8,0},{9,1},... | collective-permute-start | bytes 294920 | tf_op jit(solution)/shard_map/ppermute | solution.py:506
  14.8 3.8 %collective-permute-start.7 = (bf16[1,144,384]{2,1,0:T(8,128)(2,1)S(1)}, bf16[1,144,384]{2,1,0:T(8,128)(2,1)S(1)}, u32[]{:S(2)}, u32[]{:S(2)}) collective-permute-start(bf16[1,144,384]{2,1,0:T(8,128)(2,1)S(1)} %collective-permute-done.4.refs_4_.refs_3_), channel_id=1, source_target_pairs={{0,1},{1,0},{2,3},{3,2},{4,5},{5,4},{6,7},{7,6},{8,9},{9,8},{10,11... | collective-permute-start | bytes 331784 | tf_op jit(solution)/shard_map/ppermute | solution.py:506
  15.1 3.5 %collective-permute-start.6 = (bf16[1,144,384]{2,1,0:T(8,128)(2,1)S(1)}, bf16[1,144,384]{2,1,0:T(8,128)(2,1)S(1)}, u32[]{:S(2)}, u32[]{:S(2)}) collective-permute-start(bf16[1,144,384]{2,1,0:T(8,128)(2,1)S(1)} %collective-permute-done.3.refs_3_.refs_2_), channel_id=1, source_target_pairs={{0,1},{1,0},{2,3},{3,2},{4,5},{5,4},{6,7},{7,6},{8,9},{9,8},{10,11... | collective-permute-start | bytes 331784 | tf_op jit(solution)/shard_map/ppermute | solution.py:506
  15.4 3.2 %collective-permute-start.5 = (bf16[1,144,384]{2,1,0:T(8,128)(2,1)S(1)}, bf16[1,144,384]{2,1,0:T(8,128)(2,1)S(1)}, u32[]{:S(2)}, u32[]{:S(2)}) collective-permute-start(bf16[1,144,384]{2,1,0:T(8,128)(2,1)S(1)} %collective-permute-done.2.refs_2_.refs_1_), channel_id=1, source_target_pairs={{0,1},{1,0},{2,3},{3,2},{4,5},{5,4},{6,7},{7,6},{8,9},{9,8},{10,11... | collective-permute-start | bytes 331784 | tf_op jit(solution)/shard_map/ppermute | solution.py:506
  19.5 6.6 %copy-start = (bf16[384,3072]{1,0:T(8,128)(2,1)S(1)}, bf16[384,3072]{1,0:T(8,128)(2,1)}, u32[]{:S(2)}) copy-start(bf16[384,3072]{1,0:T(8,128)(2,1)} %w_ref.1) | copy-start | bytes 7077892
  19.5 6.6 %collective-permute-start.8 = (bf16[256,128]{1,0:T(8,128)(2,1)S(1)}, bf16[256,128]{1,0:T(8,128)(2,1)S(1)}, u32[]{:S(2)}, u32[]{:S(2)}) collective-permute-start(bf16[256,128]{1,0:T(8,128)(2,1)S(1)} %get-tuple-element.30), channel_id=1, source_target_pairs={{0,8},{1,9},{2,10},{3,11},{4,12},{5,13},{6,14},{7,15},{8,0},{9,1},... | collective-permute-start | bytes 196616 | tf_op jit(solution)/shard_map/ppermute | solution.py:506

commit v7 on v6

--- a/solution.py
+++ b/solution.py
@@ -537,7 +537,7 @@
         name="near",
     )(qkv, center_rows, refresh, value_rows)
 
-    for i in range(1, len(held)):
+    for i in (1,):
         x, _ = lax.optimization_barrier((held[i][0], rel))
         held[i] = (x, held[i][1])
     held.insert(1, (swap(payload, 1), [1]))

time: 28.4 us -> 27.1 us (0.954)
  the two profiles are of different devices: /device:TPU:6 before, /device:TPU:0 now
where the time goes in v7:
time: 27.1 us; the launch traced here: 26.8 us
  Pallas kernels  13.5 us (50%)
  starting transfers between devices  11.2 us (41%)
  waiting for transfers between devices  1.26 us (5%)
  between operations  0.74 us (3%)
    ppermute x9, starting transfers between devices, swap(): return lax.ppermute(x, 'seq', [(i, i ^ mask) for i in range(seq)])  11.2 us
    pallas_call x1, Pallas kernels, per_device(): pl.pallas_call(functools.partial(project_kernel, **sizes, rank=rank, log_...  5.21 us
    pallas_call x1, Pallas kernels, per_device(): pl.pallas_call(functools.partial(near_kernel, **sizes, rank=rank), in_spe...  2.79 us
    pallas_call x1, Pallas kernels, per_device(): pl.pallas_call(functools.partial(finish_kernel, **sizes, rank=rank, lengt...  2.13 us
    pallas_call x1, Pallas kernels, per_device(): pl.pallas_call(functools.partial(own_kernel, **sizes, rank=rank), in_spec...  1.64 us
    ppermute x9, waiting for transfers between devices, swap(): return lax.ppermute(x, 'seq', [(i, i ^ mask) for i in range(seq)])  1.26 us
    pallas_call x1, Pallas kernels, per_device(): pl.pallas_call(functools.partial(early_kernel, **sizes, rank=rank), in_sp...  0.98 us
    pallas_call x1, Pallas kernels, per_device(): pl.pallas_call(functools.partial(partner_kernel, **sizes, rank=rank, orde...  0.78 us
  transfers between devices with their start and end apart: 9, of which 4 were waited for; matrix products, arithmetic and copies ran while one was open for 0% of the time, Pallas kernels for 20%

profile of v7, /device:TPU:0, one launch (start us, length us, event | category | flops | bytes accessed | tf_op | source)
XLA Modules:
  0.0 26.8 jit_solution(6956353521730762532)
XLA Ops:
  0.6 0.0 copy-start.1
  0.6 0.0 copy-start.2
  0.7 0.0 copy-start.3
  0.7 5.2 %project.1 = (bf16[1,144,384]{2,1,0:T(8,128)(2,1)S(1)}, bf16[128,384]{1,0:T(8,128)(2,1)S(1)}, f32[256,1152]{1,0:T(8,128)S(1)}) custom-call(bf16[256,3072]{1,0:T(8,128)(2,1)} %bitcast.13, bf16[3072,1152]{1,0:T(8,128)(2,1)} %w_hbm.1, f32[9,128]{1,0:T(8,128)} %bitcast.15, f32[1,128]{1,0:T(1,128)} %bitcast.16, f32[1,128]{1,0:T(1,128)} %bitcast.17, ...), custom_call_target="tpu_custom_call" | custom-call | tf_op jit(solution)/shard_map/project/pallas_call | solution.py:468
  5.9 3.0 %collective-permute-start.2 = (bf16[1,144,384]{2,1,0:T(8,128)(2,1)S(1)}, bf16[1,144,384]{2,1,0:T(8,128)(2,1)S(1)}, u32[]{:S(2)}, u32[]{:S(2)}) collective-permute-start(bf16[1,144,384]{2,1,0:T(8,128)(2,1)S(1)} %get-tuple-element.20.refs_0_), channel_id=1, source_target_pairs={{0,2},{1,3},{2,0},{3,1},{4,6},{5,7},{6,4},{7,5},{8,10},{9,11},{10,... | collective-permute-start | bytes 331784 | tf_op jit(solution)/shard_map/ppermute | solution.py:506
  8.9 1.6 %collective-permute-start.3 = (bf16[1,144,384]{2,1,0:T(8,128)(2,1)S(1)}, bf16[1,144,384]{2,1,0:T(8,128)(2,1)S(1)}, u32[]{:S(2)}, u32[]{:S(2)}) collective-permute-start(bf16[1,144,384]{2,1,0:T(8,128)(2,1)S(1)} %get-tuple-element.20.refs_0_), channel_id=1, source_target_pairs={{0,4},{1,5},{2,6},{3,7},{4,0},{5,1},{6,2},{7,3},{8,12},{9,13},{10,... | collective-permute-start | bytes 331784 | tf_op jit(solution)/shard_map/ppermute | solution.py:506
  10.5 0.0 collective-permute-start.4
  10.5 0.0 collective-permute-start.1
  10.5 3.0 %collective-permute-start = (bf16[128,384]{1,0:T(8,128)(2,1)S(1)}, bf16[128,384]{1,0:T(8,128)(2,1)S(1)}, u32[]{:S(2)}, u32[]{:S(2)}) collective-permute-start(bf16[128,384]{1,0:T(8,128)(2,1)S(1)} %get-tuple-element.19.query_ref), channel_id=1, source_target_pairs={{0,8},{1,9},{2,10},{3,11},{4,12},{5,13},{6,14},{7,15},{8,0},{9,1},... | collective-permute-start | bytes 294920 | tf_op jit(solution)/shard_map/ppermute | solution.py:506
  13.5 0.0 copy-done.1
  13.5 0.0 copy-done.2
  13.5 0.0 copy-done.3
  13.5 2.8 %near.1 = (f32[256,384]{1,0:T(8,128)S(1)}, f32[256,384]{1,0:T(8,128)S(1)}, bf16[2,128,384]{2,1,0:T(8,128)(2,1)S(1)}, bf16[2,128,384]{2,1,0:T(8,128)(2,1)S(1)}, f32[32,128]{1,0:T(8,128)S(1)}) custom-call(f32[256,1152]{1,0:T(8,128)S(1)} %get-tuple-element.21.qkv_ref, f32[2,3,2,128]{3,2,1,0:T(2,128)S(1)} %bitcast.12, s32[2,3]{1,0:T(2,128)S(1)} %copy-done.3, ...), custom_call_target="tpu_custom_call" | custom-call | flops 15099494400 | bytes 19660800 | tf_op jit(solution)/shard_map/near/pallas_call | solution.py:522
  16.3 0.0 collective-permute-done.2.refs_2_.refs_1_
  16.3 0.3 %collective-permute-start.5 = (bf16[1,144,384]{2,1,0:T(8,128)(2,1)S(1)}, bf16[1,144,384]{2,1,0:T(8,128)(2,1)S(1)}, u32[]{:S(2)}, u32[]{:S(2)}) collective-permute-start(bf16[1,144,384]{2,1,0:T(8,128)(2,1)S(1)} %collective-permute-done.2.refs_2_.refs_1_), channel_id=1, source_target_pairs={{0,1},{1,0},{2,3},{3,2},{4,5},{5,4},{6,7},{7,6},{8,9},{9,8},{10,11... | collective-permute-start | bytes 331784 | tf_op jit(solution)/shard_map/ppermute | solution.py:506
  16.6 0.0 collective-permute-done.3.refs_3_.refs_2_
  16.6 0.3 %collective-permute-start.6 = (bf16[1,144,384]{2,1,0:T(8,128)(2,1)S(1)}, bf16[1,144,384]{2,1,0:T(8,128)(2,1)S(1)}, u32[]{:S(2)}, u32[]{:S(2)}) collective-permute-start(bf16[1,144,384]{2,1,0:T(8,128)(2,1)S(1)} %collective-permute-done.3.refs_3_.refs_2_), channel_id=1, source_target_pairs={{0,1},{1,0},{2,3},{3,2},{4,5},{5,4},{6,7},{7,6},{8,9},{9,8},{10,11... | collective-permute-start | bytes 331784 | tf_op jit(solution)/shard_map/ppermute | solution.py:506
  16.9 0.4 %collective-permute-done.4.refs_4_.refs_3_ = bf16[1,144,384]{2,1,0:T(8,128)(2,1)S(1)} collective-permute-done((bf16[1,144,384]{2,1,0:T(8,128)(2,1)S(1)}, bf16[1,144,384]{2,1,0:T(8,128)(2,1)S(1)}, u32[]{:S(2)}, u32[]{:S(2)}) %collective-permute-start.4) | collective-permute-done | bytes 110624 | tf_op jit(solution)/shard_map/ppermute | solution.py:506
  17.2 0.0 collective-permute-start.7
  17.2 0.2 collective-permute-done.query_ref
  17.4 0.0 collective-permute-done.1.refs_1_.refs_0_
  17.4 1.0 %early.1 = (f32[256,128]{1,0:T(8,128)S(1)}, f32[256,128]{1,0:T(8,128)S(1)}) custom-call(bf16[128,384]{1,0:T(8,128)(2,1)S(1)} %collective-permute-done.query_ref, bf16[1,144,384]{2,1,0:T(8,128)(2,1)S(1)} %get-tuple-element.20.refs_0_, bf16[1,144,384]{2,1,0:T(8,128)(2,1)S(1)} %collective-permute-done.1.refs_1_.refs_0_, ...), custom_call_target="tpu_custom_call" | custom-call | flops 503316480 | bytes 491520 | tf_op jit(solution)/shard_map/early/pallas_call | solution.py:558
  18.4 0.0 collective-permute-done.5.refs_5_.refs_4_
  18.4 0.0 collective-permute-done.6.refs_6_.refs_5_
  18.5 0.1 collective-permute-done.7.refs_7_.refs_6_
  18.5 0.8 %partner.1 = (bf16[256,128]{1,0:T(8,128)(2,1)S(1)}, f32[16,128]{1,0:T(8,128)S(1)}) custom-call(bf16[128,384]{1,0:T(8,128)(2,1)S(1)} %collective-permute-done.query_ref, f32[256,128]{1,0:T(8,128)S(1)} %get-tuple-element.24.part_ref, f32[256,128]{1,0:T(8,128)S(1)} %get-tuple-element.25.part_log_ref, bf16[1,144,384]{2,1,0:T(8,128)(2,1)S(1)} %get-tuple-element.20.refs_0_, ...), custom_call_target="tpu_custom_call" | custom-call | flops 805306368 | bytes 786432 | tf_op jit(solution)/shard_map/partner/pallas_call | solution.py:567
  19.3 0.0 copy-start
  19.3 3.0 %collective-permute-start.8 = (bf16[256,128]{1,0:T(8,128)(2,1)S(1)}, bf16[256,128]{1,0:T(8,128)(2,1)S(1)}, u32[]{:S(2)}, u32[]{:S(2)}) collective-permute-start(bf16[256,128]{1,0:T(8,128)(2,1)S(1)} %get-tuple-element.26), channel_id=1, source_target_pairs={{0,8},{1,9},{2,10},{3,11},{4,12},{5,13},{6,14},{7,15},{8,0},{9,1},... | collective-permute-start | bytes 196616 | tf_op jit(solution)/shard_map/ppermute | solution.py:506
  22.4 1.6 %own.1 = (f32[256,384]{1,0:T(8,128)S(1)}, f32[256,128]{1,0:T(8,128)S(1)}) custom-call(bf16[128,384]{1,0:T(8,128)(2,1)S(1)} %get-tuple-element.19.query_ref, f32[256,384]{1,0:T(8,128)S(1)} %get-tuple-element.28.near_ref, f32[256,384]{1,0:T(8,128)S(1)} %get-tuple-element.22.rel_ref, f32[32,128]{1,0:T(8,128)S(1)} %get-tuple-element.29.old_ref, ...), custom_call_target="tpu_custom_call" | custom-call | flops 805306368 | bytes 786432 | tf_op jit(solution)/shard_map/own/pallas_call | solution.py:582
  24.0 0.6 %collective-permute-done.8.back_ref = bf16[256,128]{1,0:T(8,128)(2,1)S(1)} collective-permute-done((bf16[256,128]{1,0:T(8,128)(2,1)S(1)}, bf16[256,128]{1,0:T(8,128)(2,1)S(1)}, u32[]{:S(2)}, u32[]{:S(2)}) %collective-permute-start.8) | collective-permute-done | bytes 65568 | tf_op jit(solution)/shard_map/ppermute | solution.py:506
  24.6 0.0 copy-done
  24.6 2.1 %finish.1 = (bf16[256,3072]{1,0:T(8,128)(2,1)}, f32[2,3,2,128]{3,2,1,0:T(2,128)}) custom-call(bf16[256,128]{1,0:T(8,128)(2,1)S(1)} %collective-permute-done.8.back_ref, f32[16,128]{1,0:T(8,128)S(1)} %get-tuple-element.27.half_ref, f32[256,384]{1,0:T(8,128)S(1)} %get-tuple-element.32.merged_ref, f32[256,128]{1,0:T(8,128)S(1)} %get-tuple-element.33.log_ref, ...), custom_call_target="tpu_custom_call" | custom-call | tf_op jit(solution)/shard_map/finish/pallas_call | solution.py:596
Async XLA Ops:
  0.6 12.8 %copy-start.1 = (f32[3,128,32]{1,2,0:T(8,128)S(1)}, f32[3,128,32]{1,2,0:T(8,128)}, u32[]{:S(2)}) copy-start(f32[3,128,32]{1,2,0:T(8,128)} %param.16) | copy-start | bytes 147460
  0.6 12.8 %copy-start.2 = (f32[2,2,3,128]{3,1,2,0:T(2,128)S(1)}, f32[2,2,3,128]{3,1,2,0:T(2,128)}, u32[]{:S(2)}) copy-start(f32[2,2,3,128]{3,1,2,0:T(2,128)} %param.17) | copy-start | bytes 18436
  0.7 12.8 %copy-start.3 = (s32[2,3]{1,0:T(2,128)S(1)}, s32[2,3]{1,0:T(2,128)}, u32[]{:S(2)}) copy-start(s32[2,3]{1,0:T(2,128)} %refresh_ref.1) | copy-start | bytes 76
  5.9 10.4 %collective-permute-start.2 = (bf16[1,144,384]{2,1,0:T(8,128)(2,1)S(1)}, bf16[1,144,384]{2,1,0:T(8,128)(2,1)S(1)}, u32[]{:S(2)}, u32[]{:S(2)}) collective-permute-start(bf16[1,144,384]{2,1,0:T(8,128)(2,1)S(1)} %get-tuple-element.20.refs_0_), channel_id=1, source_target_pairs={{0,2},{1,3},{2,0},{3,1},{4,6},{5,7},{6,4},{7,5},{8,10},{9,11},{10,... | collective-permute-start | bytes 331784 | tf_op jit(solution)/shard_map/ppermute | solution.py:506
  8.9 7.7 %collective-permute-start.3 = (bf16[1,144,384]{2,1,0:T(8,128)(2,1)S(1)}, bf16[1,144,384]{2,1,0:T(8,128)(2,1)S(1)}, u32[]{:S(2)}, u32[]{:S(2)}) collective-permute-start(bf16[1,144,384]{2,1,0:T(8,128)(2,1)S(1)} %get-tuple-element.20.refs_0_), channel_id=1, source_target_pairs={{0,4},{1,5},{2,6},{3,7},{4,0},{5,1},{6,2},{7,3},{8,12},{9,13},{10,... | collective-permute-start | bytes 331784 | tf_op jit(solution)/shard_map/ppermute | solution.py:506
  10.5 6.7 %collective-permute-start.4 = (bf16[1,144,384]{2,1,0:T(8,128)(2,1)S(1)}, bf16[1,144,384]{2,1,0:T(8,128)(2,1)S(1)}, u32[]{:S(2)}, u32[]{:S(2)}) collective-permute-start(bf16[1,144,384]{2,1,0:T(8,128)(2,1)S(1)} %get-tuple-element.20.refs_0_), channel_id=1, source_target_pairs={{0,6},{1,7},{2,4},{3,5},{4,2},{5,3},{6,0},{7,1},{8,14},{9,15},{10,... | collective-permute-start | bytes 331784 | tf_op jit(solution)/shard_map/ppermute | solution.py:506
  10.5 7.0 %collective-permute-start.1 = (bf16[1,144,384]{2,1,0:T(8,128)(2,1)S(1)}, bf16[1,144,384]{2,1,0:T(8,128)(2,1)S(1)}, u32[]{:S(2)}, u32[]{:S(2)}) collective-permute-start(bf16[1,144,384]{2,1,0:T(8,128)(2,1)S(1)} %get-tuple-element.20.refs_0_), channel_id=1, source_target_pairs={{0,1},{1,0},{2,3},{3,2},{4,5},{5,4},{6,7},{7,6},{8,9},{9,8},{10,11... | collective-permute-start | bytes 331784 | tf_op jit(solution)/shard_map/ppermute | solution.py:506
  10.5 6.9 %collective-permute-start = (bf16[128,384]{1,0:T(8,128)(2,1)S(1)}, bf16[128,384]{1,0:T(8,128)(2,1)S(1)}, u32[]{:S(2)}, u32[]{:S(2)}) collective-permute-start(bf16[128,384]{1,0:T(8,128)(2,1)S(1)} %get-tuple-element.19.query_ref), channel_id=1, source_target_pairs={{0,8},{1,9},{2,10},{3,11},{4,12},{5,13},{6,14},{7,15},{8,0},{9,1},... | collective-permute-start | bytes 294920 | tf_op jit(solution)/shard_map/ppermute | solution.py:506
  16.3 2.2 %collective-permute-start.5 = (bf16[1,144,384]{2,1,0:T(8,128)(2,1)S(1)}, bf16[1,144,384]{2,1,0:T(8,128)(2,1)S(1)}, u32[]{:S(2)}, u32[]{:S(2)}) collective-permute-start(bf16[1,144,384]{2,1,0:T(8,128)(2,1)S(1)} %collective-permute-done.2.refs_2_.refs_1_), channel_id=1, source_target_pairs={{0,1},{1,0},{2,3},{3,2},{4,5},{5,4},{6,7},{7,6},{8,9},{9,8},{10,11... | collective-permute-start | bytes 331784 | tf_op jit(solution)/shard_map/ppermute | solution.py:506
  16.6 1.9 %collective-permute-start.6 = (bf16[1,144,384]{2,1,0:T(8,128)(2,1)S(1)}, bf16[1,144,384]{2,1,0:T(8,128)(2,1)S(1)}, u32[]{:S(2)}, u32[]{:S(2)}) collective-permute-start(bf16[1,144,384]{2,1,0:T(8,128)(2,1)S(1)} %collective-permute-done.3.refs_3_.refs_2_), channel_id=1, source_target_pairs={{0,1},{1,0},{2,3},{3,2},{4,5},{5,4},{6,7},{7,6},{8,9},{9,8},{10,11... | collective-permute-start | bytes 331784 | tf_op jit(solution)/shard_map/ppermute | solution.py:506
  17.2 1.3 %collective-permute-start.7 = (bf16[1,144,384]{2,1,0:T(8,128)(2,1)S(1)}, bf16[1,144,384]{2,1,0:T(8,128)(2,1)S(1)}, u32[]{:S(2)}, u32[]{:S(2)}) collective-permute-start(bf16[1,144,384]{2,1,0:T(8,128)(2,1)S(1)} %collective-permute-done.4.refs_4_.refs_3_), channel_id=1, source_target_pairs={{0,1},{1,0},{2,3},{3,2},{4,5},{5,4},{6,7},{7,6},{8,9},{9,8},{10,11... | collective-permute-start | bytes 331784 | tf_op jit(solution)/shard_map/ppermute | solution.py:506
  19.3 5.3 %copy-start = (bf16[384,3072]{1,0:T(8,128)(2,1)S(1)}, bf16[384,3072]{1,0:T(8,128)(2,1)}, u32[]{:S(2)}) copy-start(bf16[384,3072]{1,0:T(8,128)(2,1)} %w_ref.1) | copy-start | bytes 7077892
  19.3 5.3 %collective-permute-start.8 = (bf16[256,128]{1,0:T(8,128)(2,1)S(1)}, bf16[256,128]{1,0:T(8,128)(2,1)S(1)}, u32[]{:S(2)}, u32[]{:S(2)}) collective-permute-start(bf16[256,128]{1,0:T(8,128)(2,1)S(1)} %get-tuple-element.26), channel_id=1, source_target_pairs={{0,8},{1,9},{2,10},{3,11},{4,12},{5,13},{6,14},{7,15},{8,0},{9,1},... | collective-permute-start | bytes 196616 | tf_op jit(solution)/shard_map/ppermute | solution.py:506

commit v8 on v7

--- a/solution.py
+++ b/solution.py
@@ -405,7 +405,7 @@
     mixed_hbm, new_hbm, attended_ref, mixed_ref, new_ref, sem, new_sem,
     *, samples, tokens, heads, dim, rank, length,
 ):
-    chunks, columns = mixed_ref.shape[1], mixed_ref.shape[3]
+    chunks, columns = mixed_ref.shape[0], mixed_ref.shape[2]
     copies = []
     sums = jnp.zeros((tokens, dim), f32)
     for b in range(samples):
@@ -423,22 +423,20 @@
             near = merged_ref[rows, head]
             value = far[:, head] + old_ref[row : row + 1, :] - near
             attended_ref[rows, head] = (near + value * share[:, at : at + 1]).astype(bf16)
-        for c in range(chunks):
-            place = slice(c * columns, (c + 1) * columns)
-            mixed_ref[b, c] = dot(attended_ref[rows, :], w_ref[:, place]).astype(bf16)
-            copy = pltpu.make_async_copy(
-                mixed_ref.at[b, c], mixed_hbm.at[rows, place], sem.at[b, c]
-            )
-            copy.start()
-            copies.append(copy)
-    fresh = (half_ref[...] + sums.T[:SUM_ROWS, :]) * (1.0 / length)
-    fresh = jnp.where(old_ref[SUM_ROWS:, :] > 0.5, old_ref[:SUM_ROWS, :], fresh)
-    for b in range(samples):
-        for h in range(heads):
-            row = (b * heads + h) * 2
-            new_ref[b, h] = fresh[row : row + 2, :]
-    copies.append(pltpu.make_async_copy(new_ref, new_hbm, new_sem.at[0]))
-    copies[-1].start()
+    for c in range(chunks):
+        place = slice(c * columns, (c + 1) * columns)
+        mixed_ref[c] = dot(attended_ref[...], w_ref[:, place]).astype(bf16)
+        copies.append(pltpu.make_async_copy(mixed_ref.at[c], mixed_hbm.at[:, place], sem.at[c]))
+        copies[-1].start()
+        if c == 1:
+            fresh = (half_ref[...] + sums.T[:SUM_ROWS, :]) * (1.0 / length)
+            fresh = jnp.where(old_ref[SUM_ROWS:, :] > 0.5, old_ref[:SUM_ROWS, :], fresh)
+            for b in range(samples):
+                for h in range(heads):
+                    row = (b * heads + h) * 2
+                    new_ref[b, h] = fresh[row : row + 2, :]
+            copies.append(pltpu.make_async_copy(new_ref, new_hbm, new_sem.at[0]))
+            copies[-1].start()
     for copy in copies:
         copy.wait()
 
@@ -592,7 +590,7 @@
         name="own",
     )(query, near, rel, old, basis_high, basis_low, *arrays[1:])
 
-    columns = 768
+    columns = 512
     mixed, new_centers = pl.pallas_call(
         functools.partial(finish_kernel, **sizes, rank=rank, length=tokens * seq),
         in_specs=[VMEM] * 8,
@@ -603,9 +601,9 @@
         ],
         scratch_shapes=[
             pltpu.VMEM((rows, width), bf16),
-            pltpu.VMEM((samples, model // columns, tokens, columns), bf16),
+            pltpu.VMEM((model // columns, rows, columns), bf16),
             pltpu.VMEM((samples, heads, 2, dim), f32),
-            pltpu.SemaphoreType.DMA((samples, model // columns)),
+            pltpu.SemaphoreType.DMA((model // columns,)),
             pltpu.SemaphoreType.DMA((1,)),
         ],
         compiler_params=params(24),

time: 27.1 us -> 26.9 us (level)
  no operation moved by 1% of the time
where the time goes in v8:
time: 26.9 us; the launch traced here: 26.6 us
  Pallas kernels  13.4 us (50%)
  starting transfers between devices  11.2 us (42%)
  waiting for transfers between devices  1.26 us (5%)
  between operations  0.74 us (3%)
    ppermute x9, starting transfers between devices, swap(): return lax.ppermute(x, 'seq', [(i, i ^ mask) for i in range(seq)])  11.2 us
    pallas_call x1, Pallas kernels, per_device(): pl.pallas_call(functools.partial(project_kernel, **sizes, rank=rank, log_...  5.21 us
    pallas_call x1, Pallas kernels, per_device(): pl.pallas_call(functools.partial(near_kernel, **sizes, rank=rank), in_spe...  2.79 us
    pallas_call x1, Pallas kernels, per_device(): pl.pallas_call(functools.partial(finish_kernel, **sizes, rank=rank, lengt...  1.99 us
    pallas_call x1, Pallas kernels, per_device(): pl.pallas_call(functools.partial(own_kernel, **sizes, rank=rank), in_spec...  1.64 us
    ppermute x9, waiting for transfers between devices, swap(): return lax.ppermute(x, 'seq', [(i, i ^ mask) for i in range(seq)])  1.26 us
    pallas_call x1, Pallas kernels, per_device(): pl.pallas_call(functools.partial(early_kernel, **sizes, rank=rank), in_sp...  0.98 us
    pallas_call x1, Pallas kernels, per_device(): pl.pallas_call(functools.partial(partner_kernel, **sizes, rank=rank, orde...  0.78 us
  transfers between devices with their start and end apart: 9, of which 4 were waited for; matrix products, arithmetic and copies ran while one was open for 0% of the time, Pallas kernels for 20%

profile of v8, /device:TPU:0, one launch (start us, length us, event | category | flops | bytes accessed | tf_op | source)
XLA Modules:
  0.0 26.6 jit_solution(599266518299447584)
XLA Ops:
  0.6 0.0 copy-start.1
  0.6 0.0 copy-start.2
  0.7 0.0 copy-start.3
  0.7 5.2 %project.1 = (bf16[1,144,384]{2,1,0:T(8,128)(2,1)S(1)}, bf16[128,384]{1,0:T(8,128)(2,1)S(1)}, f32[256,1152]{1,0:T(8,128)S(1)}) custom-call(bf16[256,3072]{1,0:T(8,128)(2,1)} %bitcast.13, bf16[3072,1152]{1,0:T(8,128)(2,1)} %w_hbm.1, f32[9,128]{1,0:T(8,128)} %bitcast.15, f32[1,128]{1,0:T(1,128)} %bitcast.16, f32[1,128]{1,0:T(1,128)} %bitcast.17, ...), custom_call_target="tpu_custom_call" | custom-call | tf_op jit(solution)/shard_map/project/pallas_call | solution.py:466
  5.9 3.0 %collective-permute-start.2 = (bf16[1,144,384]{2,1,0:T(8,128)(2,1)S(1)}, bf16[1,144,384]{2,1,0:T(8,128)(2,1)S(1)}, u32[]{:S(2)}, u32[]{:S(2)}) collective-permute-start(bf16[1,144,384]{2,1,0:T(8,128)(2,1)S(1)} %get-tuple-element.20.refs_0_), channel_id=1, source_target_pairs={{0,2},{1,3},{2,0},{3,1},{4,6},{5,7},{6,4},{7,5},{8,10},{9,11},{10,... | collective-permute-start | bytes 331784 | tf_op jit(solution)/shard_map/ppermute | solution.py:504
  8.9 1.6 %collective-permute-start.3 = (bf16[1,144,384]{2,1,0:T(8,128)(2,1)S(1)}, bf16[1,144,384]{2,1,0:T(8,128)(2,1)S(1)}, u32[]{:S(2)}, u32[]{:S(2)}) collective-permute-start(bf16[1,144,384]{2,1,0:T(8,128)(2,1)S(1)} %get-tuple-element.20.refs_0_), channel_id=1, source_target_pairs={{0,4},{1,5},{2,6},{3,7},{4,0},{5,1},{6,2},{7,3},{8,12},{9,13},{10,... | collective-permute-start | bytes 331784 | tf_op jit(solution)/shard_map/ppermute | solution.py:504
  10.5 0.0 collective-permute-start.4
  10.5 0.0 collective-permute-start.1
  10.5 3.0 %collective-permute-start = (bf16[128,384]{1,0:T(8,128)(2,1)S(1)}, bf16[128,384]{1,0:T(8,128)(2,1)S(1)}, u32[]{:S(2)}, u32[]{:S(2)}) collective-permute-start(bf16[128,384]{1,0:T(8,128)(2,1)S(1)} %get-tuple-element.19.query_ref), channel_id=1, source_target_pairs={{0,8},{1,9},{2,10},{3,11},{4,12},{5,13},{6,14},{7,15},{8,0},{9,1},... | collective-permute-start | bytes 294920 | tf_op jit(solution)/shard_map/ppermute | solution.py:504
  13.5 0.0 copy-done.1
  13.5 0.0 copy-done.2
  13.5 0.0 copy-done.3
  13.5 2.8 %near.1 = (f32[256,384]{1,0:T(8,128)S(1)}, f32[256,384]{1,0:T(8,128)S(1)}, bf16[2,128,384]{2,1,0:T(8,128)(2,1)S(1)}, bf16[2,128,384]{2,1,0:T(8,128)(2,1)S(1)}, f32[32,128]{1,0:T(8,128)S(1)}) custom-call(f32[256,1152]{1,0:T(8,128)S(1)} %get-tuple-element.21.qkv_ref, f32[2,3,2,128]{3,2,1,0:T(2,128)S(1)} %bitcast.12, s32[2,3]{1,0:T(2,128)S(1)} %copy-done.3, ...), custom_call_target="tpu_custom_call" | custom-call | flops 15099494400 | bytes 19660800 | tf_op jit(solution)/shard_map/near/pallas_call | solution.py:520
  16.3 0.0 collective-permute-done.2.refs_2_.refs_1_
  16.3 0.3 %collective-permute-start.5 = (bf16[1,144,384]{2,1,0:T(8,128)(2,1)S(1)}, bf16[1,144,384]{2,1,0:T(8,128)(2,1)S(1)}, u32[]{:S(2)}, u32[]{:S(2)}) collective-permute-start(bf16[1,144,384]{2,1,0:T(8,128)(2,1)S(1)} %collective-permute-done.2.refs_2_.refs_1_), channel_id=1, source_target_pairs={{0,1},{1,0},{2,3},{3,2},{4,5},{5,4},{6,7},{7,6},{8,9},{9,8},{10,11... | collective-permute-start | bytes 331784 | tf_op jit(solution)/shard_map/ppermute | solution.py:504
  16.6 0.0 collective-permute-done.3.refs_3_.refs_2_
  16.6 0.3 %collective-permute-start.6 = (bf16[1,144,384]{2,1,0:T(8,128)(2,1)S(1)}, bf16[1,144,384]{2,1,0:T(8,128)(2,1)S(1)}, u32[]{:S(2)}, u32[]{:S(2)}) collective-permute-start(bf16[1,144,384]{2,1,0:T(8,128)(2,1)S(1)} %collective-permute-done.3.refs_3_.refs_2_), channel_id=1, source_target_pairs={{0,1},{1,0},{2,3},{3,2},{4,5},{5,4},{6,7},{7,6},{8,9},{9,8},{10,11... | collective-permute-start | bytes 331784 | tf_op jit(solution)/shard_map/ppermute | solution.py:504
  16.9 0.4 %collective-permute-done.4.refs_4_.refs_3_ = bf16[1,144,384]{2,1,0:T(8,128)(2,1)S(1)} collective-permute-done((bf16[1,144,384]{2,1,0:T(8,128)(2,1)S(1)}, bf16[1,144,384]{2,1,0:T(8,128)(2,1)S(1)}, u32[]{:S(2)}, u32[]{:S(2)}) %collective-permute-start.4) | collective-permute-done | bytes 110624 | tf_op jit(solution)/shard_map/ppermute | solution.py:504
  17.2 0.0 collective-permute-start.7
  17.2 0.2 collective-permute-done.query_ref
  17.4 0.0 collective-permute-done.1.refs_1_.refs_0_
  17.4 1.0 %early.1 = (f32[256,128]{1,0:T(8,128)S(1)}, f32[256,128]{1,0:T(8,128)S(1)}) custom-call(bf16[128,384]{1,0:T(8,128)(2,1)S(1)} %collective-permute-done.query_ref, bf16[1,144,384]{2,1,0:T(8,128)(2,1)S(1)} %get-tuple-element.20.refs_0_, bf16[1,144,384]{2,1,0:T(8,128)(2,1)S(1)} %collective-permute-done.1.refs_1_.refs_0_, ...), custom_call_target="tpu_custom_call" | custom-call | flops 503316480 | bytes 491520 | tf_op jit(solution)/shard_map/early/pallas_call | solution.py:556
  18.4 0.0 collective-permute-done.5.refs_5_.refs_4_
  18.4 0.0 collective-permute-done.6.refs_6_.refs_5_
  18.5 0.1 collective-permute-done.7.refs_7_.refs_6_
  18.5 0.8 %partner.1 = (bf16[256,128]{1,0:T(8,128)(2,1)S(1)}, f32[16,128]{1,0:T(8,128)S(1)}) custom-call(bf16[128,384]{1,0:T(8,128)(2,1)S(1)} %collective-permute-done.query_ref, f32[256,128]{1,0:T(8,128)S(1)} %get-tuple-element.24.part_ref, f32[256,128]{1,0:T(8,128)S(1)} %get-tuple-element.25.part_log_ref, bf16[1,144,384]{2,1,0:T(8,128)(2,1)S(1)} %get-tuple-element.20.refs_0_, ...), custom_call_target="tpu_custom_call" | custom-call | flops 805306368 | bytes 786432 | tf_op jit(solution)/shard_map/partner/pallas_call | solution.py:565
  19.3 0.0 copy-start
  19.3 3.0 %collective-permute-start.8 = (bf16[256,128]{1,0:T(8,128)(2,1)S(1)}, bf16[256,128]{1,0:T(8,128)(2,1)S(1)}, u32[]{:S(2)}, u32[]{:S(2)}) collective-permute-start(bf16[256,128]{1,0:T(8,128)(2,1)S(1)} %get-tuple-element.26), channel_id=1, source_target_pairs={{0,8},{1,9},{2,10},{3,11},{4,12},{5,13},{6,14},{7,15},{8,0},{9,1},... | collective-permute-start | bytes 196616 | tf_op jit(solution)/shard_map/ppermute | solution.py:504
  22.4 1.6 %own.1 = (f32[256,384]{1,0:T(8,128)S(1)}, f32[256,128]{1,0:T(8,128)S(1)}) custom-call(bf16[128,384]{1,0:T(8,128)(2,1)S(1)} %get-tuple-element.19.query_ref, f32[256,384]{1,0:T(8,128)S(1)} %get-tuple-element.28.near_ref, f32[256,384]{1,0:T(8,128)S(1)} %get-tuple-element.22.rel_ref, f32[32,128]{1,0:T(8,128)S(1)} %get-tuple-element.29.old_ref, ...), custom_call_target="tpu_custom_call" | custom-call | flops 805306368 | bytes 786432 | tf_op jit(solution)/shard_map/own/pallas_call | solution.py:580
  24.0 0.6 %collective-permute-done.8.back_ref = bf16[256,128]{1,0:T(8,128)(2,1)S(1)} collective-permute-done((bf16[256,128]{1,0:T(8,128)(2,1)S(1)}, bf16[256,128]{1,0:T(8,128)(2,1)S(1)}, u32[]{:S(2)}, u32[]{:S(2)}) %collective-permute-start.8) | collective-permute-done | bytes 65568 | tf_op jit(solution)/shard_map/ppermute | solution.py:504
  24.6 0.0 copy-done
  24.6 2.0 %finish.1 = (bf16[256,3072]{1,0:T(8,128)(2,1)}, f32[2,3,2,128]{3,2,1,0:T(2,128)}) custom-call(bf16[256,128]{1,0:T(8,128)(2,1)S(1)} %collective-permute-done.8.back_ref, f32[16,128]{1,0:T(8,128)S(1)} %get-tuple-element.27.half_ref, f32[256,384]{1,0:T(8,128)S(1)} %get-tuple-element.32.merged_ref, f32[256,128]{1,0:T(8,128)S(1)} %get-tuple-element.33.log_ref, ...), custom_call_target="tpu_custom_call" | custom-call | tf_op jit(solution)/shard_map/finish/pallas_call | solution.py:594
Async XLA Ops:
  0.6 12.8 %copy-start.1 = (f32[3,128,32]{1,2,0:T(8,128)S(1)}, f32[3,128,32]{1,2,0:T(8,128)}, u32[]{:S(2)}) copy-start(f32[3,128,32]{1,2,0:T(8,128)} %param.16) | copy-start | bytes 147460
  0.6 12.8 %copy-start.2 = (f32[2,2,3,128]{3,1,2,0:T(2,128)S(1)}, f32[2,2,3,128]{3,1,2,0:T(2,128)}, u32[]{:S(2)}) copy-start(f32[2,2,3,128]{3,1,2,0:T(2,128)} %param.17) | copy-start | bytes 18436
  0.7 12.8 %copy-start.3 = (s32[2,3]{1,0:T(2,128)S(1)}, s32[2,3]{1,0:T(2,128)}, u32[]{:S(2)}) copy-start(s32[2,3]{1,0:T(2,128)} %refresh_ref.1) | copy-start | bytes 76
  5.9 10.4 %collective-permute-start.2 = (bf16[1,144,384]{2,1,0:T(8,128)(2,1)S(1)}, bf16[1,144,384]{2,1,0:T(8,128)(2,1)S(1)}, u32[]{:S(2)}, u32[]{:S(2)}) collective-permute-start(bf16[1,144,384]{2,1,0:T(8,128)(2,1)S(1)} %get-tuple-element.20.refs_0_), channel_id=1, source_target_pairs={{0,2},{1,3},{2,0},{3,1},{4,6},{5,7},{6,4},{7,5},{8,10},{9,11},{10,... | collective-permute-start | bytes 331784 | tf_op jit(solution)/shard_map/ppermute | solution.py:504
  8.9 7.7 %collective-permute-start.3 = (bf16[1,144,384]{2,1,0:T(8,128)(2,1)S(1)}, bf16[1,144,384]{2,1,0:T(8,128)(2,1)S(1)}, u32[]{:S(2)}, u32[]{:S(2)}) collective-permute-start(bf16[1,144,384]{2,1,0:T(8,128)(2,1)S(1)} %get-tuple-element.20.refs_0_), channel_id=1, source_target_pairs={{0,4},{1,5},{2,6},{3,7},{4,0},{5,1},{6,2},{7,3},{8,12},{9,13},{10,... | collective-permute-start | bytes 331784 | tf_op jit(solution)/shard_map/ppermute | solution.py:504
  10.5 6.7 %collective-permute-start.4 = (bf16[1,144,384]{2,1,0:T(8,128)(2,1)S(1)}, bf16[1,144,384]{2,1,0:T(8,128)(2,1)S(1)}, u32[]{:S(2)}, u32[]{:S(2)}) collective-permute-start(bf16[1,144,384]{2,1,0:T(8,128)(2,1)S(1)} %get-tuple-element.20.refs_0_), channel_id=1, source_target_pairs={{0,6},{1,7},{2,4},{3,5},{4,2},{5,3},{6,0},{7,1},{8,14},{9,15},{10,... | collective-permute-start | bytes 331784 | tf_op jit(solution)/shard_map/ppermute | solution.py:504
  10.5 7.0 %collective-permute-start.1 = (bf16[1,144,384]{2,1,0:T(8,128)(2,1)S(1)}, bf16[1,144,384]{2,1,0:T(8,128)(2,1)S(1)}, u32[]{:S(2)}, u32[]{:S(2)}) collective-permute-start(bf16[1,144,384]{2,1,0:T(8,128)(2,1)S(1)} %get-tuple-element.20.refs_0_), channel_id=1, source_target_pairs={{0,1},{1,0},{2,3},{3,2},{4,5},{5,4},{6,7},{7,6},{8,9},{9,8},{10,11... | collective-permute-start | bytes 331784 | tf_op jit(solution)/shard_map/ppermute | solution.py:504
  10.5 6.9 %collective-permute-start = (bf16[128,384]{1,0:T(8,128)(2,1)S(1)}, bf16[128,384]{1,0:T(8,128)(2,1)S(1)}, u32[]{:S(2)}, u32[]{:S(2)}) collective-permute-start(bf16[128,384]{1,0:T(8,128)(2,1)S(1)} %get-tuple-element.19.query_ref), channel_id=1, source_target_pairs={{0,8},{1,9},{2,10},{3,11},{4,12},{5,13},{6,14},{7,15},{8,0},{9,1},... | collective-permute-start | bytes 294920 | tf_op jit(solution)/shard_map/ppermute | solution.py:504
  16.3 2.2 %collective-permute-start.5 = (bf16[1,144,384]{2,1,0:T(8,128)(2,1)S(1)}, bf16[1,144,384]{2,1,0:T(8,128)(2,1)S(1)}, u32[]{:S(2)}, u32[]{:S(2)}) collective-permute-start(bf16[1,144,384]{2,1,0:T(8,128)(2,1)S(1)} %collective-permute-done.2.refs_2_.refs_1_), channel_id=1, source_target_pairs={{0,1},{1,0},{2,3},{3,2},{4,5},{5,4},{6,7},{7,6},{8,9},{9,8},{10,11... | collective-permute-start | bytes 331784 | tf_op jit(solution)/shard_map/ppermute | solution.py:504
  16.6 1.9 %collective-permute-start.6 = (bf16[1,144,384]{2,1,0:T(8,128)(2,1)S(1)}, bf16[1,144,384]{2,1,0:T(8,128)(2,1)S(1)}, u32[]{:S(2)}, u32[]{:S(2)}) collective-permute-start(bf16[1,144,384]{2,1,0:T(8,128)(2,1)S(1)} %collective-permute-done.3.refs_3_.refs_2_), channel_id=1, source_target_pairs={{0,1},{1,0},{2,3},{3,2},{4,5},{5,4},{6,7},{7,6},{8,9},{9,8},{10,11... | collective-permute-start | bytes 331784 | tf_op jit(solution)/shard_map/ppermute | solution.py:504
  17.2 1.3 %collective-permute-start.7 = (bf16[1,144,384]{2,1,0:T(8,128)(2,1)S(1)}, bf16[1,144,384]{2,1,0:T(8,128)(2,1)S(1)}, u32[]{:S(2)}, u32[]{:S(2)}) collective-permute-start(bf16[1,144,384]{2,1,0:T(8,128)(2,1)S(1)} %collective-permute-done.4.refs_4_.refs_3_), channel_id=1, source_target_pairs={{0,1},{1,0},{2,3},{3,2},{4,5},{5,4},{6,7},{7,6},{8,9},{9,8},{10,11... | collective-permute-start | bytes 331784 | tf_op jit(solution)/shard_map/ppermute | solution.py:504
  19.3 5.3 %copy-start = (bf16[384,3072]{1,0:T(8,128)(2,1)S(1)}, bf16[384,3072]{1,0:T(8,128)(2,1)}, u32[]{:S(2)}) copy-start(bf16[384,3072]{1,0:T(8,128)(2,1)} %w_ref.1) | copy-start | bytes 7077892
  19.3 5.3 %collective-permute-start.8 = (bf16[256,128]{1,0:T(8,128)(2,1)S(1)}, bf16[256,128]{1,0:T(8,128)(2,1)S(1)}, u32[]{:S(2)}, u32[]{:S(2)}) collective-permute-start(bf16[256,128]{1,0:T(8,128)(2,1)S(1)} %get-tuple-element.26), channel_id=1, source_target_pairs={{0,8},{1,9},{2,10},{3,11},{4,12},{5,13},{6,14},{7,15},{8,0},{9,1},... | collective-permute-start | bytes 196616 | tf_op jit(solution)/shard_map/ppermute | solution.py:504

commit v9 on v8

--- a/solution.py
+++ b/solution.py
@@ -111,8 +111,8 @@
     for copy in small:
         copy.start()
     for c in range(len(places)):
+        w_copy(c).start()
         x_copy(c).start()
-        w_copy(c).start()
     main_ref[...] = jnp.zeros_like(main_ref)
     tail_ref[...] = jnp.zeros_like(tail_ref)
     sums_ref[...] = jnp.zeros_like(sums_ref)
@@ -459,7 +459,7 @@
     key_rows = key_basis.transpose(0, 2, 1)
     value_rows = value_basis.transpose(0, 2, 1)
     center_rows = centers.transpose(0, 2, 1, 3)
-    cuts = tuple(model * i // 3 for i in range(4))
+    cuts = tuple(model * i // 4 for i in range(5))
     shard = (1, tokens + SUM_ROWS, width)
     params = lambda mib: pltpu.CompilerParams(vmem_limit_bytes=mib * 2**20)
 

time: 26.9 us -> 26.8 us (level)
  no operation moved by 1% of the time
where the time goes in v9:
time: 26.8 us; the launch traced here: 26.5 us
  Pallas kernels  13.3 us (50%)
  starting transfers between devices  11.2 us (42%)
  waiting for transfers between devices  1.27 us (5%)
  between operations  0.74 us (3%)
    ppermute x9, starting transfers between devices, swap(): return lax.ppermute(x, 'seq', [(i, i ^ mask) for i in range(seq)])  11.2 us
    pallas_call x1, Pallas kernels, per_device(): pl.pallas_call(functools.partial(project_kernel, **sizes, rank=rank, log_...  5.09 us
    pallas_call x1, Pallas kernels, per_device(): pl.pallas_call(functools.partial(near_kernel, **sizes, rank=rank), in_spe...  2.79 us
    pallas_call x1, Pallas kernels, per_device(): pl.pallas_call(functools.partial(finish_kernel, **sizes, rank=rank, lengt...  1.99 us
    pallas_call x1, Pallas kernels, per_device(): pl.pallas_call(functools.partial(own_kernel, **sizes, rank=rank), in_spec...  1.64 us
    ppermute x9, waiting for transfers between devices, swap(): return lax.ppermute(x, 'seq', [(i, i ^ mask) for i in range(seq)])  1.27 us
    pallas_call x1, Pallas kernels, per_device(): pl.pallas_call(functools.partial(early_kernel, **sizes, rank=rank), in_sp...  0.98 us
    pallas_call x1, Pallas kernels, per_device(): pl.pallas_call(functools.partial(partner_kernel, **sizes, rank=rank, orde...  0.78 us
  transfers between devices with their start and end apart: 9, of which 4 were waited for; matrix products, arithmetic and copies ran while one was open for 0% of the time, Pallas kernels for 20%

profile of v9, /device:TPU:0, one launch (start us, length us, event | category | flops | bytes accessed | tf_op | source)
XLA Modules:
  0.0 26.5 jit_solution(1352956569910020628)
XLA Ops:
  0.6 0.0 copy-start.1
  0.6 0.0 copy-start.2
  0.7 0.0 copy-start.3
  0.7 5.1 %project.1 = (bf16[1,144,384]{2,1,0:T(8,128)(2,1)S(1)}, bf16[128,384]{1,0:T(8,128)(2,1)S(1)}, f32[256,1152]{1,0:T(8,128)S(1)}) custom-call(bf16[256,3072]{1,0:T(8,128)(2,1)} %bitcast.13, bf16[3072,1152]{1,0:T(8,128)(2,1)} %w_hbm.1, f32[9,128]{1,0:T(8,128)} %bitcast.15, f32[1,128]{1,0:T(1,128)} %bitcast.16, f32[1,128]{1,0:T(1,128)} %bitcast.17, ...), custom_call_target="tpu_custom_call" | custom-call | tf_op jit(solution)/shard_map/project/pallas_call | solution.py:466
  5.8 3.0 %collective-permute-start.2 = (bf16[1,144,384]{2,1,0:T(8,128)(2,1)S(1)}, bf16[1,144,384]{2,1,0:T(8,128)(2,1)S(1)}, u32[]{:S(2)}, u32[]{:S(2)}) collective-permute-start(bf16[1,144,384]{2,1,0:T(8,128)(2,1)S(1)} %get-tuple-element.20.refs_0_), channel_id=1, source_target_pairs={{0,2},{1,3},{2,0},{3,1},{4,6},{5,7},{6,4},{7,5},{8,10},{9,11},{10,... | collective-permute-start | bytes 331784 | tf_op jit(solution)/shard_map/ppermute | solution.py:504
  8.8 1.6 %collective-permute-start.3 = (bf16[1,144,384]{2,1,0:T(8,128)(2,1)S(1)}, bf16[1,144,384]{2,1,0:T(8,128)(2,1)S(1)}, u32[]{:S(2)}, u32[]{:S(2)}) collective-permute-start(bf16[1,144,384]{2,1,0:T(8,128)(2,1)S(1)} %get-tuple-element.20.refs_0_), channel_id=1, source_target_pairs={{0,4},{1,5},{2,6},{3,7},{4,0},{5,1},{6,2},{7,3},{8,12},{9,13},{10,... | collective-permute-start | bytes 331784 | tf_op jit(solution)/shard_map/ppermute | solution.py:504
  10.4 0.0 collective-permute-start.4
  10.4 0.0 collective-permute-start.1
  10.4 3.0 %collective-permute-start = (bf16[128,384]{1,0:T(8,128)(2,1)S(1)}, bf16[128,384]{1,0:T(8,128)(2,1)S(1)}, u32[]{:S(2)}, u32[]{:S(2)}) collective-permute-start(bf16[128,384]{1,0:T(8,128)(2,1)S(1)} %get-tuple-element.19.query_ref), channel_id=1, source_target_pairs={{0,8},{1,9},{2,10},{3,11},{4,12},{5,13},{6,14},{7,15},{8,0},{9,1},... | collective-permute-start | bytes 294920 | tf_op jit(solution)/shard_map/ppermute | solution.py:504
  13.4 0.0 copy-done.1
  13.4 0.0 copy-done.2
  13.4 0.0 copy-done.3
  13.4 2.8 %near.1 = (f32[256,384]{1,0:T(8,128)S(1)}, f32[256,384]{1,0:T(8,128)S(1)}, bf16[2,128,384]{2,1,0:T(8,128)(2,1)S(1)}, bf16[2,128,384]{2,1,0:T(8,128)(2,1)S(1)}, f32[32,128]{1,0:T(8,128)S(1)}) custom-call(f32[256,1152]{1,0:T(8,128)S(1)} %get-tuple-element.21.qkv_ref, f32[2,3,2,128]{3,2,1,0:T(2,128)S(1)} %bitcast.12, s32[2,3]{1,0:T(2,128)S(1)} %copy-done.3, ...), custom_call_target="tpu_custom_call" | custom-call | flops 15099494400 | bytes 19660800 | tf_op jit(solution)/shard_map/near/pallas_call | solution.py:520
  16.2 0.0 collective-permute-done.2.refs_2_.refs_1_
  16.2 0.3 %collective-permute-start.5 = (bf16[1,144,384]{2,1,0:T(8,128)(2,1)S(1)}, bf16[1,144,384]{2,1,0:T(8,128)(2,1)S(1)}, u32[]{:S(2)}, u32[]{:S(2)}) collective-permute-start(bf16[1,144,384]{2,1,0:T(8,128)(2,1)S(1)} %collective-permute-done.2.refs_2_.refs_1_), channel_id=1, source_target_pairs={{0,1},{1,0},{2,3},{3,2},{4,5},{5,4},{6,7},{7,6},{8,9},{9,8},{10,11... | collective-permute-start | bytes 331784 | tf_op jit(solution)/shard_map/ppermute | solution.py:504
  16.5 0.0 collective-permute-done.3.refs_3_.refs_2_
  16.5 0.3 %collective-permute-start.6 = (bf16[1,144,384]{2,1,0:T(8,128)(2,1)S(1)}, bf16[1,144,384]{2,1,0:T(8,128)(2,1)S(1)}, u32[]{:S(2)}, u32[]{:S(2)}) collective-permute-start(bf16[1,144,384]{2,1,0:T(8,128)(2,1)S(1)} %collective-permute-done.3.refs_3_.refs_2_), channel_id=1, source_target_pairs={{0,1},{1,0},{2,3},{3,2},{4,5},{5,4},{6,7},{7,6},{8,9},{9,8},{10,11... | collective-permute-start | bytes 331784 | tf_op jit(solution)/shard_map/ppermute | solution.py:504
  16.7 0.4 %collective-permute-done.4.refs_4_.refs_3_ = bf16[1,144,384]{2,1,0:T(8,128)(2,1)S(1)} collective-permute-done((bf16[1,144,384]{2,1,0:T(8,128)(2,1)S(1)}, bf16[1,144,384]{2,1,0:T(8,128)(2,1)S(1)}, u32[]{:S(2)}, u32[]{:S(2)}) %collective-permute-start.4) | collective-permute-done | bytes 110624 | tf_op jit(solution)/shard_map/ppermute | solution.py:504
  17.1 0.0 collective-permute-start.7
  17.1 0.2 collective-permute-done.query_ref
  17.3 0.0 collective-permute-done.1.refs_1_.refs_0_
  17.3 1.0 %early.1 = (f32[256,128]{1,0:T(8,128)S(1)}, f32[256,128]{1,0:T(8,128)S(1)}) custom-call(bf16[128,384]{1,0:T(8,128)(2,1)S(1)} %collective-permute-done.query_ref, bf16[1,144,384]{2,1,0:T(8,128)(2,1)S(1)} %get-tuple-element.20.refs_0_, bf16[1,144,384]{2,1,0:T(8,128)(2,1)S(1)} %collective-permute-done.1.refs_1_.refs_0_, ...), custom_call_target="tpu_custom_call" | custom-call | flops 503316480 | bytes 491520 | tf_op jit(solution)/shard_map/early/pallas_call | solution.py:556
  18.3 0.0 collective-permute-done.5.refs_5_.refs_4_
  18.3 0.0 collective-permute-done.6.refs_6_.refs_5_
  18.3 0.1 collective-permute-done.7.refs_7_.refs_6_
  18.4 0.8 %partner.1 = (bf16[256,128]{1,0:T(8,128)(2,1)S(1)}, f32[16,128]{1,0:T(8,128)S(1)}) custom-call(bf16[128,384]{1,0:T(8,128)(2,1)S(1)} %collective-permute-done.query_ref, f32[256,128]{1,0:T(8,128)S(1)} %get-tuple-element.24.part_ref, f32[256,128]{1,0:T(8,128)S(1)} %get-tuple-element.25.part_log_ref, bf16[1,144,384]{2,1,0:T(8,128)(2,1)S(1)} %get-tuple-element.20.refs_0_, ...), custom_call_target="tpu_custom_call" | custom-call | flops 805306368 | bytes 786432 | tf_op jit(solution)/shard_map/partner/pallas_call | solution.py:565
  19.2 0.0 copy-start
  19.2 3.0 %collective-permute-start.8 = (bf16[256,128]{1,0:T(8,128)(2,1)S(1)}, bf16[256,128]{1,0:T(8,128)(2,1)S(1)}, u32[]{:S(2)}, u32[]{:S(2)}) collective-permute-start(bf16[256,128]{1,0:T(8,128)(2,1)S(1)} %get-tuple-element.26), channel_id=1, source_target_pairs={{0,8},{1,9},{2,10},{3,11},{4,12},{5,13},{6,14},{7,15},{8,0},{9,1},... | collective-permute-start | bytes 196616 | tf_op jit(solution)/shard_map/ppermute | solution.py:504
  22.3 1.6 %own.1 = (f32[256,384]{1,0:T(8,128)S(1)}, f32[256,128]{1,0:T(8,128)S(1)}) custom-call(bf16[128,384]{1,0:T(8,128)(2,1)S(1)} %get-tuple-element.19.query_ref, f32[256,384]{1,0:T(8,128)S(1)} %get-tuple-element.28.near_ref, f32[256,384]{1,0:T(8,128)S(1)} %get-tuple-element.22.rel_ref, f32[32,128]{1,0:T(8,128)S(1)} %get-tuple-element.29.old_ref, ...), custom_call_target="tpu_custom_call" | custom-call | flops 805306368 | bytes 786432 | tf_op jit(solution)/shard_map/own/pallas_call | solution.py:580
  23.9 0.6 %collective-permute-done.8.back_ref = bf16[256,128]{1,0:T(8,128)(2,1)S(1)} collective-permute-done((bf16[256,128]{1,0:T(8,128)(2,1)S(1)}, bf16[256,128]{1,0:T(8,128)(2,1)S(1)}, u32[]{:S(2)}, u32[]{:S(2)}) %collective-permute-start.8) | collective-permute-done | bytes 65568 | tf_op jit(solution)/shard_map/ppermute | solution.py:504
  24.5 0.0 copy-done
  24.5 2.0 %finish.1 = (bf16[256,3072]{1,0:T(8,128)(2,1)}, f32[2,3,2,128]{3,2,1,0:T(2,128)}) custom-call(bf16[256,128]{1,0:T(8,128)(2,1)S(1)} %collective-permute-done.8.back_ref, f32[16,128]{1,0:T(8,128)S(1)} %get-tuple-element.27.half_ref, f32[256,384]{1,0:T(8,128)S(1)} %get-tuple-element.32.merged_ref, f32[256,128]{1,0:T(8,128)S(1)} %get-tuple-element.33.log_ref, ...), custom_call_target="tpu_custom_call" | custom-call | tf_op jit(solution)/shard_map/finish/pallas_call | solution.py:594
Async XLA Ops:
  0.6 12.7 %copy-start.1 = (f32[3,128,32]{1,2,0:T(8,128)S(1)}, f32[3,128,32]{1,2,0:T(8,128)}, u32[]{:S(2)}) copy-start(f32[3,128,32]{1,2,0:T(8,128)} %param.16) | copy-start | bytes 147460
  0.6 12.7 %copy-start.2 = (f32[2,2,3,128]{3,1,2,0:T(2,128)S(1)}, f32[2,2,3,128]{3,1,2,0:T(2,128)}, u32[]{:S(2)}) copy-start(f32[2,2,3,128]{3,1,2,0:T(2,128)} %param.17) | copy-start | bytes 18436
  0.7 12.7 %copy-start.3 = (s32[2,3]{1,0:T(2,128)S(1)}, s32[2,3]{1,0:T(2,128)}, u32[]{:S(2)}) copy-start(s32[2,3]{1,0:T(2,128)} %refresh_ref.1) | copy-start | bytes 76
  5.8 10.4 %collective-permute-start.2 = (bf16[1,144,384]{2,1,0:T(8,128)(2,1)S(1)}, bf16[1,144,384]{2,1,0:T(8,128)(2,1)S(1)}, u32[]{:S(2)}, u32[]{:S(2)}) collective-permute-start(bf16[1,144,384]{2,1,0:T(8,128)(2,1)S(1)} %get-tuple-element.20.refs_0_), channel_id=1, source_target_pairs={{0,2},{1,3},{2,0},{3,1},{4,6},{5,7},{6,4},{7,5},{8,10},{9,11},{10,... | collective-permute-start | bytes 331784 | tf_op jit(solution)/shard_map/ppermute | solution.py:504
  8.8 7.7 %collective-permute-start.3 = (bf16[1,144,384]{2,1,0:T(8,128)(2,1)S(1)}, bf16[1,144,384]{2,1,0:T(8,128)(2,1)S(1)}, u32[]{:S(2)}, u32[]{:S(2)}) collective-permute-start(bf16[1,144,384]{2,1,0:T(8,128)(2,1)S(1)} %get-tuple-element.20.refs_0_), channel_id=1, source_target_pairs={{0,4},{1,5},{2,6},{3,7},{4,0},{5,1},{6,2},{7,3},{8,12},{9,13},{10,... | collective-permute-start | bytes 331784 | tf_op jit(solution)/shard_map/ppermute | solution.py:504
  10.4 6.7 %collective-permute-start.4 = (bf16[1,144,384]{2,1,0:T(8,128)(2,1)S(1)}, bf16[1,144,384]{2,1,0:T(8,128)(2,1)S(1)}, u32[]{:S(2)}, u32[]{:S(2)}) collective-permute-start(bf16[1,144,384]{2,1,0:T(8,128)(2,1)S(1)} %get-tuple-element.20.refs_0_), channel_id=1, source_target_pairs={{0,6},{1,7},{2,4},{3,5},{4,2},{5,3},{6,0},{7,1},{8,14},{9,15},{10,... | collective-permute-start | bytes 331784 | tf_op jit(solution)/shard_map/ppermute | solution.py:504
  10.4 7.0 %collective-permute-start.1 = (bf16[1,144,384]{2,1,0:T(8,128)(2,1)S(1)}, bf16[1,144,384]{2,1,0:T(8,128)(2,1)S(1)}, u32[]{:S(2)}, u32[]{:S(2)}) collective-permute-start(bf16[1,144,384]{2,1,0:T(8,128)(2,1)S(1)} %get-tuple-element.20.refs_0_), channel_id=1, source_target_pairs={{0,1},{1,0},{2,3},{3,2},{4,5},{5,4},{6,7},{7,6},{8,9},{9,8},{10,11... | collective-permute-start | bytes 331784 | tf_op jit(solution)/shard_map/ppermute | solution.py:504
  10.4 7.0 %collective-permute-start = (bf16[128,384]{1,0:T(8,128)(2,1)S(1)}, bf16[128,384]{1,0:T(8,128)(2,1)S(1)}, u32[]{:S(2)}, u32[]{:S(2)}) collective-permute-start(bf16[128,384]{1,0:T(8,128)(2,1)S(1)} %get-tuple-element.19.query_ref), channel_id=1, source_target_pairs={{0,8},{1,9},{2,10},{3,11},{4,12},{5,13},{6,14},{7,15},{8,0},{9,1},... | collective-permute-start | bytes 294920 | tf_op jit(solution)/shard_map/ppermute | solution.py:504
  16.2 2.2 %collective-permute-start.5 = (bf16[1,144,384]{2,1,0:T(8,128)(2,1)S(1)}, bf16[1,144,384]{2,1,0:T(8,128)(2,1)S(1)}, u32[]{:S(2)}, u32[]{:S(2)}) collective-permute-start(bf16[1,144,384]{2,1,0:T(8,128)(2,1)S(1)} %collective-permute-done.2.refs_2_.refs_1_), channel_id=1, source_target_pairs={{0,1},{1,0},{2,3},{3,2},{4,5},{5,4},{6,7},{7,6},{8,9},{9,8},{10,11... | collective-permute-start | bytes 331784 | tf_op jit(solution)/shard_map/ppermute | solution.py:504
  16.5 1.9 %collective-permute-start.6 = (bf16[1,144,384]{2,1,0:T(8,128)(2,1)S(1)}, bf16[1,144,384]{2,1,0:T(8,128)(2,1)S(1)}, u32[]{:S(2)}, u32[]{:S(2)}) collective-permute-start(bf16[1,144,384]{2,1,0:T(8,128)(2,1)S(1)} %collective-permute-done.3.refs_3_.refs_2_), channel_id=1, source_target_pairs={{0,1},{1,0},{2,3},{3,2},{4,5},{5,4},{6,7},{7,6},{8,9},{9,8},{10,11... | collective-permute-start | bytes 331784 | tf_op jit(solution)/shard_map/ppermute | solution.py:504
  17.1 1.3 %collective-permute-start.7 = (bf16[1,144,384]{2,1,0:T(8,128)(2,1)S(1)}, bf16[1,144,384]{2,1,0:T(8,128)(2,1)S(1)}, u32[]{:S(2)}, u32[]{:S(2)}) collective-permute-start(bf16[1,144,384]{2,1,0:T(8,128)(2,1)S(1)} %collective-permute-done.4.refs_4_.refs_3_), channel_id=1, source_target_pairs={{0,1},{1,0},{2,3},{3,2},{4,5},{5,4},{6,7},{7,6},{8,9},{9,8},{10,11... | collective-permute-start | bytes 331784 | tf_op jit(solution)/shard_map/ppermute | solution.py:504
  19.2 5.3 %copy-start = (bf16[384,3072]{1,0:T(8,128)(2,1)S(1)}, bf16[384,3072]{1,0:T(8,128)(2,1)}, u32[]{:S(2)}) copy-start(bf16[384,3072]{1,0:T(8,128)(2,1)} %w_ref.1) | copy-start | bytes 7077892
  19.2 5.3 %collective-permute-start.8 = (bf16[256,128]{1,0:T(8,128)(2,1)S(1)}, bf16[256,128]{1,0:T(8,128)(2,1)S(1)}, u32[]{:S(2)}, u32[]{:S(2)}) collective-permute-start(bf16[256,128]{1,0:T(8,128)(2,1)S(1)} %get-tuple-element.26), channel_id=1, source_target_pairs={{0,8},{1,9},{2,10},{3,11},{4,12},{5,13},{6,14},{7,15},{8,0},{9,1},... | collective-permute-start | bytes 196616 | tf_op jit(solution)/shard_map/ppermute | solution.py:504

commit v10 on v9

--- a/solution.py
+++ b/solution.py
@@ -538,9 +538,8 @@
     for i in (1,):
         x, _ = lax.optimization_barrier((held[i][0], rel))
         held[i] = (x, held[i][1])
-    held.insert(1, (swap(payload, 1), [1]))
     early = [a for a, _ in held]
-    held += [(swap(a, 1), [m ^ 1 for m in ms]) for a, ms in held[2:]]
+    held += [(swap(a, 1), [m ^ 1 for m in ms]) for a, ms in held]
     arrays = [a for a, _ in held]
     names = [m for _, ms in held for m in ms]
     order = tuple(names.index(m) for m in range(len(names)))

time: 26.8 us -> 26.7 us (level)
  waiting for transfers between devices: 1.27 us -> 1.7 us
    ppermute x9, waiting for transfers between devices: 1.27 us -> 1.7 us  [swap(): return lax.ppermute(x, 'seq', [(i, i ^ mask) for i in range(seq)])]
  transfers between devices with their start and end apart: 9 -> 9, of which waited for: 4 -> 4; matrix products, arithmetic and copies ran while one was open for 0% -> 0% of each run, Pallas kernels for 20% -> 19%
where the time goes in v10:
time: 26.7 us; the launch traced here: 26.5 us
  Pallas kernels  13.1 us (49%)
  starting transfers between devices  11 us (41%)
  waiting for transfers between devices  1.7 us (6%)
  between operations  0.74 us (3%)
    ppermute x9, starting transfers between devices, swap(): return lax.ppermute(x, 'seq', [(i, i ^ mask) for i in range(seq)])  11 us
    pallas_call x1, Pallas kernels, per_device(): pl.pallas_call(functools.partial(project_kernel, **sizes, rank=rank, log_...  5.09 us
    pallas_call x1, Pallas kernels, per_device(): pl.pallas_call(functools.partial(near_kernel, **sizes, rank=rank), in_spe...  2.79 us
    pallas_call x1, Pallas kernels, per_device(): pl.pallas_call(functools.partial(finish_kernel, **sizes, rank=rank, lengt...  1.99 us
    ppermute x9, waiting for transfers between devices, swap(): return lax.ppermute(x, 'seq', [(i, i ^ mask) for i in range(seq)])  1.7 us
    pallas_call x1, Pallas kernels, per_device(): pl.pallas_call(functools.partial(own_kernel, **sizes, rank=rank), in_spec...  1.66 us
    pallas_call x1, Pallas kernels, per_device(): pl.pallas_call(functools.partial(partner_kernel, **sizes, rank=rank, orde...  0.85 us
    pallas_call x1, Pallas kernels, per_device(): pl.pallas_call(functools.partial(early_kernel, **sizes, rank=rank), in_sp...  0.72 us
  transfers between devices with their start and end apart: 9, of which 4 were waited for; matrix products, arithmetic and copies ran while one was open for 0% of the time, Pallas kernels for 19%

profile of v10, /device:TPU:0, one launch (start us, length us, event | category | flops | bytes accessed | tf_op | source)
XLA Modules:
  0.0 26.5 jit_solution(8602138413000072332)
XLA Ops:
  0.6 0.0 copy-start.1
  0.6 0.0 copy-start.2
  0.7 0.0 copy-start.3
  0.7 5.1 %project.1 = (bf16[1,144,384]{2,1,0:T(8,128)(2,1)S(1)}, bf16[128,384]{1,0:T(8,128)(2,1)S(1)}, f32[256,1152]{1,0:T(8,128)S(1)}) custom-call(bf16[256,3072]{1,0:T(8,128)(2,1)} %bitcast.13, bf16[3072,1152]{1,0:T(8,128)(2,1)} %w_hbm.1, f32[9,128]{1,0:T(8,128)} %bitcast.15, f32[1,128]{1,0:T(1,128)} %bitcast.16, f32[1,128]{1,0:T(1,128)} %bitcast.17, ...), custom_call_target="tpu_custom_call" | custom-call | tf_op jit(solution)/shard_map/project/pallas_call | solution.py:466
  5.8 3.0 %collective-permute-start.1 = (bf16[1,144,384]{2,1,0:T(8,128)(2,1)S(1)}, bf16[1,144,384]{2,1,0:T(8,128)(2,1)S(1)}, u32[]{:S(2)}, u32[]{:S(2)}) collective-permute-start(bf16[1,144,384]{2,1,0:T(8,128)(2,1)S(1)} %get-tuple-element.20.refs_0_), channel_id=1, source_target_pairs={{0,2},{1,3},{2,0},{3,1},{4,6},{5,7},{6,4},{7,5},{8,10},{9,11},{10,... | collective-permute-start | bytes 331784 | tf_op jit(solution)/shard_map/ppermute | solution.py:504
  8.8 1.6 %collective-permute-start.2 = (bf16[1,144,384]{2,1,0:T(8,128)(2,1)S(1)}, bf16[1,144,384]{2,1,0:T(8,128)(2,1)S(1)}, u32[]{:S(2)}, u32[]{:S(2)}) collective-permute-start(bf16[1,144,384]{2,1,0:T(8,128)(2,1)S(1)} %get-tuple-element.20.refs_0_), channel_id=1, source_target_pairs={{0,4},{1,5},{2,6},{3,7},{4,0},{5,1},{6,2},{7,3},{8,12},{9,13},{10,... | collective-permute-start | bytes 331784 | tf_op jit(solution)/shard_map/ppermute | solution.py:504
  10.4 0.0 collective-permute-start.3
  10.4 0.0 collective-permute-start.4
  10.4 3.0 %collective-permute-start = (bf16[128,384]{1,0:T(8,128)(2,1)S(1)}, bf16[128,384]{1,0:T(8,128)(2,1)S(1)}, u32[]{:S(2)}, u32[]{:S(2)}) collective-permute-start(bf16[128,384]{1,0:T(8,128)(2,1)S(1)} %get-tuple-element.19.query_ref), channel_id=1, source_target_pairs={{0,8},{1,9},{2,10},{3,11},{4,12},{5,13},{6,14},{7,15},{8,0},{9,1},... | collective-permute-start | bytes 294920 | tf_op jit(solution)/shard_map/ppermute | solution.py:504
  13.4 0.0 copy-done.1
  13.4 0.0 copy-done.2
  13.4 0.0 copy-done.3
  13.4 2.8 %near.1 = (f32[256,384]{1,0:T(8,128)S(1)}, f32[256,384]{1,0:T(8,128)S(1)}, bf16[2,128,384]{2,1,0:T(8,128)(2,1)S(1)}, bf16[2,128,384]{2,1,0:T(8,128)(2,1)S(1)}, f32[32,128]{1,0:T(8,128)S(1)}) custom-call(f32[256,1152]{1,0:T(8,128)S(1)} %get-tuple-element.21.qkv_ref, f32[2,3,2,128]{3,2,1,0:T(2,128)S(1)} %bitcast.12, s32[2,3]{1,0:T(2,128)S(1)} %copy-done.3, ...), custom_call_target="tpu_custom_call" | custom-call | flops 15099494400 | bytes 19660800 | tf_op jit(solution)/shard_map/near/pallas_call | solution.py:520
  16.2 0.0 collective-permute-done.1.refs_1_.refs_0_
  16.2 0.3 %collective-permute-start.5 = (bf16[1,144,384]{2,1,0:T(8,128)(2,1)S(1)}, bf16[1,144,384]{2,1,0:T(8,128)(2,1)S(1)}, u32[]{:S(2)}, u32[]{:S(2)}) collective-permute-start(bf16[1,144,384]{2,1,0:T(8,128)(2,1)S(1)} %collective-permute-done.1.refs_1_.refs_0_), channel_id=1, source_target_pairs={{0,1},{1,0},{2,3},{3,2},{4,5},{5,4},{6,7},{7,6},{8,9},{9,8},{10,11... | collective-permute-start | bytes 331784 | tf_op jit(solution)/shard_map/ppermute | solution.py:504
  16.5 0.0 collective-permute-done.2.refs_2_.refs_1_
  16.5 0.3 %collective-permute-start.6 = (bf16[1,144,384]{2,1,0:T(8,128)(2,1)S(1)}, bf16[1,144,384]{2,1,0:T(8,128)(2,1)S(1)}, u32[]{:S(2)}, u32[]{:S(2)}) collective-permute-start(bf16[1,144,384]{2,1,0:T(8,128)(2,1)S(1)} %collective-permute-done.2.refs_2_.refs_1_), channel_id=1, source_target_pairs={{0,1},{1,0},{2,3},{3,2},{4,5},{5,4},{6,7},{7,6},{8,9},{9,8},{10,11... | collective-permute-start | bytes 331784 | tf_op jit(solution)/shard_map/ppermute | solution.py:504
  16.7 0.4 %collective-permute-done.3.refs_3_.refs_2_ = bf16[1,144,384]{2,1,0:T(8,128)(2,1)S(1)} collective-permute-done((bf16[1,144,384]{2,1,0:T(8,128)(2,1)S(1)}, bf16[1,144,384]{2,1,0:T(8,128)(2,1)S(1)}, u32[]{:S(2)}, u32[]{:S(2)}) %collective-permute-start.3) | collective-permute-done | bytes 110624 | tf_op jit(solution)/shard_map/ppermute | solution.py:504
  17.1 0.0 collective-permute-start.7
  17.1 0.2 collective-permute-done.query_ref
  17.3 0.7 %early.1 = (f32[256,128]{1,0:T(8,128)S(1)}, f32[256,128]{1,0:T(8,128)S(1)}) custom-call(bf16[128,384]{1,0:T(8,128)(2,1)S(1)} %collective-permute-done.query_ref, bf16[1,144,384]{2,1,0:T(8,128)(2,1)S(1)} %get-tuple-element.20.refs_0_, bf16[1,144,384]{2,1,0:T(8,128)(2,1)S(1)} %collective-permute-done.1.refs_1_.refs_0_, ...), custom_call_target="tpu_custom_call" | custom-call | flops 402653184 | bytes 393216 | tf_op jit(solution)/shard_map/early/pallas_call | solution.py:555
  18.1 0.0 collective-permute-done.4.refs_4_.refs_3_
  18.1 0.0 collective-permute-done.5.refs_5_.refs_4_
  18.1 0.0 collective-permute-done.6.refs_6_.refs_5_
  18.1 0.3 %collective-permute-done.7.refs_7_.refs_6_ = bf16[1,144,384]{2,1,0:T(8,128)(2,1)S(1)} collective-permute-done((bf16[1,144,384]{2,1,0:T(8,128)(2,1)S(1)}, bf16[1,144,384]{2,1,0:T(8,128)(2,1)S(1)}, u32[]{:S(2)}, u32[]{:S(2)}) %collective-permute-start.7) | collective-permute-done | bytes 110624 | tf_op jit(solution)/shard_map/ppermute | solution.py:504
  18.4 0.8 %partner.1 = (bf16[256,128]{1,0:T(8,128)(2,1)S(1)}, f32[16,128]{1,0:T(8,128)S(1)}) custom-call(bf16[128,384]{1,0:T(8,128)(2,1)S(1)} %collective-permute-done.query_ref, f32[256,128]{1,0:T(8,128)S(1)} %get-tuple-element.24.part_ref, f32[256,128]{1,0:T(8,128)S(1)} %get-tuple-element.25.part_log_ref, bf16[1,144,384]{2,1,0:T(8,128)(2,1)S(1)} %get-tuple-element.20.refs_0_, ...), custom_call_target="tpu_custom_call" | custom-call | flops 805306368 | bytes 786432 | tf_op jit(solution)/shard_map/partner/pallas_call | solution.py:564
  19.3 0.0 copy-start
  19.3 2.8 %collective-permute-start.8 = (bf16[256,128]{1,0:T(8,128)(2,1)S(1)}, bf16[256,128]{1,0:T(8,128)(2,1)S(1)}, u32[]{:S(2)}, u32[]{:S(2)}) collective-permute-start(bf16[256,128]{1,0:T(8,128)(2,1)S(1)} %get-tuple-element.26), channel_id=1, source_target_pairs={{0,8},{1,9},{2,10},{3,11},{4,12},{5,13},{6,14},{7,15},{8,0},{9,1},... | collective-permute-start | bytes 196616 | tf_op jit(solution)/shard_map/ppermute | solution.py:504
  22.1 1.7 %own.1 = (f32[256,384]{1,0:T(8,128)S(1)}, f32[256,128]{1,0:T(8,128)S(1)}) custom-call(bf16[128,384]{1,0:T(8,128)(2,1)S(1)} %get-tuple-element.19.query_ref, f32[256,384]{1,0:T(8,128)S(1)} %get-tuple-element.28.near_ref, f32[256,384]{1,0:T(8,128)S(1)} %get-tuple-element.22.rel_ref, f32[32,128]{1,0:T(8,128)S(1)} %get-tuple-element.29.old_ref, ...), custom_call_target="tpu_custom_call" | custom-call | flops 805306368 | bytes 786432 | tf_op jit(solution)/shard_map/own/pallas_call | solution.py:579
  23.7 0.8 %collective-permute-done.8.back_ref = bf16[256,128]{1,0:T(8,128)(2,1)S(1)} collective-permute-done((bf16[256,128]{1,0:T(8,128)(2,1)S(1)}, bf16[256,128]{1,0:T(8,128)(2,1)S(1)}, u32[]{:S(2)}, u32[]{:S(2)}) %collective-permute-start.8) | collective-permute-done | bytes 65568 | tf_op jit(solution)/shard_map/ppermute | solution.py:504
  24.5 0.0 copy-done
  24.5 2.0 %finish.1 = (bf16[256,3072]{1,0:T(8,128)(2,1)}, f32[2,3,2,128]{3,2,1,0:T(2,128)}) custom-call(bf16[256,128]{1,0:T(8,128)(2,1)S(1)} %collective-permute-done.8.back_ref, f32[16,128]{1,0:T(8,128)S(1)} %get-tuple-element.27.half_ref, f32[256,384]{1,0:T(8,128)S(1)} %get-tuple-element.32.merged_ref, f32[256,128]{1,0:T(8,128)S(1)} %get-tuple-element.33.log_ref, ...), custom_call_target="tpu_custom_call" | custom-call | tf_op jit(solution)/shard_map/finish/pallas_call | solution.py:593
Async XLA Ops:
  0.6 12.7 %copy-start.1 = (f32[3,128,32]{1,2,0:T(8,128)S(1)}, f32[3,128,32]{1,2,0:T(8,128)}, u32[]{:S(2)}) copy-start(f32[3,128,32]{1,2,0:T(8,128)} %param.16) | copy-start | bytes 147460
  0.6 12.7 %copy-start.2 = (f32[2,2,3,128]{3,1,2,0:T(2,128)S(1)}, f32[2,2,3,128]{3,1,2,0:T(2,128)}, u32[]{:S(2)}) copy-start(f32[2,2,3,128]{3,1,2,0:T(2,128)} %param.17) | copy-start | bytes 18436
  0.7 12.7 %copy-start.3 = (s32[2,3]{1,0:T(2,128)S(1)}, s32[2,3]{1,0:T(2,128)}, u32[]{:S(2)}) copy-start(s32[2,3]{1,0:T(2,128)} %refresh_ref.1) | copy-start | bytes 76
  5.8 10.4 %collective-permute-start.1 = (bf16[1,144,384]{2,1,0:T(8,128)(2,1)S(1)}, bf16[1,144,384]{2,1,0:T(8,128)(2,1)S(1)}, u32[]{:S(2)}, u32[]{:S(2)}) collective-permute-start(bf16[1,144,384]{2,1,0:T(8,128)(2,1)S(1)} %get-tuple-element.20.refs_0_), channel_id=1, source_target_pairs={{0,2},{1,3},{2,0},{3,1},{4,6},{5,7},{6,4},{7,5},{8,10},{9,11},{10,... | collective-permute-start | bytes 331784 | tf_op jit(solution)/shard_map/ppermute | solution.py:504
  8.8 7.7 %collective-permute-start.2 = (bf16[1,144,384]{2,1,0:T(8,128)(2,1)S(1)}, bf16[1,144,384]{2,1,0:T(8,128)(2,1)S(1)}, u32[]{:S(2)}, u32[]{:S(2)}) collective-permute-start(bf16[1,144,384]{2,1,0:T(8,128)(2,1)S(1)} %get-tuple-element.20.refs_0_), channel_id=1, source_target_pairs={{0,4},{1,5},{2,6},{3,7},{4,0},{5,1},{6,2},{7,3},{8,12},{9,13},{10,... | collective-permute-start | bytes 331784 | tf_op jit(solution)/shard_map/ppermute | solution.py:504
  10.4 6.7 %collective-permute-start.3 = (bf16[1,144,384]{2,1,0:T(8,128)(2,1)S(1)}, bf16[1,144,384]{2,1,0:T(8,128)(2,1)S(1)}, u32[]{:S(2)}, u32[]{:S(2)}) collective-permute-start(bf16[1,144,384]{2,1,0:T(8,128)(2,1)S(1)} %get-tuple-element.20.refs_0_), channel_id=1, source_target_pairs={{0,6},{1,7},{2,4},{3,5},{4,2},{5,3},{6,0},{7,1},{8,14},{9,15},{10,... | collective-permute-start | bytes 331784 | tf_op jit(solution)/shard_map/ppermute | solution.py:504
  10.4 7.7 %collective-permute-start.4 = (bf16[1,144,384]{2,1,0:T(8,128)(2,1)S(1)}, bf16[1,144,384]{2,1,0:T(8,128)(2,1)S(1)}, u32[]{:S(2)}, u32[]{:S(2)}) collective-permute-start(bf16[1,144,384]{2,1,0:T(8,128)(2,1)S(1)} %get-tuple-element.20.refs_0_), channel_id=1, source_target_pairs={{0,1},{1,0},{2,3},{3,2},{4,5},{5,4},{6,7},{7,6},{8,9},{9,8},{10,11... | collective-permute-start | bytes 331784 | tf_op jit(solution)/shard_map/ppermute | solution.py:504
  10.4 7.0 %collective-permute-start = (bf16[128,384]{1,0:T(8,128)(2,1)S(1)}, bf16[128,384]{1,0:T(8,128)(2,1)S(1)}, u32[]{:S(2)}, u32[]{:S(2)}) collective-permute-start(bf16[128,384]{1,0:T(8,128)(2,1)S(1)} %get-tuple-element.19.query_ref), channel_id=1, source_target_pairs={{0,8},{1,9},{2,10},{3,11},{4,12},{5,13},{6,14},{7,15},{8,0},{9,1},... | collective-permute-start | bytes 294920 | tf_op jit(solution)/shard_map/ppermute | solution.py:504
  16.2 1.9 %collective-permute-start.5 = (bf16[1,144,384]{2,1,0:T(8,128)(2,1)S(1)}, bf16[1,144,384]{2,1,0:T(8,128)(2,1)S(1)}, u32[]{:S(2)}, u32[]{:S(2)}) collective-permute-start(bf16[1,144,384]{2,1,0:T(8,128)(2,1)S(1)} %collective-permute-done.1.refs_1_.refs_0_), channel_id=1, source_target_pairs={{0,1},{1,0},{2,3},{3,2},{4,5},{5,4},{6,7},{7,6},{8,9},{9,8},{10,11... | collective-permute-start | bytes 331784 | tf_op jit(solution)/shard_map/ppermute | solution.py:504
  16.5 1.6 %collective-permute-start.6 = (bf16[1,144,384]{2,1,0:T(8,128)(2,1)S(1)}, bf16[1,144,384]{2,1,0:T(8,128)(2,1)S(1)}, u32[]{:S(2)}, u32[]{:S(2)}) collective-permute-start(bf16[1,144,384]{2,1,0:T(8,128)(2,1)S(1)} %collective-permute-done.2.refs_2_.refs_1_), channel_id=1, source_target_pairs={{0,1},{1,0},{2,3},{3,2},{4,5},{5,4},{6,7},{7,6},{8,9},{9,8},{10,11... | collective-permute-start | bytes 331784 | tf_op jit(solution)/shard_map/ppermute | solution.py:504
  17.1 1.3 %collective-permute-start.7 = (bf16[1,144,384]{2,1,0:T(8,128)(2,1)S(1)}, bf16[1,144,384]{2,1,0:T(8,128)(2,1)S(1)}, u32[]{:S(2)}, u32[]{:S(2)}) collective-permute-start(bf16[1,144,384]{2,1,0:T(8,128)(2,1)S(1)} %collective-permute-done.3.refs_3_.refs_2_), channel_id=1, source_target_pairs={{0,1},{1,0},{2,3},{3,2},{4,5},{5,4},{6,7},{7,6},{8,9},{9,8},{10,11... | collective-permute-start | bytes 331784 | tf_op jit(solution)/shard_map/ppermute | solution.py:504
  19.3 5.2 %copy-start = (bf16[384,3072]{1,0:T(8,128)(2,1)S(1)}, bf16[384,3072]{1,0:T(8,128)(2,1)}, u32[]{:S(2)}) copy-start(bf16[384,3072]{1,0:T(8,128)(2,1)} %w_ref.1) | copy-start | bytes 7077892
  19.3 5.2 %collective-permute-start.8 = (bf16[256,128]{1,0:T(8,128)(2,1)S(1)}, bf16[256,128]{1,0:T(8,128)(2,1)S(1)}, u32[]{:S(2)}, u32[]{:S(2)}) collective-permute-start(bf16[256,128]{1,0:T(8,128)(2,1)S(1)} %get-tuple-element.26), channel_id=1, source_target_pairs={{0,8},{1,9},{2,10},{3,11},{4,12},{5,13},{6,14},{7,15},{8,0},{9,1},... | collective-permute-start | bytes 196616 | tf_op jit(solution)/shard_map/ppermute | solution.py:504

commit v11 on v10

--- a/solution.py
+++ b/solution.py
@@ -12,7 +12,8 @@
 log2_e = math.log2(math.e)
 f32 = jnp.float32
 bf16 = jnp.bfloat16
-SUM_ROWS = 16
+SUM_ROWS = 8
+EXTRA_ROWS = 16
 NT = (((1,), (1,)), ((), ()))
 NN = (((1,), (0,)), ((), ()))
 
@@ -62,8 +63,12 @@
     return free_lane(sample, rank) + 8 * piece + head
 
 
-def sum_lane(sample, rank):
-    return free_lane(sample, rank) + 20
+def return_lane(head, rank, heads):
+    return {heads - 1: 0, 0: rank, 1: 2 * rank}[head]
+
+
+def center_row(sample, head, kind):
+    return head * SUM_ROWS + sample * 2 + kind
 
 
 def within(lanes, start, count):
@@ -79,6 +84,9 @@
             at = value_lane(b, h, rank, heads)
             basis_h[b, at : at + rank, h * dim : (h + 1) * dim] = vh
             basis_l[b, at : at + rank, h * dim : (h + 1) * dim] = vl
+        at = return_lane(h, rank, heads)
+        basis_h[samples, at : at + rank, h * dim : (h + 1) * dim] = vh
+        basis_l[samples, at : at + rank, h * dim : (h + 1) * dim] = vl
 
 
 def project_kernel(
@@ -115,7 +123,6 @@
         x_copy(c).start()
     main_ref[...] = jnp.zeros_like(main_ref)
     tail_ref[...] = jnp.zeros_like(tail_ref)
-    sums_ref[...] = jnp.zeros_like(sums_ref)
     half = dim // 2
 
     def build():
@@ -161,11 +168,17 @@
         values.append(v)
         for b in range(samples):
             rows = slice(b * tokens, (b + 1) * tokens)
-            row = (b * heads + h) * 2
-            sums_ref[row : row + 1, :] = jnp.sum(k[rows], axis=0, keepdims=True)
-            sums_ref[row + 1 : row + 2, :] = jnp.sum(v[rows], axis=0, keepdims=True)
-    for p, piece in enumerate(pieces_of(sums_ref[...], 3)):
-        payload_ref[0, tokens : tokens + SUM_ROWS, p * dim : (p + 1) * dim] = piece
+            for row, x in enumerate((k, v)):
+                total = jnp.sum(x[rows], axis=0, keepdims=True)
+                for again in range(2):
+                    at = again * 4 + b * 2 + row
+                    sums_ref[at : at + 1, h * dim : (h + 1) * dim] = total
+    total = sums_ref[...]
+    top = total.astype(bf16).astype(f32)
+    first = lax.broadcasted_iota(jnp.int32, total.shape, 0) < 4
+    total = jnp.where(first, top, total - top)
+    empty = jnp.zeros((EXTRA_ROWS - SUM_ROWS, width), f32)
+    payload_ref[0, tokens:, :] = jnp.concatenate([total, empty], axis=0).astype(bf16)
     def by_sample(j):
         rows = [centers_ref[b, h, j : j + 1, :] for b in range(samples) for h in range(heads)]
         return [
@@ -219,10 +232,11 @@
     for b in range(samples):
         for h in range(heads):
             for j in range(2):
-                row = (b * heads + h) * 2 + j
+                row = center_row(b, h, j)
                 keep = jnp.where(refresh_ref[j, h] == 1, 0.0, 1.0)
                 old_ref[row : row + 1, :] = centers_ref[b, h, j : j + 1, :]
-                old_ref[SUM_ROWS + row : SUM_ROWS + row + 1, :] = jnp.full((1, dim), keep, f32)
+                row += heads * SUM_ROWS
+                old_ref[row : row + 1, :] = jnp.full((1, dim), keep, f32)
     for b in range(samples):
         rows = slice(b * tokens, (b + 1) * tokens)
         for h in range(heads):
@@ -339,36 +353,45 @@
 ):
     out_ref, half_ref = refs[-2:]
     tiles = tiles_of(refs[:-2])
-    parts = []
-    for place in order:
-        ref, i = tiles[place]
-        rows = slice(tokens, tokens + SUM_ROWS)
-        pieces = [ref[i, rows, p * dim : (p + 1) * dim].astype(f32) for p in range(3)]
-        parts.append(pieces[0] + (pieces[1] + pieces[2]))
-    pieces = [piece.astype(f32) for piece in pieces_of(tree_sum(parts), 2)]
-    half_ref[...] = pieces[0] + pieces[1]
-    empty = jnp.zeros((tokens - SUM_ROWS, dim), f32)
-    turned = [jnp.concatenate([piece, empty], axis=0).T for piece in pieces]
+    end = tokens + SUM_ROWS
+    parts = [tiles[place][0][tiles[place][1], tokens:end, :].astype(f32) for place in order]
+    total = tree_sum(parts)
+    total = total + pltpu.roll(total, 4, 0)
+    total = jnp.concatenate([total[:, h * dim : (h + 1) * dim] for h in range(heads)], axis=0)
+    top = total.astype(bf16).astype(f32)
+    rest = (total - top).astype(bf16).astype(f32)
+    half_ref[...] = top + rest
+    in_eight = lax.broadcasted_iota(jnp.int32, total.shape, 0) % SUM_ROWS
+    sums = jnp.where(in_eight < 4, top, rest)
     lanes = lane_ids(tokens, dim)
     outs, all_logs = code_attention(
         query_ref, tiles[-late:], samples=samples, tokens=tokens, heads=heads, dim=dim, rank=rank
     )
+    kept = []
     for b in range(samples):
         rows = slice(b * tokens, (b + 1) * tokens)
-        out, logs = outs[b], all_logs[b]
         before, before_log = part_ref[rows, :], part_log_ref[rows, :]
-        log = spread(b, logs, tokens, heads, dim, rank)
+        log = spread(b, all_logs[b], tokens, heads, dim, rank)
         top = jnp.maximum(log, before_log)
         new = jnp.exp2(log - top)
         whole = new + jnp.exp2(before_log - top)
-        out = before + (out - before) * (new / whole)
+        outs[b] = before + (outs[b] - before) * (new / whole)
         log = top + jnp.log(whole) * log2_e
+        tile = jnp.zeros_like(log)
         for p, piece in enumerate(pieces_of(log, 3)):
             place = within(lanes, log_lane(b, 0, p, rank), heads)
-            out = jnp.where(place, piece.astype(f32), out)
-        at = sum_lane(b, rank)
-        out = jnp.where(within(lanes, at, 2 * samples * heads), pltpu.roll(turned[b], at, 1), out)
-        out_ref[rows, :] = out.astype(bf16)
+            tile = jnp.where(place, piece.astype(f32), tile)
+        kept.append(tile)
+    first = free_lane(0, rank)
+    out_ref[:tokens, :] = jnp.where(within(lanes, first, rank), outs[1], outs[0]).astype(bf16)
+    folded = pltpu.roll(outs[1], rank, 1)
+    middle = tokens // 2
+    back = pltpu.roll(folded[middle:], dim // 2, 1)
+    folded = jnp.where(lanes[:middle] < dim // 2, folded[:middle], back)
+    out_ref[tokens : tokens + middle, :] = folded.astype(bf16)
+    logs = kept[0] + pltpu.roll(kept[1], first + 4 - free_lane(1, rank), 1)
+    logs = logs.T[first : first + 3 * SUM_ROWS, :]
+    out_ref[tokens + middle :, :] = jnp.concatenate([logs, sums], axis=0).astype(bf16)
 
 
 def own_kernel(
@@ -378,6 +401,7 @@
     merged_ref, log_ref = refs[-2:]
     tiles = tiles_of(refs[:-2])
     lanes = lane_ids(tokens, dim)
+    kept = jnp.zeros((tokens, dim), f32)
     outs, all_logs = code_attention(
         query_ref, tiles, samples=samples, tokens=tokens, heads=heads, dim=dim, rank=rank
     )
@@ -385,19 +409,18 @@
         rows = slice(b * tokens, (b + 1) * tokens)
         out, logs = outs[b], all_logs[b]
         far = dot3(split(out), (basis_h[b], basis_l[b]))
-        kept = jnp.zeros((tokens, dim), f32)
         for h in range(heads):
             columns = slice(h * dim, (h + 1) * dim)
             near, rel = near_ref[rows, columns], rel_ref[rows, columns]
             top = jnp.maximum(rel, logs[h])
             far_part = jnp.exp2(logs[h] - top)
             whole = jnp.exp2(rel - top) + far_part
-            row = (b * heads + h) * 2 + 1
+            row = center_row(b, h, 1)
             value = far[:, columns] + old_ref[row : row + 1, :] - near
             merged_ref[rows, columns] = near + value * (far_part / whole)
             log = top + jnp.log(whole) * log2_e
-            kept = jnp.where(lanes == log_lane(b, h, 0, rank), log, kept)
-        log_ref[rows, :] = kept
+            kept = jnp.where(lanes == 4 * b + h, log, kept)
+    log_ref[...] = kept
 
 
 def finish_kernel(
@@ -407,19 +430,26 @@
 ):
     chunks, columns = mixed_ref.shape[0], mixed_ref.shape[2]
     copies = []
-    sums = jnp.zeros((tokens, dim), f32)
-    for b in range(samples):
+    middle = tokens // 2
+    count = heads * SUM_ROWS
+    lanes = lane_ids(tokens, dim)
+    extra = back_ref[tokens + middle :, :].astype(f32)
+    empty = jnp.zeros((tokens - 3 * SUM_ROWS, dim), f32)
+    far_log = jnp.concatenate([extra[: 3 * SUM_ROWS], empty], axis=0).T
+    far_log = far_log + (pltpu.roll(far_log, dim - 8, 1) + pltpu.roll(far_log, dim - 16, 1))
+    share = 1.0 / (1.0 + jnp.exp2(log_ref[...] - far_log))
+    straight = back_ref[:tokens, :]
+    folded = back_ref[tokens : tokens + middle, :].astype(f32)
+    folded = jnp.concatenate([folded, pltpu.roll(folded, dim // 2, 1)], axis=0)
+    own_lanes = within(lanes, free_lane(0, rank), rank)
+    second = jnp.where(own_lanes, straight.astype(f32), folded).astype(bf16)
+    for b, (codes, place) in enumerate(((straight, 0), (second, samples))):
         rows = slice(b * tokens, (b + 1) * tokens)
-        codes = back_ref[rows, :]
-        extra = codes.astype(f32)
-        sums = sums + pltpu.roll(extra, dim - sum_lane(b, rank), 1)
-        far_log = extra + (pltpu.roll(extra, dim - 8, 1) + pltpu.roll(extra, dim - 16, 1))
-        share = 1.0 / (1.0 + jnp.exp2(log_ref[rows, :] - far_log))
-        far = dot(codes, basis_h[b]) + dot(codes, basis_l[b])
+        far = dot(codes, basis_h[place]) + dot(codes, basis_l[place])
         for h in range(heads):
             head = slice(h * dim, (h + 1) * dim)
-            at = log_lane(b, h, 0, rank)
-            row = (b * heads + h) * 2 + 1
+            at = 4 * b + h
+            row = center_row(b, h, 1)
             near = merged_ref[rows, head]
             value = far[:, head] + old_ref[row : row + 1, :] - near
             attended_ref[rows, head] = (near + value * share[:, at : at + 1]).astype(bf16)
@@ -429,11 +459,13 @@
         copies.append(pltpu.make_async_copy(mixed_ref.at[c], mixed_hbm.at[:, place], sem.at[c]))
         copies[-1].start()
         if c == 1:
-            fresh = (half_ref[...] + sums.T[:SUM_ROWS, :]) * (1.0 / length)
-            fresh = jnp.where(old_ref[SUM_ROWS:, :] > 0.5, old_ref[:SUM_ROWS, :], fresh)
+            sums = extra[3 * SUM_ROWS :]
+            sums = sums + pltpu.roll(sums, 4, 0)
+            fresh = (half_ref[...] + sums) * (1.0 / length)
+            fresh = jnp.where(old_ref[count:, :] > 0.5, old_ref[:count, :], fresh)
             for b in range(samples):
                 for h in range(heads):
-                    row = (b * heads + h) * 2
+                    row = center_row(b, h, 0)
                     new_ref[b, h] = fresh[row : row + 2, :]
             copies.append(pltpu.make_async_copy(new_ref, new_hbm, new_sem.at[0]))
             copies[-1].start()
@@ -460,7 +492,7 @@
     value_rows = value_basis.transpose(0, 2, 1)
     center_rows = centers.transpose(0, 2, 1, 3)
     cuts = tuple(model * i // 4 for i in range(5))
-    shard = (1, tokens + SUM_ROWS, width)
+    shard = (1, tokens + EXTRA_ROWS, width)
     params = lambda mib: pltpu.CompilerParams(vmem_limit_bytes=mib * 2**20)
 
     payload, query, qkv = pl.pallas_call(
@@ -484,7 +516,7 @@
             pltpu.VMEM((rows, 3 * width), f32),
             pltpu.VMEM((2 * dim, width + dim), bf16),
             pltpu.VMEM((dim, width - dim), bf16),
-            pltpu.VMEM((SUM_ROWS, dim), f32),
+            pltpu.VMEM((SUM_ROWS, width), f32),
             pltpu.SemaphoreType.DMA((2, len(cuts) - 1)),
             pltpu.SemaphoreType.DMA((6,)),
         ],
@@ -524,9 +556,9 @@
         out_shape=[
             jax.ShapeDtypeStruct((rows, width), f32),
             jax.ShapeDtypeStruct((rows, width), f32),
-            jax.ShapeDtypeStruct((samples, dim, width), bf16),
-            jax.ShapeDtypeStruct((samples, dim, width), bf16),
-            jax.ShapeDtypeStruct((2 * SUM_ROWS, dim), f32),
+            jax.ShapeDtypeStruct((samples + 1, dim, width), bf16),
+            jax.ShapeDtypeStruct((samples + 1, dim, width), bf16),
+            jax.ShapeDtypeStruct((2 * heads * SUM_ROWS, dim), f32),
         ],
         compiler_params=params(24),
         cost_estimate=pl.CostEstimate(
@@ -568,8 +600,8 @@
         in_specs=[VMEM] * (3 + len(arrays)),
         out_specs=[VMEM] * 2,
         out_shape=[
-            jax.ShapeDtypeStruct((rows, dim), bf16),
-            jax.ShapeDtypeStruct((SUM_ROWS, dim), f32),
+            jax.ShapeDtypeStruct((tokens + tokens // 2 + (3 + heads) * SUM_ROWS, dim), bf16),
+            jax.ShapeDtypeStruct((heads * SUM_ROWS, dim), f32),
         ],
         compiler_params=params(32),
         cost_estimate=cost(len(names)),
@@ -582,7 +614,7 @@
         out_specs=[VMEM] * 2,
         out_shape=[
             jax.ShapeDtypeStruct((rows, width), f32),
-            jax.ShapeDtypeStruct((rows, dim), f32),
+            jax.ShapeDtypeStruct((tokens, dim), f32),
         ],
         compiler_params=params(32),
         cost_estimate=cost(len(names)),

time: 26.7 us -> 26.8 us (level)
  no operation moved by 1% of the time
where the time goes in v11:
time: 26.8 us; the launch traced here: 26.7 us
  Pallas kernels  13.3 us (50%)
  starting transfers between devices  11 us (41%)
  waiting for transfers between devices  1.64 us (6%)
  between operations  0.74 us (3%)
    ppermute x9, starting transfers between devices, swap(): return lax.ppermute(x, 'seq', [(i, i ^ mask) for i in range(seq)])  11 us
    pallas_call x1, Pallas kernels, per_device(): pl.pallas_call(functools.partial(project_kernel, **sizes, rank=rank, log_...  5.08 us
    pallas_call x1, Pallas kernels, per_device(): pl.pallas_call(functools.partial(near_kernel, **sizes, rank=rank), in_spe...  2.8 us
    pallas_call x1, Pallas kernels, per_device(): pl.pallas_call(functools.partial(finish_kernel, **sizes, rank=rank, lengt...  2.09 us
    pallas_call x1, Pallas kernels, per_device(): pl.pallas_call(functools.partial(own_kernel, **sizes, rank=rank), in_spec...  1.65 us
    ppermute x9, waiting for transfers between devices, swap(): return lax.ppermute(x, 'seq', [(i, i ^ mask) for i in range(seq)])  1.64 us
    pallas_call x1, Pallas kernels, per_device(): pl.pallas_call(functools.partial(partner_kernel, **sizes, rank=rank, orde...  0.94 us
    pallas_call x1, Pallas kernels, per_device(): pl.pallas_call(functools.partial(early_kernel, **sizes, rank=rank), in_sp...  0.72 us
  transfers between devices with their start and end apart: 9, of which 4 were waited for; matrix products, arithmetic and copies ran while one was open for 0% of the time, Pallas kernels for 19%

profile of v11, /device:TPU:0, one launch (start us, length us, event | category | flops | bytes accessed | tf_op | source)
XLA Modules:
  0.0 26.7 jit_solution(10326697499156151632)
XLA Ops:
  0.6 0.0 copy-start.1
  0.6 0.0 copy-start.2
  0.7 0.0 copy-start.3
  0.7 5.1 %project.1 = (bf16[1,144,384]{2,1,0:T(8,128)(2,1)S(1)}, bf16[128,384]{1,0:T(8,128)(2,1)S(1)}, f32[256,1152]{1,0:T(8,128)S(1)}) custom-call(bf16[256,3072]{1,0:T(8,128)(2,1)} %bitcast.13, bf16[3072,1152]{1,0:T(8,128)(2,1)} %w_hbm.1, f32[9,128]{1,0:T(8,128)} %bitcast.15, f32[1,128]{1,0:T(1,128)} %bitcast.16, f32[1,128]{1,0:T(1,128)} %bitcast.17, ...), custom_call_target="tpu_custom_call" | custom-call | tf_op jit(solution)/shard_map/project/pallas_call | solution.py:498
  5.8 3.0 %collective-permute-start.1 = (bf16[1,144,384]{2,1,0:T(8,128)(2,1)S(1)}, bf16[1,144,384]{2,1,0:T(8,128)(2,1)S(1)}, u32[]{:S(2)}, u32[]{:S(2)}) collective-permute-start(bf16[1,144,384]{2,1,0:T(8,128)(2,1)S(1)} %get-tuple-element.20.refs_0_), channel_id=1, source_target_pairs={{0,2},{1,3},{2,0},{3,1},{4,6},{5,7},{6,4},{7,5},{8,10},{9,11},{10,... | collective-permute-start | bytes 331784 | tf_op jit(solution)/shard_map/ppermute | solution.py:536
  8.8 1.6 %collective-permute-start.2 = (bf16[1,144,384]{2,1,0:T(8,128)(2,1)S(1)}, bf16[1,144,384]{2,1,0:T(8,128)(2,1)S(1)}, u32[]{:S(2)}, u32[]{:S(2)}) collective-permute-start(bf16[1,144,384]{2,1,0:T(8,128)(2,1)S(1)} %get-tuple-element.20.refs_0_), channel_id=1, source_target_pairs={{0,4},{1,5},{2,6},{3,7},{4,0},{5,1},{6,2},{7,3},{8,12},{9,13},{10,... | collective-permute-start | bytes 331784 | tf_op jit(solution)/shard_map/ppermute | solution.py:536
  10.4 0.0 collective-permute-start.3
  10.4 0.0 collective-permute-start.4
  10.4 3.0 %collective-permute-start = (bf16[128,384]{1,0:T(8,128)(2,1)S(1)}, bf16[128,384]{1,0:T(8,128)(2,1)S(1)}, u32[]{:S(2)}, u32[]{:S(2)}) collective-permute-start(bf16[128,384]{1,0:T(8,128)(2,1)S(1)} %get-tuple-element.19.query_ref), channel_id=1, source_target_pairs={{0,8},{1,9},{2,10},{3,11},{4,12},{5,13},{6,14},{7,15},{8,0},{9,1},... | collective-permute-start | bytes 294920 | tf_op jit(solution)/shard_map/ppermute | solution.py:536
  13.3 0.0 copy-done.1
  13.4 0.0 copy-done.2
  13.4 0.0 copy-done.3
  13.4 2.8 %near.1 = (f32[256,384]{1,0:T(8,128)S(1)}, f32[256,384]{1,0:T(8,128)S(1)}, bf16[3,128,384]{2,1,0:T(8,128)(2,1)S(1)}, bf16[3,128,384]{2,1,0:T(8,128)(2,1)S(1)}, f32[48,128]{1,0:T(8,128)S(1)}) custom-call(f32[256,1152]{1,0:T(8,128)S(1)} %get-tuple-element.21.qkv_ref, f32[2,3,2,128]{3,2,1,0:T(2,128)S(1)} %bitcast.12, s32[2,3]{1,0:T(2,128)S(1)} %copy-done.3, ...), custom_call_target="tpu_custom_call" | custom-call | flops 15099494400 | bytes 19660800 | tf_op jit(solution)/shard_map/near/pallas_call | solution.py:552
  16.2 0.0 collective-permute-done.1.refs_1_.refs_0_
  16.2 0.3 %collective-permute-start.5 = (bf16[1,144,384]{2,1,0:T(8,128)(2,1)S(1)}, bf16[1,144,384]{2,1,0:T(8,128)(2,1)S(1)}, u32[]{:S(2)}, u32[]{:S(2)}) collective-permute-start(bf16[1,144,384]{2,1,0:T(8,128)(2,1)S(1)} %collective-permute-done.1.refs_1_.refs_0_), channel_id=1, source_target_pairs={{0,1},{1,0},{2,3},{3,2},{4,5},{5,4},{6,7},{7,6},{8,9},{9,8},{10,11... | collective-permute-start | bytes 331784 | tf_op jit(solution)/shard_map/ppermute | solution.py:536
  16.5 0.0 collective-permute-done.2.refs_2_.refs_1_
  16.5 0.3 %collective-permute-start.6 = (bf16[1,144,384]{2,1,0:T(8,128)(2,1)S(1)}, bf16[1,144,384]{2,1,0:T(8,128)(2,1)S(1)}, u32[]{:S(2)}, u32[]{:S(2)}) collective-permute-start(bf16[1,144,384]{2,1,0:T(8,128)(2,1)S(1)} %collective-permute-done.2.refs_2_.refs_1_), channel_id=1, source_target_pairs={{0,1},{1,0},{2,3},{3,2},{4,5},{5,4},{6,7},{7,6},{8,9},{9,8},{10,11... | collective-permute-start | bytes 331784 | tf_op jit(solution)/shard_map/ppermute | solution.py:536
  16.8 0.3 %collective-permute-done.3.refs_3_.refs_2_ = bf16[1,144,384]{2,1,0:T(8,128)(2,1)S(1)} collective-permute-done((bf16[1,144,384]{2,1,0:T(8,128)(2,1)S(1)}, bf16[1,144,384]{2,1,0:T(8,128)(2,1)S(1)}, u32[]{:S(2)}, u32[]{:S(2)}) %collective-permute-start.3) | collective-permute-done | bytes 110624 | tf_op jit(solution)/shard_map/ppermute | solution.py:536
  17.1 0.0 collective-permute-start.7
  17.1 0.2 collective-permute-done.query_ref
  17.3 0.7 %early.1 = (f32[256,128]{1,0:T(8,128)S(1)}, f32[256,128]{1,0:T(8,128)S(1)}) custom-call(bf16[128,384]{1,0:T(8,128)(2,1)S(1)} %collective-permute-done.query_ref, bf16[1,144,384]{2,1,0:T(8,128)(2,1)S(1)} %get-tuple-element.20.refs_0_, bf16[1,144,384]{2,1,0:T(8,128)(2,1)S(1)} %collective-permute-done.1.refs_1_.refs_0_, ...), custom_call_target="tpu_custom_call" | custom-call | flops 402653184 | bytes 393216 | tf_op jit(solution)/shard_map/early/pallas_call | solution.py:587
  18.1 0.0 collective-permute-done.4.refs_4_.refs_3_
  18.1 0.0 collective-permute-done.5.refs_5_.refs_4_
  18.1 0.0 collective-permute-done.6.refs_6_.refs_5_
  18.1 0.3 %collective-permute-done.7.refs_7_.refs_6_ = bf16[1,144,384]{2,1,0:T(8,128)(2,1)S(1)} collective-permute-done((bf16[1,144,384]{2,1,0:T(8,128)(2,1)S(1)}, bf16[1,144,384]{2,1,0:T(8,128)(2,1)S(1)}, u32[]{:S(2)}, u32[]{:S(2)}) %collective-permute-start.7) | collective-permute-done | bytes 110624 | tf_op jit(solution)/shard_map/ppermute | solution.py:536
  18.4 0.9 %partner.1 = (bf16[240,128]{1,0:T(8,128)(2,1)S(1)}, f32[24,128]{1,0:T(8,128)S(1)}) custom-call(bf16[128,384]{1,0:T(8,128)(2,1)S(1)} %collective-permute-done.query_ref, f32[256,128]{1,0:T(8,128)S(1)} %get-tuple-element.24.part_ref, f32[256,128]{1,0:T(8,128)S(1)} %get-tuple-element.25.part_log_ref, bf16[1,144,384]{2,1,0:T(8,128)(2,1)S(1)} %get-tuple-element.20.refs_0_, ...), custom_call_target="tpu_custom_call" | custom-call | flops 805306368 | bytes 786432 | tf_op jit(solution)/shard_map/partner/pallas_call | solution.py:596
  19.4 0.0 copy-start
  19.4 2.8 %collective-permute-start.8 = (bf16[240,128]{1,0:T(8,128)(2,1)S(1)}, bf16[240,128]{1,0:T(8,128)(2,1)S(1)}, u32[]{:S(2)}, u32[]{:S(2)}) collective-permute-start(bf16[240,128]{1,0:T(8,128)(2,1)S(1)} %get-tuple-element.26), channel_id=1, source_target_pairs={{0,8},{1,9},{2,10},{3,11},{4,12},{5,13},{6,14},{7,15},{8,0},{9,1},... | collective-permute-start | bytes 184328 | tf_op jit(solution)/shard_map/ppermute | solution.py:536
  22.2 1.7 %own.1 = (f32[256,384]{1,0:T(8,128)S(1)}, f32[128,128]{1,0:T(8,128)S(1)}) custom-call(bf16[128,384]{1,0:T(8,128)(2,1)S(1)} %get-tuple-element.19.query_ref, f32[256,384]{1,0:T(8,128)S(1)} %get-tuple-element.28.near_ref, f32[256,384]{1,0:T(8,128)S(1)} %get-tuple-element.22.rel_ref, f32[48,128]{1,0:T(8,128)S(1)} %get-tuple-element.29.old_ref, ...), custom_call_target="tpu_custom_call" | custom-call | flops 805306368 | bytes 786432 | tf_op jit(solution)/shard_map/own/pallas_call | solution.py:611
  23.8 0.7 %collective-permute-done.8.back_ref = bf16[240,128]{1,0:T(8,128)(2,1)S(1)} collective-permute-done((bf16[240,128]{1,0:T(8,128)(2,1)S(1)}, bf16[240,128]{1,0:T(8,128)(2,1)S(1)}, u32[]{:S(2)}, u32[]{:S(2)}) %collective-permute-start.8) | collective-permute-done | bytes 61472 | tf_op jit(solution)/shard_map/ppermute | solution.py:536
  24.6 0.0 copy-done
  24.6 2.1 %finish.1 = (bf16[256,3072]{1,0:T(8,128)(2,1)}, f32[2,3,2,128]{3,2,1,0:T(2,128)}) custom-call(bf16[240,128]{1,0:T(8,128)(2,1)S(1)} %collective-permute-done.8.back_ref, f32[24,128]{1,0:T(8,128)S(1)} %get-tuple-element.27.half_ref, f32[256,384]{1,0:T(8,128)S(1)} %get-tuple-element.32.merged_ref, f32[128,128]{1,0:T(8,128)S(1)} %get-tuple-element.33.log_ref, ...), custom_call_target="tpu_custom_call" | custom-call | tf_op jit(solution)/shard_map/finish/pallas_call | solution.py:625
Async XLA Ops:
  0.6 12.7 %copy-start.1 = (f32[3,128,32]{1,2,0:T(8,128)S(1)}, f32[3,128,32]{1,2,0:T(8,128)}, u32[]{:S(2)}) copy-start(f32[3,128,32]{1,2,0:T(8,128)} %param.16) | copy-start | bytes 147460
  0.6 12.7 %copy-start.2 = (f32[2,2,3,128]{3,1,2,0:T(2,128)S(1)}, f32[2,2,3,128]{3,1,2,0:T(2,128)}, u32[]{:S(2)}) copy-start(f32[2,2,3,128]{3,1,2,0:T(2,128)} %param.17) | copy-start | bytes 18436
  0.7 12.7 %copy-start.3 = (s32[2,3]{1,0:T(2,128)S(1)}, s32[2,3]{1,0:T(2,128)}, u32[]{:S(2)}) copy-start(s32[2,3]{1,0:T(2,128)} %refresh_ref.1) | copy-start | bytes 76
  5.8 10.4 %collective-permute-start.1 = (bf16[1,144,384]{2,1,0:T(8,128)(2,1)S(1)}, bf16[1,144,384]{2,1,0:T(8,128)(2,1)S(1)}, u32[]{:S(2)}, u32[]{:S(2)}) collective-permute-start(bf16[1,144,384]{2,1,0:T(8,128)(2,1)S(1)} %get-tuple-element.20.refs_0_), channel_id=1, source_target_pairs={{0,2},{1,3},{2,0},{3,1},{4,6},{5,7},{6,4},{7,5},{8,10},{9,11},{10,... | collective-permute-start | bytes 331784 | tf_op jit(solution)/shard_map/ppermute | solution.py:536
  8.8 7.7 %collective-permute-start.2 = (bf16[1,144,384]{2,1,0:T(8,128)(2,1)S(1)}, bf16[1,144,384]{2,1,0:T(8,128)(2,1)S(1)}, u32[]{:S(2)}, u32[]{:S(2)}) collective-permute-start(bf16[1,144,384]{2,1,0:T(8,128)(2,1)S(1)} %get-tuple-element.20.refs_0_), channel_id=1, source_target_pairs={{0,4},{1,5},{2,6},{3,7},{4,0},{5,1},{6,2},{7,3},{8,12},{9,13},{10,... | collective-permute-start | bytes 331784 | tf_op jit(solution)/shard_map/ppermute | solution.py:536
  10.4 6.7 %collective-permute-start.3 = (bf16[1,144,384]{2,1,0:T(8,128)(2,1)S(1)}, bf16[1,144,384]{2,1,0:T(8,128)(2,1)S(1)}, u32[]{:S(2)}, u32[]{:S(2)}) collective-permute-start(bf16[1,144,384]{2,1,0:T(8,128)(2,1)S(1)} %get-tuple-element.20.refs_0_), channel_id=1, source_target_pairs={{0,6},{1,7},{2,4},{3,5},{4,2},{5,3},{6,0},{7,1},{8,14},{9,15},{10,... | collective-permute-start | bytes 331784 | tf_op jit(solution)/shard_map/ppermute | solution.py:536
  10.4 7.7 %collective-permute-start.4 = (bf16[1,144,384]{2,1,0:T(8,128)(2,1)S(1)}, bf16[1,144,384]{2,1,0:T(8,128)(2,1)S(1)}, u32[]{:S(2)}, u32[]{:S(2)}) collective-permute-start(bf16[1,144,384]{2,1,0:T(8,128)(2,1)S(1)} %get-tuple-element.20.refs_0_), channel_id=1, source_target_pairs={{0,1},{1,0},{2,3},{3,2},{4,5},{5,4},{6,7},{7,6},{8,9},{9,8},{10,11... | collective-permute-start | bytes 331784 | tf_op jit(solution)/shard_map/ppermute | solution.py:536
  10.4 7.0 %collective-permute-start = (bf16[128,384]{1,0:T(8,128)(2,1)S(1)}, bf16[128,384]{1,0:T(8,128)(2,1)S(1)}, u32[]{:S(2)}, u32[]{:S(2)}) collective-permute-start(bf16[128,384]{1,0:T(8,128)(2,1)S(1)} %get-tuple-element.19.query_ref), channel_id=1, source_target_pairs={{0,8},{1,9},{2,10},{3,11},{4,12},{5,13},{6,14},{7,15},{8,0},{9,1},... | collective-permute-start | bytes 294920 | tf_op jit(solution)/shard_map/ppermute | solution.py:536
  16.2 1.9 %collective-permute-start.5 = (bf16[1,144,384]{2,1,0:T(8,128)(2,1)S(1)}, bf16[1,144,384]{2,1,0:T(8,128)(2,1)S(1)}, u32[]{:S(2)}, u32[]{:S(2)}) collective-permute-start(bf16[1,144,384]{2,1,0:T(8,128)(2,1)S(1)} %collective-permute-done.1.refs_1_.refs_0_), channel_id=1, source_target_pairs={{0,1},{1,0},{2,3},{3,2},{4,5},{5,4},{6,7},{7,6},{8,9},{9,8},{10,11... | collective-permute-start | bytes 331784 | tf_op jit(solution)/shard_map/ppermute | solution.py:536
  16.5 1.6 %collective-permute-start.6 = (bf16[1,144,384]{2,1,0:T(8,128)(2,1)S(1)}, bf16[1,144,384]{2,1,0:T(8,128)(2,1)S(1)}, u32[]{:S(2)}, u32[]{:S(2)}) collective-permute-start(bf16[1,144,384]{2,1,0:T(8,128)(2,1)S(1)} %collective-permute-done.2.refs_2_.refs_1_), channel_id=1, source_target_pairs={{0,1},{1,0},{2,3},{3,2},{4,5},{5,4},{6,7},{7,6},{8,9},{9,8},{10,11... | collective-permute-start | bytes 331784 | tf_op jit(solution)/shard_map/ppermute | solution.py:536
  17.1 1.3 %collective-permute-start.7 = (bf16[1,144,384]{2,1,0:T(8,128)(2,1)S(1)}, bf16[1,144,384]{2,1,0:T(8,128)(2,1)S(1)}, u32[]{:S(2)}, u32[]{:S(2)}) collective-permute-start(bf16[1,144,384]{2,1,0:T(8,128)(2,1)S(1)} %collective-permute-done.3.refs_3_.refs_2_), channel_id=1, source_target_pairs={{0,1},{1,0},{2,3},{3,2},{4,5},{5,4},{6,7},{7,6},{8,9},{9,8},{10,11... | collective-permute-start | bytes 331784 | tf_op jit(solution)/shard_map/ppermute | solution.py:536
  19.4 5.2 %copy-start = (bf16[384,3072]{1,0:T(8,128)(2,1)S(1)}, bf16[384,3072]{1,0:T(8,128)(2,1)}, u32[]{:S(2)}) copy-start(bf16[384,3072]{1,0:T(8,128)(2,1)} %w_ref.1) | copy-start | bytes 7077892
  19.4 5.2 %collective-permute-start.8 = (bf16[240,128]{1,0:T(8,128)(2,1)S(1)}, bf16[240,128]{1,0:T(8,128)(2,1)S(1)}, u32[]{:S(2)}, u32[]{:S(2)}) collective-permute-start(bf16[240,128]{1,0:T(8,128)(2,1)S(1)} %get-tuple-element.26), channel_id=1, source_target_pairs={{0,8},{1,9},{2,10},{3,11},{4,12},{5,13},{6,14},{7,15},{8,0},{9,1},... | collective-permute-start | bytes 184328 | tf_op jit(solution)/shard_map/ppermute | solution.py:536

commit v12 on v10

--- a/solution.py
+++ b/solution.py
@@ -589,7 +589,7 @@
         name="own",
     )(query, near, rel, old, basis_high, basis_low, *arrays[1:])
 
-    columns = 512
+    columns = 384
     mixed, new_centers = pl.pallas_call(
         functools.partial(finish_kernel, **sizes, rank=rank, length=tokens * seq),
         in_specs=[VMEM] * 8,

time: 26.7 us -> 26.8 us (level)
  no operation moved by 1% of the time
where the time goes in v12:
time: 26.8 us; the launch traced here: 26.6 us
  Pallas kernels  13.2 us (49%)
  starting transfers between devices  11 us (41%)
  waiting for transfers between devices  1.7 us (6%)
  between operations  0.74 us (3%)
    ppermute x9, starting transfers between devices, swap(): return lax.ppermute(x, 'seq', [(i, i ^ mask) for i in range(seq)])  11 us
    pallas_call x1, Pallas kernels, per_device(): pl.pallas_call(functools.partial(project_kernel, **sizes, rank=rank, log_...  5.09 us
    pallas_call x1, Pallas kernels, per_device(): pl.pallas_call(functools.partial(near_kernel, **sizes, rank=rank), in_spe...  2.79 us
    pallas_call x1, Pallas kernels, per_device(): pl.pallas_call(functools.partial(finish_kernel, **sizes, rank=rank, lengt...  2.13 us
    ppermute x9, waiting for transfers between devices, swap(): return lax.ppermute(x, 'seq', [(i, i ^ mask) for i in range(seq)])  1.7 us
    pallas_call x1, Pallas kernels, per_device(): pl.pallas_call(functools.partial(own_kernel, **sizes, rank=rank), in_spec...  1.66 us
    pallas_call x1, Pallas kernels, per_device(): pl.pallas_call(functools.partial(partner_kernel, **sizes, rank=rank, orde...  0.85 us
    pallas_call x1, Pallas kernels, per_device(): pl.pallas_call(functools.partial(early_kernel, **sizes, rank=rank), in_sp...  0.72 us
  transfers between devices with their start and end apart: 9, of which 4 were waited for; matrix products, arithmetic and copies ran while one was open for 0% of the time, Pallas kernels for 19%

profile of v12, /device:TPU:0, one launch (start us, length us, event | category | flops | bytes accessed | tf_op | source)
XLA Modules:
  0.0 26.6 jit_solution(7595531949472367380)
XLA Ops:
  0.6 0.0 copy-start.1
  0.6 0.0 copy-start.2
  0.7 0.0 copy-start.3
  0.7 5.1 %project.1 = (bf16[1,144,384]{2,1,0:T(8,128)(2,1)S(1)}, bf16[128,384]{1,0:T(8,128)(2,1)S(1)}, f32[256,1152]{1,0:T(8,128)S(1)}) custom-call(bf16[256,3072]{1,0:T(8,128)(2,1)} %bitcast.13, bf16[3072,1152]{1,0:T(8,128)(2,1)} %w_hbm.1, f32[9,128]{1,0:T(8,128)} %bitcast.15, f32[1,128]{1,0:T(1,128)} %bitcast.16, f32[1,128]{1,0:T(1,128)} %bitcast.17, ...), custom_call_target="tpu_custom_call" | custom-call | tf_op jit(solution)/shard_map/project/pallas_call | solution.py:466
  5.8 3.0 %collective-permute-start.1 = (bf16[1,144,384]{2,1,0:T(8,128)(2,1)S(1)}, bf16[1,144,384]{2,1,0:T(8,128)(2,1)S(1)}, u32[]{:S(2)}, u32[]{:S(2)}) collective-permute-start(bf16[1,144,384]{2,1,0:T(8,128)(2,1)S(1)} %get-tuple-element.20.refs_0_), channel_id=1, source_target_pairs={{0,2},{1,3},{2,0},{3,1},{4,6},{5,7},{6,4},{7,5},{8,10},{9,11},{10,... | collective-permute-start | bytes 331784 | tf_op jit(solution)/shard_map/ppermute | solution.py:504
  8.8 1.6 %collective-permute-start.2 = (bf16[1,144,384]{2,1,0:T(8,128)(2,1)S(1)}, bf16[1,144,384]{2,1,0:T(8,128)(2,1)S(1)}, u32[]{:S(2)}, u32[]{:S(2)}) collective-permute-start(bf16[1,144,384]{2,1,0:T(8,128)(2,1)S(1)} %get-tuple-element.20.refs_0_), channel_id=1, source_target_pairs={{0,4},{1,5},{2,6},{3,7},{4,0},{5,1},{6,2},{7,3},{8,12},{9,13},{10,... | collective-permute-start | bytes 331784 | tf_op jit(solution)/shard_map/ppermute | solution.py:504
  10.4 0.0 collective-permute-start.3
  10.4 0.0 collective-permute-start.4
  10.4 3.0 %collective-permute-start = (bf16[128,384]{1,0:T(8,128)(2,1)S(1)}, bf16[128,384]{1,0:T(8,128)(2,1)S(1)}, u32[]{:S(2)}, u32[]{:S(2)}) collective-permute-start(bf16[128,384]{1,0:T(8,128)(2,1)S(1)} %get-tuple-element.19.query_ref), channel_id=1, source_target_pairs={{0,8},{1,9},{2,10},{3,11},{4,12},{5,13},{6,14},{7,15},{8,0},{9,1},... | collective-permute-start | bytes 294920 | tf_op jit(solution)/shard_map/ppermute | solution.py:504
  13.4 0.0 copy-done.1
  13.4 0.0 copy-done.2
  13.4 0.0 copy-done.3
  13.4 2.8 %near.1 = (f32[256,384]{1,0:T(8,128)S(1)}, f32[256,384]{1,0:T(8,128)S(1)}, bf16[2,128,384]{2,1,0:T(8,128)(2,1)S(1)}, bf16[2,128,384]{2,1,0:T(8,128)(2,1)S(1)}, f32[32,128]{1,0:T(8,128)S(1)}) custom-call(f32[256,1152]{1,0:T(8,128)S(1)} %get-tuple-element.21.qkv_ref, f32[2,3,2,128]{3,2,1,0:T(2,128)S(1)} %bitcast.12, s32[2,3]{1,0:T(2,128)S(1)} %copy-done.3, ...), custom_call_target="tpu_custom_call" | custom-call | flops 15099494400 | bytes 19660800 | tf_op jit(solution)/shard_map/near/pallas_call | solution.py:520
  16.2 0.0 collective-permute-done.1.refs_1_.refs_0_
  16.2 0.3 %collective-permute-start.5 = (bf16[1,144,384]{2,1,0:T(8,128)(2,1)S(1)}, bf16[1,144,384]{2,1,0:T(8,128)(2,1)S(1)}, u32[]{:S(2)}, u32[]{:S(2)}) collective-permute-start(bf16[1,144,384]{2,1,0:T(8,128)(2,1)S(1)} %collective-permute-done.1.refs_1_.refs_0_), channel_id=1, source_target_pairs={{0,1},{1,0},{2,3},{3,2},{4,5},{5,4},{6,7},{7,6},{8,9},{9,8},{10,11... | collective-permute-start | bytes 331784 | tf_op jit(solution)/shard_map/ppermute | solution.py:504
  16.5 0.0 collective-permute-done.2.refs_2_.refs_1_
  16.5 0.3 %collective-permute-start.6 = (bf16[1,144,384]{2,1,0:T(8,128)(2,1)S(1)}, bf16[1,144,384]{2,1,0:T(8,128)(2,1)S(1)}, u32[]{:S(2)}, u32[]{:S(2)}) collective-permute-start(bf16[1,144,384]{2,1,0:T(8,128)(2,1)S(1)} %collective-permute-done.2.refs_2_.refs_1_), channel_id=1, source_target_pairs={{0,1},{1,0},{2,3},{3,2},{4,5},{5,4},{6,7},{7,6},{8,9},{9,8},{10,11... | collective-permute-start | bytes 331784 | tf_op jit(solution)/shard_map/ppermute | solution.py:504
  16.7 0.4 %collective-permute-done.3.refs_3_.refs_2_ = bf16[1,144,384]{2,1,0:T(8,128)(2,1)S(1)} collective-permute-done((bf16[1,144,384]{2,1,0:T(8,128)(2,1)S(1)}, bf16[1,144,384]{2,1,0:T(8,128)(2,1)S(1)}, u32[]{:S(2)}, u32[]{:S(2)}) %collective-permute-start.3) | collective-permute-done | bytes 110624 | tf_op jit(solution)/shard_map/ppermute | solution.py:504
  17.1 0.0 collective-permute-start.7
  17.1 0.2 collective-permute-done.query_ref
  17.3 0.7 %early.1 = (f32[256,128]{1,0:T(8,128)S(1)}, f32[256,128]{1,0:T(8,128)S(1)}) custom-call(bf16[128,384]{1,0:T(8,128)(2,1)S(1)} %collective-permute-done.query_ref, bf16[1,144,384]{2,1,0:T(8,128)(2,1)S(1)} %get-tuple-element.20.refs_0_, bf16[1,144,384]{2,1,0:T(8,128)(2,1)S(1)} %collective-permute-done.1.refs_1_.refs_0_, ...), custom_call_target="tpu_custom_call" | custom-call | flops 402653184 | bytes 393216 | tf_op jit(solution)/shard_map/early/pallas_call | solution.py:555
  18.1 0.0 collective-permute-done.4.refs_4_.refs_3_
  18.1 0.0 collective-permute-done.5.refs_5_.refs_4_
  18.1 0.0 collective-permute-done.6.refs_6_.refs_5_
  18.1 0.3 %collective-permute-done.7.refs_7_.refs_6_ = bf16[1,144,384]{2,1,0:T(8,128)(2,1)S(1)} collective-permute-done((bf16[1,144,384]{2,1,0:T(8,128)(2,1)S(1)}, bf16[1,144,384]{2,1,0:T(8,128)(2,1)S(1)}, u32[]{:S(2)}, u32[]{:S(2)}) %collective-permute-start.7) | collective-permute-done | bytes 110624 | tf_op jit(solution)/shard_map/ppermute | solution.py:504
  18.4 0.8 %partner.1 = (bf16[256,128]{1,0:T(8,128)(2,1)S(1)}, f32[16,128]{1,0:T(8,128)S(1)}) custom-call(bf16[128,384]{1,0:T(8,128)(2,1)S(1)} %collective-permute-done.query_ref, f32[256,128]{1,0:T(8,128)S(1)} %get-tuple-element.24.part_ref, f32[256,128]{1,0:T(8,128)S(1)} %get-tuple-element.25.part_log_ref, bf16[1,144,384]{2,1,0:T(8,128)(2,1)S(1)} %get-tuple-element.20.refs_0_, ...), custom_call_target="tpu_custom_call" | custom-call | flops 805306368 | bytes 786432 | tf_op jit(solution)/shard_map/partner/pallas_call | solution.py:564
  19.3 0.0 copy-start
  19.3 2.8 %collective-permute-start.8 = (bf16[256,128]{1,0:T(8,128)(2,1)S(1)}, bf16[256,128]{1,0:T(8,128)(2,1)S(1)}, u32[]{:S(2)}, u32[]{:S(2)}) collective-permute-start(bf16[256,128]{1,0:T(8,128)(2,1)S(1)} %get-tuple-element.26), channel_id=1, source_target_pairs={{0,8},{1,9},{2,10},{3,11},{4,12},{5,13},{6,14},{7,15},{8,0},{9,1},... | collective-permute-start | bytes 196616 | tf_op jit(solution)/shard_map/ppermute | solution.py:504
  22.1 1.7 %own.1 = (f32[256,384]{1,0:T(8,128)S(1)}, f32[256,128]{1,0:T(8,128)S(1)}) custom-call(bf16[128,384]{1,0:T(8,128)(2,1)S(1)} %get-tuple-element.19.query_ref, f32[256,384]{1,0:T(8,128)S(1)} %get-tuple-element.28.near_ref, f32[256,384]{1,0:T(8,128)S(1)} %get-tuple-element.22.rel_ref, f32[32,128]{1,0:T(8,128)S(1)} %get-tuple-element.29.old_ref, ...), custom_call_target="tpu_custom_call" | custom-call | flops 805306368 | bytes 786432 | tf_op jit(solution)/shard_map/own/pallas_call | solution.py:579
  23.7 0.8 %collective-permute-done.8.back_ref = bf16[256,128]{1,0:T(8,128)(2,1)S(1)} collective-permute-done((bf16[256,128]{1,0:T(8,128)(2,1)S(1)}, bf16[256,128]{1,0:T(8,128)(2,1)S(1)}, u32[]{:S(2)}, u32[]{:S(2)}) %collective-permute-start.8) | collective-permute-done | bytes 65568 | tf_op jit(solution)/shard_map/ppermute | solution.py:504
  24.5 0.0 copy-done
  24.5 2.1 %finish.1 = (bf16[256,3072]{1,0:T(8,128)(2,1)}, f32[2,3,2,128]{3,2,1,0:T(2,128)}) custom-call(bf16[256,128]{1,0:T(8,128)(2,1)S(1)} %collective-permute-done.8.back_ref, f32[16,128]{1,0:T(8,128)S(1)} %get-tuple-element.27.half_ref, f32[256,384]{1,0:T(8,128)S(1)} %get-tuple-element.32.merged_ref, f32[256,128]{1,0:T(8,128)S(1)} %get-tuple-element.33.log_ref, ...), custom_call_target="tpu_custom_call" | custom-call | tf_op jit(solution)/shard_map/finish/pallas_call | solution.py:593
Async XLA Ops:
  0.6 12.7 %copy-start.1 = (f32[3,128,32]{1,2,0:T(8,128)S(1)}, f32[3,128,32]{1,2,0:T(8,128)}, u32[]{:S(2)}) copy-start(f32[3,128,32]{1,2,0:T(8,128)} %param.16) | copy-start | bytes 147460
  0.6 12.7 %copy-start.2 = (f32[2,2,3,128]{3,1,2,0:T(2,128)S(1)}, f32[2,2,3,128]{3,1,2,0:T(2,128)}, u32[]{:S(2)}) copy-start(f32[2,2,3,128]{3,1,2,0:T(2,128)} %param.17) | copy-start | bytes 18436
  0.7 12.7 %copy-start.3 = (s32[2,3]{1,0:T(2,128)S(1)}, s32[2,3]{1,0:T(2,128)}, u32[]{:S(2)}) copy-start(s32[2,3]{1,0:T(2,128)} %refresh_ref.1) | copy-start | bytes 76
  5.8 10.4 %collective-permute-start.1 = (bf16[1,144,384]{2,1,0:T(8,128)(2,1)S(1)}, bf16[1,144,384]{2,1,0:T(8,128)(2,1)S(1)}, u32[]{:S(2)}, u32[]{:S(2)}) collective-permute-start(bf16[1,144,384]{2,1,0:T(8,128)(2,1)S(1)} %get-tuple-element.20.refs_0_), channel_id=1, source_target_pairs={{0,2},{1,3},{2,0},{3,1},{4,6},{5,7},{6,4},{7,5},{8,10},{9,11},{10,... | collective-permute-start | bytes 331784 | tf_op jit(solution)/shard_map/ppermute | solution.py:504
  8.8 7.7 %collective-permute-start.2 = (bf16[1,144,384]{2,1,0:T(8,128)(2,1)S(1)}, bf16[1,144,384]{2,1,0:T(8,128)(2,1)S(1)}, u32[]{:S(2)}, u32[]{:S(2)}) collective-permute-start(bf16[1,144,384]{2,1,0:T(8,128)(2,1)S(1)} %get-tuple-element.20.refs_0_), channel_id=1, source_target_pairs={{0,4},{1,5},{2,6},{3,7},{4,0},{5,1},{6,2},{7,3},{8,12},{9,13},{10,... | collective-permute-start | bytes 331784 | tf_op jit(solution)/shard_map/ppermute | solution.py:504
  10.4 6.7 %collective-permute-start.3 = (bf16[1,144,384]{2,1,0:T(8,128)(2,1)S(1)}, bf16[1,144,384]{2,1,0:T(8,128)(2,1)S(1)}, u32[]{:S(2)}, u32[]{:S(2)}) collective-permute-start(bf16[1,144,384]{2,1,0:T(8,128)(2,1)S(1)} %get-tuple-element.20.refs_0_), channel_id=1, source_target_pairs={{0,6},{1,7},{2,4},{3,5},{4,2},{5,3},{6,0},{7,1},{8,14},{9,15},{10,... | collective-permute-start | bytes 331784 | tf_op jit(solution)/shard_map/ppermute | solution.py:504
  10.4 7.7 %collective-permute-start.4 = (bf16[1,144,384]{2,1,0:T(8,128)(2,1)S(1)}, bf16[1,144,384]{2,1,0:T(8,128)(2,1)S(1)}, u32[]{:S(2)}, u32[]{:S(2)}) collective-permute-start(bf16[1,144,384]{2,1,0:T(8,128)(2,1)S(1)} %get-tuple-element.20.refs_0_), channel_id=1, source_target_pairs={{0,1},{1,0},{2,3},{3,2},{4,5},{5,4},{6,7},{7,6},{8,9},{9,8},{10,11... | collective-permute-start | bytes 331784 | tf_op jit(solution)/shard_map/ppermute | solution.py:504
  10.4 7.0 %collective-permute-start = (bf16[128,384]{1,0:T(8,128)(2,1)S(1)}, bf16[128,384]{1,0:T(8,128)(2,1)S(1)}, u32[]{:S(2)}, u32[]{:S(2)}) collective-permute-start(bf16[128,384]{1,0:T(8,128)(2,1)S(1)} %get-tuple-element.19.query_ref), channel_id=1, source_target_pairs={{0,8},{1,9},{2,10},{3,11},{4,12},{5,13},{6,14},{7,15},{8,0},{9,1},... | collective-permute-start | bytes 294920 | tf_op jit(solution)/shard_map/ppermute | solution.py:504
  16.2 1.9 %collective-permute-start.5 = (bf16[1,144,384]{2,1,0:T(8,128)(2,1)S(1)}, bf16[1,144,384]{2,1,0:T(8,128)(2,1)S(1)}, u32[]{:S(2)}, u32[]{:S(2)}) collective-permute-start(bf16[1,144,384]{2,1,0:T(8,128)(2,1)S(1)} %collective-permute-done.1.refs_1_.refs_0_), channel_id=1, source_target_pairs={{0,1},{1,0},{2,3},{3,2},{4,5},{5,4},{6,7},{7,6},{8,9},{9,8},{10,11... | collective-permute-start | bytes 331784 | tf_op jit(solution)/shard_map/ppermute | solution.py:504
  16.5 1.6 %collective-permute-start.6 = (bf16[1,144,384]{2,1,0:T(8,128)(2,1)S(1)}, bf16[1,144,384]{2,1,0:T(8,128)(2,1)S(1)}, u32[]{:S(2)}, u32[]{:S(2)}) collective-permute-start(bf16[1,144,384]{2,1,0:T(8,128)(2,1)S(1)} %collective-permute-done.2.refs_2_.refs_1_), channel_id=1, source_target_pairs={{0,1},{1,0},{2,3},{3,2},{4,5},{5,4},{6,7},{7,6},{8,9},{9,8},{10,11... | collective-permute-start | bytes 331784 | tf_op jit(solution)/shard_map/ppermute | solution.py:504
  17.1 1.3 %collective-permute-start.7 = (bf16[1,144,384]{2,1,0:T(8,128)(2,1)S(1)}, bf16[1,144,384]{2,1,0:T(8,128)(2,1)S(1)}, u32[]{:S(2)}, u32[]{:S(2)}) collective-permute-start(bf16[1,144,384]{2,1,0:T(8,128)(2,1)S(1)} %collective-permute-done.3.refs_3_.refs_2_), channel_id=1, source_target_pairs={{0,1},{1,0},{2,3},{3,2},{4,5},{5,4},{6,7},{7,6},{8,9},{9,8},{10,11... | collective-permute-start | bytes 331784 | tf_op jit(solution)/shard_map/ppermute | solution.py:504
  19.3 5.2 %copy-start = (bf16[384,3072]{1,0:T(8,128)(2,1)S(1)}, bf16[384,3072]{1,0:T(8,128)(2,1)}, u32[]{:S(2)}) copy-start(bf16[384,3072]{1,0:T(8,128)(2,1)} %w_ref.1) | copy-start | bytes 7077892
  19.3 5.2 %collective-permute-start.8 = (bf16[256,128]{1,0:T(8,128)(2,1)S(1)}, bf16[256,128]{1,0:T(8,128)(2,1)S(1)}, u32[]{:S(2)}, u32[]{:S(2)}) collective-permute-start(bf16[256,128]{1,0:T(8,128)(2,1)S(1)} %get-tuple-element.26), channel_id=1, source_target_pairs={{0,8},{1,9},{2,10},{3,11},{4,12},{5,13},{6,14},{7,15},{8,0},{9,1},... | collective-permute-start | bytes 196616 | tf_op jit(solution)/shard_map/ppermute | solution.py:504
